TPU v7x, 32 devices: a whole 2x2x4 slice. The times are simulated.
32 devices in a mesh: dp: 8 (over z, x), head: 4 (over y, core).
Axes of the slice: x: 2, y: 2, z: 4, core: 2. Of those that a mesh axis runs over, the one named last changes fastest.
Arguments:
- tokens: bfloat16 [4096, 4096], P('dp'), may hold values from -6 to 6
- q_weight: bfloat16 [4096, 8192], P('dp', 'head'), may hold values from -0.09375 to 0.09375
- kv_weight: bfloat16 [4096, 1024], P('dp', 'head'), may hold values from -0.09375 to 0.09375
- q_gain: float32 [128], replicated, may hold values from 0.1 to 1.9
- k_gain: float32 [128], replicated, may hold values from 0.1 to 1.9
- doc_lengths: int32 [8, 16], replicated, may hold values from 0 to 512, as said below
Outputs:
- attended: bfloat16 [4096, 8192], P('dp', 'head')
Inputs may be any that keep to these rules, and one draw needn't show every extreme that they name: `doc_lengths`: row r lists the lengths of the documents packed in order on index r of dp and sums to 512; some rank holds a single document of 512 tokens.
All inputs are finite; a program needn't handle non-finite values.
Results may differ from a plain program's by a relative error of at most 0.0068.
Values may be sent and summed in bfloat16 or wider, within the bound.
No kernel may reach another device: no remote copies, remote signals or barrier semaphores. Data moves between devices by JAX's collectives and lax.ppermute only.
A program may use at most 64 MiB of HBM per device.

v0:
```python
import math

import jax
import jax.numpy as jnp
from jax import lax
from jax.sharding import PartitionSpec as P

KVH = 4
HD = 128


theta_base = 1000000.0
norm_eps = 1e-06


def doc_layout(lengths, count):
    doc_ends = jnp.cumsum(lengths)
    places = jnp.arange(count, dtype=jnp.int32)
    passed = (places[:, None] >= doc_ends[None, :]).astype(jnp.int32)
    doc_ids = jnp.sum(passed, axis=1)
    starts = jnp.sum(passed * lengths[None, :], axis=1)
    return (doc_ids, places - starts)


def norm_rope(raw, gain, positions):
    half_width = raw.shape[-1] // 2
    inv_rms = lax.rsqrt(jnp.mean(raw * raw, axis=-1, keepdims=True) + norm_eps)
    normed = raw * inv_rms * gain
    frequency = jnp.exp(
        jnp.arange(half_width, dtype=jnp.float32) * (-2.0 * math.log(theta_base) / raw.shape[-1])
    )
    angles = positions.astype(jnp.float32)[:, None] * frequency[None, :]
    cosine = jnp.cos(angles)[:, None, :]
    sine_table = jnp.sin(angles)[:, None, :]
    lower_half = normed[..., :half_width]
    second = normed[..., half_width:]
    return jnp.concatenate(
        [lower_half * cosine - second * sine_table, second * cosine + lower_half * sine_table],
        axis=-1,
    ).astype(jnp.bfloat16)


def shards(tokens, q_weight, kv_weight, q_gain, k_gain, doc_lengths):
    rows_here = tokens.shape[0]
    heads_here = q_weight.shape[1] // HD
    own_rank = lax.axis_index("dp")
    kv_all = lax.all_gather(kv_weight, "head", axis=1, tiled=True)
    kv_head = lax.axis_index("head") * KVH // lax.axis_size("head")
    key_cols = lax.dynamic_slice_in_dim(kv_all, kv_head * HD, HD, 1)
    value_cols = lax.dynamic_slice_in_dim(kv_all, (KVH + kv_head) * HD, HD, 1)
    pair_cols = jnp.concatenate([key_cols, value_cols], axis=1)

    def add_rows(shard_rows):
        return jnp.dot(tokens, shard_rows, preferred_element_type=jnp.float32)

    q_sum = add_rows(lax.all_gather(q_weight, "dp", axis=0, tiled=True))
    pair_sum = add_rows(lax.all_gather(pair_cols, "dp", axis=0, tiled=True))
    lengths = lax.dynamic_index_in_dim(doc_lengths, own_rank, 0, keepdims=False)
    doc_ids, positions = doc_layout(lengths, rows_here)
    places = jnp.arange(rows_here, dtype=jnp.int32)
    queries = norm_rope(q_sum.reshape(rows_here, heads_here, HD), q_gain, positions)
    key_rows = norm_rope(pair_sum[:, :HD].reshape(rows_here, 1, HD), k_gain, positions)[:, 0]
    values = pair_sum[:, HD:].astype(jnp.bfloat16)
    scores = jnp.einsum(
        "qhd,td->hqt", queries, key_rows, preferred_element_type=jnp.float32
    ) * HD ** (-0.5)
    allowed = (doc_ids[:, None] == doc_ids[None, :]) & (places[:, None] >= places[None, :])
    weights = jnp.where(allowed[None], jnp.exp(scores), 0.0)
    probs = (weights / jnp.sum(weights, axis=-1, keepdims=True)).astype(jnp.bfloat16)
    mixed_out = jnp.einsum("hqt,td->qhd", probs, values, preferred_element_type=jnp.float32)
    return mixed_out.astype(jnp.bfloat16).reshape(rows_here, heads_here * HD)


def solution(mesh):
    placed = (P("dp", None), P("dp", "head"), P("dp", "head"), P(), P(), P())
    return jax.shard_map(
        shards, mesh=mesh, in_specs=placed, out_specs=P("dp", "head"), check_vma=False
    )
```

profile of v0, /device:TPU:0, one launch (start us, length us, event | category | flops | bytes accessed | tf_op | source)
XLA Modules:
  0.0 347.7 jit_solution(16355947577026202582)
XLA Ops:
  6.5 0.7 all-gather.4.cloned.1.call-update
  7.3 21.2 %all-gather.4.cloned.1.call-done = bf16[512,1024]{1,0:T(8,128)(2,1)} async-done(((bf16[512,256]{1,0:T(8,128)(2,1)}), bf16[512,1024]{1,0:T(8,128)(2,1)}) %all-gather.4.cloned.1.call-update) | async-done | bytes 1048592 | tf_op jit(solution)/shard_map/all_gather | solution.py:47
  28.5 1.0 constant_dynamic-slice_fusion.2
  29.5 0.7 pad_maximum_fusion
  30.3 0.7 all-gather.8.cloned.1.call-update
  31.0 0.7 fusion.23
  31.8 0.1 reduce.2
  31.9 0.1 convert_reduce_fusion
  32.0 0.2 fusion.8
  32.3 1.0 multiply_cosine_fusion
  33.2 46.7 %all-gather.6.cloned.1.call-done = bf16[4096,256]{1,0:T(8,128)(2,1)} async-done(((bf16[512,256]{1,0:T(8,128)(2,1)}), bf16[4096,256]{1,0:T(8,128)(2,1)}) %all-gather.6.cloned.1.call-update) | async-done | bytes 2097168 | tf_op jit(solution)/shard_map/all_gather | solution.py:57
  79.9 4.1 %convolution_bitcast_fusion = f32[512,256]{0,1:T(8,128)S(1)} fusion(bf16[4096,256]{1,0:T(8,128)(2,1)} %all-gather.6.cloned.1.call-done, bf16[512,4096]{1,0:T(8,128)(2,1)} %param.6), kind=kOutput, calls=%fused_computation.14 | convolution fusion | flops 1073741824 | bytes 6815744 | tf_op jit(solution)/shard_map/dot_general | solution.py:54
  84.2 0.6 fusion.22
  84.8 223.5 %all-gather.8.cloned.1.call-done = bf16[4096,2048]{1,0:T(8,128)(2,1)} async-done(((bf16[512,2048]{1,0:T(8,128)(2,1)}), bf16[4096,2048]{1,0:T(8,128)(2,1)}) %all-gather.8.cloned.1.call-update) | async-done | bytes 16777232 | tf_op jit(solution)/shard_map/all_gather | solution.py:56
  308.2 12.8 %fusion.28 = f32[512,2048]{1,0:T(8,128)S(1)} fusion(bf16[512,4096]{1,0:T(8,128)(2,1)} %param.6, bf16[4096,2048]{1,0:T(8,128)(2,1)} %all-gather.8.cloned.1.call-done), kind=kOutput, calls=%fused_computation.54 | convolution fusion | flops 8589934592 | bytes 25165824 | tf_op jit(solution)/shard_map/dot_general | solution.py:54
  321.1 0.9 copy.39
  322.1 1.0 copy-done
  323.1 1.2 multiply_reduce_fusion
  324.2 0.1 copy.30
  324.3 3.6 %fusion.2 = f32[512,16,128]{2,0,1:T(8,128)S(1)} fusion(f32[128]{0:T(128)S(1)} %copy-done.2, f32[512,16]{0,1:T(8,128)S(1)} %add_rsqrt_fusion, f32[512,2048]{1,0:T(8,128)} %copy-done), kind=kLoop, calls=%fused_computation.5 | loop fusion | flops 2097152 | bytes 8421888 | tf_op jit(solution)/shard_map/mul | solution.py:28
  328.0 1.5 subtract_convert_fusion
  329.4 5.0 %fusion = (f32[16,512]{1,0:T(8,128)S(1)}, f32[512,512,16]{1,0,2:T(8,128)S(1)}) fusion(pred[512,512]{0,1:T(8,128)(4,1)S(1)} %fusion.8, bf16[512,16,64]{2,0,1:T(8,128)(2,1)S(1)} %get-tuple-element.8, bf16[512,16,64]{2,0,1:T(8,128)(2,1)S(1)} %get-tuple-element.7, bf16[512,64]{0,1:T(8,128)(2,1)S(1)} %get-tuple-element.12, bf16[512,64]{0,1:T(8,128)(2,1)S(1)} %get-tuple-element.11), kind=kOutput, calls=%fused_computation.2 | convolution fusion | flops 1090772992 | bytes 19300352 | tf_op jit(solution)/shard_map/qhd,td->hqt/dot_general | solution.py:64
  334.4 4.4 %fusion.7 = bf16[128,16,512]{2,0,1:T(8,128)(2,1)S(1)} fusion(f32[512,512,16]{1,0,2:T(8,128)S(1)} %get-tuple-element.18, f32[16,512]{1,0:T(8,128)S(1)} %get-tuple-element.17, pred[512,512]{0,1:T(8,128)(4,1)S(1)} %fusion.8, f32[512,256]{0,1:T(8,128)S(1)} %convolution_bitcast_fusion), kind=kOutput, calls=%fused_computation.13 | convolution fusion | flops 1091567616 | bytes 19300352 | tf_op jit(solution)/shard_map/hqt,td->qhd/dot_general | solution.py:70
  338.8 2.4 copy.34
  (17 shorter events, 0.4 us)
Async XLA Ops:
  6.5 22.0 %all-gather.4.cloned.1.call-start = ((), (), s32[]{:S(2)}) async-start(), calls=%async_computation | async-start | bytes 1310720 | tf_op jit(solution)/shard_map/all_gather | solution.py:47
  7.3 72.7 %all-gather.6.cloned.1.call-start = ((), (), s32[]{:S(2)}) async-start(), calls=%async_computation.1 | async-start | bytes 2359296 | tf_op jit(solution)/shard_map/all_gather | solution.py:57
  30.2 278.0 %all-gather.8.cloned.1.call-start = ((), (), s32[]{:S(2)}) async-start(), calls=%async_computation.2 | async-start | bytes 18874368 | tf_op jit(solution)/shard_map/all_gather | solution.py:56
  32.2 51.9 %copy-start.1 = (f32[128]{0:T(128)S(1)}, f32[128]{0:T(128)}, u32[]{:S(2)}) copy-start(f32[128]{0:T(128)} %param.10) | copy-start | bytes 1540
  321.1 2.0 copy-start
  323.0 1.3 copy-start.2
Sparse Core Ops, SparseCore 0:
  8.9 19.5 all-gather.3
  30.6 49.2 all-gather.5
  82.1 226.1 all-gather.7
where the time goes:
time: 348 us
  waiting for transfers between devices  293 us (84%)
  matrix products  26.3 us (8%)
  between operations  13.3 us (4%)
  other arithmetic  9.14 us (3%)
  local copies, waits for them, and re-layouts  6.19 us (2%)
    all_gather x1, waiting for transfers between devices, shards(): q_sum = add_rows(lax.all_gather(q_weight, 'dp', axis=0, tiled=True))  223 us
    all_gather x1, waiting for transfers between devices, shards(): pair_sum = add_rows(lax.all_gather(pair_cols, 'dp', axis=0, tiled=True))  46.7 us
    all_gather x1, waiting for transfers between devices, shards(): kv_all = lax.all_gather(kv_weight, 'head', axis=1, tiled=True)  21.2 us
    dot_general x2, matrix products, add_rows(): return jnp.dot(tokens, shard_rows, preferred_element_type=jnp.float32)  17 us
  transfers between devices with their start and end apart: 3, of which 3 were waited for; matrix products, arithmetic and copies ran while one was open for 2% of the time, Pallas kernels for 0%

commit v1 on v0

v1 whole, which is shorter than its diff:
```python
import functools
import math

import jax
import jax.numpy as jnp
from jax import lax
from jax.experimental import pallas as pl
from jax.experimental.pallas import tpu as pltpu
from jax.sharding import PartitionSpec as P

KVH = 4
HD = 128


theta_base = 1000000.0
norm_eps = 1e-06

CHUNK_SHARES = (4, 4, 4, 4)
KV_WITH = 1


def doc_starts(lengths, count):
    doc_ends = jnp.cumsum(lengths)
    places = jnp.arange(count, dtype=jnp.int32)
    passed = (places[:, None] >= doc_ends[None, :]).astype(jnp.int32)
    return jnp.sum(passed * lengths[None, :], axis=1)


def rope_tables(positions):
    half_width = HD // 2
    frequency = jnp.exp(
        jnp.arange(half_width, dtype=jnp.float32) * (-2.0 * math.log(theta_base) / HD)
    )
    angles = positions.astype(jnp.float32)[:, None] * frequency[None, :]
    cosine, sine = jnp.cos(angles), jnp.sin(angles)
    return (
        jnp.concatenate([cosine, cosine], axis=1),
        jnp.concatenate([-sine, sine], axis=1),
    )


def norm_rope(raw, gain, cosine, sine, swap_halves):
    inv_rms = lax.rsqrt(jnp.mean(raw * raw, axis=-1, keepdims=True) + norm_eps)
    normed = raw * inv_rms * gain
    return (normed * cosine + swap_halves(normed) * sine).astype(jnp.bfloat16)


def attend_kernel(block, mine, other, keys, values, cosine, sine, starts, gain, out):
    rows = mine.shape[0]
    raw = mine[...] + other[...].astype(jnp.float32)
    queries = norm_rope(
        raw, gain[...], cosine[...], sine[...], lambda n: pltpu.roll(n, HD // 2, 1)
    )
    for first in range(0, rows, block):
        here, upto = slice(first, first + block), first + block
        scores = lax.dot_general(
            queries[here], keys[:upto, :], (((1,), (1,)), ((), ())),
            preferred_element_type=jnp.float32,
        ) * HD ** (-0.5)
        col = lax.broadcasted_iota(jnp.int32, scores.shape, 1)
        row = lax.broadcasted_iota(jnp.int32, scores.shape, 0) + first
        allowed = (col >= starts[here, :]) & (col <= row)
        weights = jnp.where(allowed, jnp.exp(scores), 0.0)
        probs = (weights / jnp.sum(weights, axis=-1, keepdims=True)).astype(jnp.bfloat16)
        mixed = jnp.dot(probs, values[:upto, :], preferred_element_type=jnp.float32)
        out[here, :] = mixed.astype(out.dtype)


def attend(mine, other, keys, values, cosine, sine, starts, gain):
    rows, cols = mine.shape
    block = 128 if rows % 128 == 0 else rows
    by_head = pl.BlockSpec((rows, HD), lambda h: (0, h))
    whole = lambda a: pl.BlockSpec(a.shape, lambda h: (0, 0))
    return pl.pallas_call(
        functools.partial(attend_kernel, block),
        grid=(cols // HD,),
        out_shape=jax.ShapeDtypeStruct((rows, cols), jnp.bfloat16),
        in_specs=[by_head, by_head] + [whole(a) for a in (keys, values, cosine, sine, starts, gain)],
        out_specs=by_head,
        compiler_params=pltpu.CompilerParams(vmem_limit_bytes=32 << 20),
        cost_estimate=pl.CostEstimate(
            flops=4 * rows * rows * cols, bytes_accessed=8 * rows * cols,
            transcendentals=rows * rows * cols // HD,
        ),
        name="attend",
    )(mine, other, keys, values, cosine, sine, starts, gain)


def shards(tokens, q_weight, kv_weight, q_gain, k_gain, doc_lengths):
    rows, depth = tokens.shape[0], q_weight.shape[0]
    cols = q_weight.shape[1]
    n_dp, n_head = lax.axis_size("dp"), lax.axis_size("head")
    n_line = n_dp // 2
    n_pairs = n_line // 2
    rank, head = lax.axis_index("dp"), lax.axis_index("head")
    spot, side = rank // 2, rank % 2
    pair = spot // 2

    hub_of = lambda g: 2 * g + 1 if 2 * g < n_pairs else 2 * g
    hub_bit = jnp.where(2 * pair < n_pairs, 1, 0)
    is_hub = spot % 2 == hub_bit

    def on_line(moves):
        return [(2 * a + s, 2 * b + s) for a, b in moves for s in range(2)]

    swap = on_line([(a, a ^ 1) for a in range(n_line)])
    shift = [
        on_line([(hub_of(g), hub_of((g + s) % n_pairs)) for g in range(n_pairs)])
        for s in range(n_pairs)
    ]
    outward = on_line([(hub_of(g), hub_of(g) ^ 1) for g in range(n_pairs)])
    across = [(a, a ^ 1) for a in range(n_dp)]
    send = lambda value, moves: lax.ppermute(value, "dp", moves)

    order = [spot, spot ^ 1]
    for s in range(1, n_pairs):
        source = (pair - s + n_pairs) % n_pairs
        hub = 2 * source + jnp.where(2 * source < n_pairs, 1, 0)
        order += [hub, hub ^ 1]

    def features(block, of_side):
        return [
            lax.dynamic_slice_in_dim(block, (2 * at + of_side) * depth, depth, 1) for at in order
        ]

    share = rows // n_head
    quarter = lax.dynamic_slice_in_dim(tokens, head * share, share, 0)
    own_tokens = features(tokens, side)
    their_quarter = send(jnp.concatenate(features(quarter, 1 - side), axis=1), across)
    their_tokens = lax.all_gather(their_quarter, "head", axis=0, tiled=True)

    kv_all = lax.all_gather(kv_weight, "head", axis=1, tiled=True)
    kv_head = head * KVH // n_head
    kv_cols = jnp.concatenate(
        [
            lax.dynamic_slice_in_dim(kv_all, kv_head * HD, HD, 1),
            lax.dynamic_slice_in_dim(kv_all, (KVH + kv_head) * HD, HD, 1),
        ],
        axis=1,
    )

    def gather(piece):
        pieces = [piece, send(piece, swap)]
        for s in range(1, n_pairs):
            for part in pieces[:2]:
                inward = send(part, shift[s])
                pieces.append(jnp.where(is_hub, inward, send(inward, outward)))
        return pieces

    def half_sums(pieces):
        mine = sum(
            jnp.dot(t, w, preferred_element_type=jnp.float32)
            for t, w in zip(own_tokens, pieces, strict=True)
        )
        theirs = sum(
            jnp.dot(their_tokens[:, i * depth : (i + 1) * depth], w, preferred_element_type=jnp.float32)
            for i, w in enumerate(pieces)
        )
        return mine, theirs

    lengths = lax.dynamic_index_in_dim(doc_lengths, rank, 0, keepdims=False)
    starts = doc_starts(lengths, rows)
    cosine, sine = rope_tables(jnp.arange(rows, dtype=jnp.int32) - starts)

    heads = cols // HD
    bounds, taken = [], 0
    for part in CHUNK_SHARES:
        count = part * heads // sum(CHUNK_SHARES)
        bounds.append((taken * HD, (taken + count) * HD))
        taken += count
    sums = []
    for j, (low, high) in enumerate(bounds):
        piece = q_weight[:, low:high]
        if j == KV_WITH:
            piece = jnp.concatenate([piece, kv_cols], axis=1)
        mine, theirs = half_sums(gather(piece))
        width = high - low
        if j == KV_WITH:
            kv = mine[:, width:] + send(theirs[:, width:], across)
            mine, theirs = mine[:, :width], theirs[:, :width]
        sums.append((mine, send(theirs.astype(jnp.bfloat16), across)))
    keys = norm_rope(
        kv[:, :HD], k_gain, cosine, sine,
        lambda n: jnp.concatenate([n[:, HD // 2 :], n[:, : HD // 2]], axis=1),
    )
    values = kv[:, HD:].astype(jnp.bfloat16)
    parts = [
        attend(mine, other, keys, values, cosine, sine, starts[:, None], q_gain[None, :])
        for mine, other in sums
    ]
    return jnp.concatenate(parts, axis=1)


def solution(mesh):
    placed = (P("dp", None), P("dp", "head"), P("dp", "head"), P(), P(), P())
    return jax.shard_map(
        shards, mesh=mesh, in_specs=placed, out_specs=P("dp", "head"), check_vma=False
    )
```

time: 348 us -> 235 us (0.68)
  waiting for transfers between devices: 293 us -> 95.7 us
  starting transfers between devices: 0.08 us -> 40.6 us
  Pallas kernels: 0 us -> 24.1 us
  matrix products: 26.3 us -> 43.6 us
    all_gather x2 -> x1, waiting for transfers between devices: 270 us -> 0.01 us  [shards(): their_tokens = lax.all_gather(their_quarter, 'head', axis=0, tiled=True)]
    ppermute x0 -> x26, waiting for transfers between devices: none -> 95.6 us  [shards(): send = lambda value, moves: lax.ppermute(value, 'dp', moves)]
    ppermute x0 -> x26, starting transfers between devices: none -> 40.6 us  [shards(): send = lambda value, moves: lax.ppermute(value, 'dp', moves)]
    pallas_call x0 -> x4, Pallas kernels: none -> 24.1 us  [attend(): pl.pallas_call(functools.partial(attend_kernel, block), grid=(cols // HD,...]
    all_gather x1, waiting for transfers between devices: 21.2 us -> 0.02 us  [shards(): kv_all = lax.all_gather(kv_weight, 'head', axis=1, tiled=True)]
    dot_general x4 -> x32, matrix products: 26.3 us -> 43.6 us  [the longest x16 26.8 us: half_sums(): jnp.dot(t, w, preferred_element_type=jnp.float32)]
    mul x2 -> x1, other arithmetic: 3.72 us -> 0.13 us  [norm_rope(): normed = raw * inv_rms * gain]
  transfers between devices with their start and end apart: 3 -> 28, of which waited for: 3 -> 12; matrix products, arithmetic and copies ran while one was open for 2% -> 22% of each run, Pallas kernels for 0% -> 8%
where the time goes in v1:
time: 235 us; the launch traced here: 234 us
  waiting for transfers between devices  95.7 us (41%)
  matrix products  43.6 us (19%)
  starting transfers between devices  40.6 us (17%)
  Pallas kernels  24.1 us (10%)
  between operations  14.3 us (6%)
  local copies, waits for them, and re-layouts  9.25 us (4%)
  other arithmetic  6.56 us (3%)
    ppermute x26, waiting for transfers between devices, shards(): send = lambda value, moves: lax.ppermute(value, 'dp', moves)  95.6 us
    ppermute x26, starting transfers between devices, shards(): send = lambda value, moves: lax.ppermute(value, 'dp', moves)  40.6 us
    dot_general x16, matrix products, half_sums(): jnp.dot(t, w, preferred_element_type=jnp.float32)  26.8 us
    pallas_call x4, Pallas kernels, attend(): pl.pallas_call(functools.partial(attend_kernel, block), grid=(cols // HD,...  24.1 us
    dot_general x16, matrix products, half_sums(): jnp.dot(their_tokens[:, i * depth:(i + 1) * depth], w, preferred_element_...  16.9 us
  transfers between devices with their start and end apart: 28, of which 12 were waited for; matrix products, arithmetic and copies ran while one was open for 22% of the time, Pallas kernels for 8%

profile of v1, /device:TPU:0, one launch (start us, length us, event | category | flops | bytes accessed | tf_op | source)
XLA Modules:
  0.0 234.1 jit_solution(1013872616958547617)
XLA Ops:
  6.5 2.9 %fusion.75 = (bf16[512,512]{1,0:T(8,128)(2,1)}, bf16[512,512]{1,0:T(8,128)(2,1)}, bf16[512,512]{1,0:T(8,128)(2,1)}, bf16[512,512]{1,0:T(8,128)(2,1)}) fusion(bf16[512,2048]{1,0:T(8,128)(2,1)} %param.7), kind=kLoop, calls=%fused_computation.124 | loop fusion | bytes 4194304 | tf_op jit(solution)/shard_map/slice | solution.py:173
  9.4 3.0 %collective-permute-start.20 = (bf16[512,512]{1,0:T(8,128)(2,1)}, bf16[512,512]{1,0:T(8,128)(2,1)}, u32[]{:S(2)}, u32[]{:S(2)}) collective-permute-start(bf16[512,512]{1,0:T(8,128)(2,1)} %get-tuple-element.13), channel_id=1, source_target_pairs={{0,8},{4,12},{8,0},{12,4},{16,24},{20,28},{24,16},{28,20},{1,9},{5... | collective-permute-start | bytes 1572872 | tf_op jit(solution)/shard_map/ppermute | solution.py:113
  13.9 3.7 %collective-permute-start.14 = (bf16[512,512]{1,0:T(8,128)(2,1)}, bf16[512,512]{1,0:T(8,128)(2,1)}, u32[]{:S(2)}, u32[]{:S(2)}) collective-permute-start(bf16[512,512]{1,0:T(8,128)(2,1)} %get-tuple-element.14), channel_id=1, source_target_pairs={{0,8},{4,12},{8,0},{12,4},{16,24},{20,28},{24,16},{28,20},{1,9},{5... | collective-permute-start | bytes 1572872 | tf_op jit(solution)/shard_map/ppermute | solution.py:113
  24.0 2.5 %fusion.39 = f32[512,512]{1,0:T(8,128)} fusion(bf16[512,4096]{1,0:T(8,128)(2,1)} %param.6, s32[]{:T(128)S(6)} %select_n.121, bf16[512,2048]{1,0:T(8,128)(2,1)S(1)} %copy-done.3), kind=kOutput, calls=%fused_computation.74 | convolution fusion | flops 268435456 | bytes 2097156 | tf_op jit(solution)/shard_map/dot_general | solution.py:152
  28.2 2.5 %fusion.45 = f32[512,512]{1,0:T(8,128)} fusion(bf16[512,4096]{1,0:T(8,128)(2,1)} %param.6, s32[]{:T(128)S(6)} %select_n.121, bf16[512,2048]{1,0:T(8,128)(2,1)S(1)} %copy-done.3), kind=kOutput, calls=%fused_computation.80 | convolution fusion | flops 268435456 | bytes 2097156 | tf_op jit(solution)/shard_map/dot_general | solution.py:152
  32.5 1.9 collective-permute-done.5
  36.9 2.0 convolution_add_fusion.5
  41.8 2.6 %convolution_add_fusion.11 = f32[512,512]{1,0:T(8,128)} fusion(f32[512,512]{1,0:T(8,128)S(1)} %fusion.41, bf16[512,512]{1,0:T(8,128)(2,1)} %collective-permute-done.14, bf16[512,4096]{1,0:T(8,128)(2,1)} %param.6, s32[]{:T(128)S(6)} %select_n.122), kind=kOutput, calls=%fused_computation.14 | convolution fusion | flops 268697600 | bytes 3145732 | tf_op jit(solution)/shard_map/dot_general | solution.py:152
  44.4 5.2 %collective-permute-done = bf16[512,512]{1,0:T(8,128)(2,1)} collective-permute-done((bf16[512,512]{1,0:T(8,128)(2,1)}, bf16[512,512]{1,0:T(8,128)(2,1)}, u32[]{:S(2)}, u32[]{:S(2)}) %collective-permute-start) | collective-permute-done | bytes 524320 | tf_op jit(solution)/shard_map/ppermute | solution.py:113
  55.7 3.8 %collective-permute-done.22 = bf16[512,512]{1,0:T(8,128)(2,1)S(1)} collective-permute-done((bf16[512,512]{1,0:T(8,128)(2,1)}, bf16[512,512]{1,0:T(8,128)(2,1)S(1)}, u32[]{:S(2)}, u32[]{:S(2)}) %collective-permute-start.22) | collective-permute-done | bytes 524320 | tf_op jit(solution)/shard_map/ppermute | solution.py:113
  65.8 5.6 %collective-permute-done.16 = bf16[512,512]{1,0:T(8,128)(2,1)} collective-permute-done((bf16[512,512]{1,0:T(8,128)(2,1)}, bf16[512,512]{1,0:T(8,128)(2,1)}, u32[]{:S(2)}, u32[]{:S(2)}) %collective-permute-start.16) | collective-permute-done | bytes 524320 | tf_op jit(solution)/shard_map/ppermute | solution.py:113
  72.2 3.9 %collective-permute-start.7 = (bf16[512,768]{1,0:T(8,128)(2,1)S(1)}, bf16[512,768]{1,0:T(8,128)(2,1)S(1)}, u32[]{:S(2)}, u32[]{:S(2)}) collective-permute-start(bf16[512,768]{1,0:T(8,128)(2,1)S(1)} %pad_maximum_fusion.1), channel_id=1, source_target_pairs={{0,8},{4,12},{8,0},{12,4},{16,24},{20,28},{24,16},{28,20},{1,9},{5... | collective-permute-start | bytes 2359304 | tf_op jit(solution)/shard_map/ppermute | solution.py:113
  77.7 4.9 %collective-permute-done.2 = bf16[512,512]{1,0:T(8,128)(2,1)} collective-permute-done((bf16[512,512]{1,0:T(8,128)(2,1)}, bf16[512,512]{1,0:T(8,128)(2,1)}, u32[]{:S(2)}, u32[]{:S(2)}) %collective-permute-start.2) | collective-permute-done | bytes 524320 | tf_op jit(solution)/shard_map/ppermute | solution.py:113
  86.8 7.1 %collective-permute-done.24 = bf16[512,512]{1,0:T(8,128)(2,1)} collective-permute-done((bf16[512,512]{1,0:T(8,128)(2,1)}, bf16[512,512]{1,0:T(8,128)(2,1)}, u32[]{:S(2)}, u32[]{:S(2)}) %collective-permute-start.24) | collective-permute-done | bytes 524320 | tf_op jit(solution)/shard_map/ppermute | solution.py:113
  96.7 13.9 %collective-permute-done.7 = bf16[512,768]{1,0:T(8,128)(2,1)S(1)} collective-permute-done((bf16[512,768]{1,0:T(8,128)(2,1)S(1)}, bf16[512,768]{1,0:T(8,128)(2,1)S(1)}, u32[]{:S(2)}, u32[]{:S(2)}) %collective-permute-start.7) | collective-permute-done | bytes 786464 | tf_op jit(solution)/shard_map/ppermute | solution.py:113
  112.2 9.7 %collective-permute-done.18 = bf16[512,512]{1,0:T(8,128)(2,1)S(1)} collective-permute-done((bf16[512,512]{1,0:T(8,128)(2,1)}, bf16[512,512]{1,0:T(8,128)(2,1)S(1)}, u32[]{:S(2)}, u32[]{:S(2)}) %collective-permute-start.18) | collective-permute-done | bytes 524320 | tf_op jit(solution)/shard_map/ppermute | solution.py:113
  122.4 10.8 %collective-permute-done.4 = bf16[512,512]{1,0:T(8,128)(2,1)S(1)} collective-permute-done((bf16[512,512]{1,0:T(8,128)(2,1)}, bf16[512,512]{1,0:T(8,128)(2,1)S(1)}, u32[]{:S(2)}, u32[]{:S(2)}) %collective-permute-start.4) | collective-permute-done | bytes 524320 | tf_op jit(solution)/shard_map/ppermute | solution.py:113
  138.6 11.4 %collective-permute-done.9 = bf16[512,768]{1,0:T(8,128)(2,1)S(1)} collective-permute-done((bf16[512,768]{1,0:T(8,128)(2,1)S(1)}, bf16[512,768]{1,0:T(8,128)(2,1)S(1)}, u32[]{:S(2)}, u32[]{:S(2)}) %collective-permute-start.9) | collective-permute-done | bytes 786464 | tf_op jit(solution)/shard_map/ppermute | solution.py:113
  179.3 16.3 %collective-permute-done.12 = f32[512,256]{1,0:T(8,128)S(1)} collective-permute-done((f32[512,256]{1,0:T(8,128)S(1)}, f32[512,256]{1,0:T(8,128)S(1)}, u32[]{:S(2)}, u32[]{:S(2)}) %collective-permute-start.12) | collective-permute-done | bytes 524320 | tf_op jit(solution)/shard_map/ppermute | solution.py:113
  196.5 6.0 %attend.7 = bf16[512,512]{1,0:T(8,128)(2,1)S(1)} custom-call(f32[512,512]{1,0:T(8,128)S(1)} %convolution_add_fusion.3.mine, bf16[512,512]{1,0:T(8,128)(2,1)S(1)} %collective-permute-done.25.other, bf16[512,128]{1,0:T(8,128)(2,1)S(1)} %get-tuple-element.5.keys, bf16[512,128]{1,0:T(8,128)(2,1)S(1)} %slice.140.values, f32[512,128]{1,0:T(8,128)S(1)} %get-tuple-element.17.cosine, ...), custom_call_target="tpu_custom_call" | custom-call | flops 536870912 | bytes 2097152 | tf_op jit(solution)/shard_map/attend/pallas_call | solution.py:74
  202.6 6.0 %attend.6 = bf16[512,512]{1,0:T(8,128)(2,1)S(1)} custom-call(f32[512,512]{1,0:T(8,128)S(1)} %convolution_add_fusion.9.mine, bf16[512,512]{1,0:T(8,128)(2,1)S(1)} %collective-permute-done.19.other, bf16[512,128]{1,0:T(8,128)(2,1)S(1)} %get-tuple-element.5.keys, bf16[512,128]{1,0:T(8,128)(2,1)S(1)} %slice.140.values, f32[512,128]{1,0:T(8,128)S(1)} %get-tuple-element.17.cosine, ...), custom_call_target="tpu_custom_call" | custom-call | flops 536870912 | bytes 2097152 | tf_op jit(solution)/shard_map/attend/pallas_call | solution.py:74
  208.6 5.0 %collective-permute-done.13.other = bf16[512,512]{1,0:T(8,128)(2,1)S(1)} collective-permute-done((bf16[512,512]{1,0:T(8,128)(2,1)S(1)}, bf16[512,512]{1,0:T(8,128)(2,1)S(1)}, u32[]{:S(2)}, u32[]{:S(2)}) %collective-permute-start.13) | collective-permute-done | bytes 524320 | tf_op jit(solution)/shard_map/ppermute | solution.py:113
  213.6 6.0 %attend.5 = bf16[512,512]{1,0:T(8,128)(2,1)S(1)} custom-call(f32[512,512]{1,0:T(8,128)S(1)} %slice.88.mine, bf16[512,512]{1,0:T(8,128)(2,1)S(1)} %collective-permute-done.13.other, bf16[512,128]{1,0:T(8,128)(2,1)S(1)} %get-tuple-element.5.keys, bf16[512,128]{1,0:T(8,128)(2,1)S(1)} %slice.140.values, f32[512,128]{1,0:T(8,128)S(1)} %get-tuple-element.17.cosine, ...), custom_call_target="tpu_custom_call" | custom-call | flops 536870912 | bytes 2097152 | tf_op jit(solution)/shard_map/attend/pallas_call | solution.py:74
  219.6 6.0 %attend.4 = bf16[512,512]{1,0:T(8,128)(2,1)S(1)} custom-call(f32[512,512]{1,0:T(8,128)S(1)} %convolution_add_fusion.15.mine, bf16[512,512]{1,0:T(8,128)(2,1)S(1)} %collective-permute-done.6.other, bf16[512,128]{1,0:T(8,128)(2,1)S(1)} %get-tuple-element.5.keys, bf16[512,128]{1,0:T(8,128)(2,1)S(1)} %slice.140.values, f32[512,128]{1,0:T(8,128)S(1)} %get-tuple-element.17.cosine, ...), custom_call_target="tpu_custom_call" | custom-call | flops 536870912 | bytes 2097152 | tf_op jit(solution)/shard_map/attend/pallas_call | solution.py:74
  (155 shorter events, 77.1 us)
Async XLA Ops:
  6.5 57.0 %all-gather.5.cloned.1.call-start = ((), (), s32[]{:S(2)}) async-start(), calls=%async_computation.1 | async-start | bytes 1310720 | tf_op jit(solution)/shard_map/all_gather | solution.py:132
  9.4 26.0 %collective-permute-start.20 = (bf16[512,512]{1,0:T(8,128)(2,1)}, bf16[512,512]{1,0:T(8,128)(2,1)}, u32[]{:S(2)}, u32[]{:S(2)}) collective-permute-start(bf16[512,512]{1,0:T(8,128)(2,1)} %get-tuple-element.13), channel_id=1, source_target_pairs={{0,8},{4,12},{8,0},{12,4},{16,24},{20,28},{24,16},{28,20},{1,9},{5... | collective-permute-start | bytes 1572872 | tf_op jit(solution)/shard_map/ppermute | solution.py:113
  12.4 26.5 %collective-permute-start.21 = (bf16[512,512]{1,0:T(8,128)(2,1)}, bf16[512,512]{1,0:T(8,128)(2,1)}, u32[]{:S(2)}, u32[]{:S(2)}) collective-permute-start(bf16[512,512]{1,0:T(8,128)(2,1)} %get-tuple-element.13), channel_id=1, source_target_pairs={{8,16},{12,20},{16,8},{20,12},{9,17},{13,21},{17,9},{21,13},{10,18... | collective-permute-start | bytes 1572872 | tf_op jit(solution)/shard_map/ppermute | solution.py:113
  13.9 26.6 %collective-permute-start.14 = (bf16[512,512]{1,0:T(8,128)(2,1)}, bf16[512,512]{1,0:T(8,128)(2,1)}, u32[]{:S(2)}, u32[]{:S(2)}) collective-permute-start(bf16[512,512]{1,0:T(8,128)(2,1)} %get-tuple-element.14), channel_id=1, source_target_pairs={{0,8},{4,12},{8,0},{12,4},{16,24},{20,28},{24,16},{28,20},{1,9},{5... | collective-permute-start | bytes 1572872 | tf_op jit(solution)/shard_map/ppermute | solution.py:113
  17.6 35.2 %collective-permute-start.15 = (bf16[512,512]{1,0:T(8,128)(2,1)}, bf16[512,512]{1,0:T(8,128)(2,1)}, u32[]{:S(2)}, u32[]{:S(2)}) collective-permute-start(bf16[512,512]{1,0:T(8,128)(2,1)} %get-tuple-element.14), channel_id=1, source_target_pairs={{8,16},{12,20},{16,8},{20,12},{9,17},{13,21},{17,9},{21,13},{10,18... | collective-permute-start | bytes 1572872 | tf_op jit(solution)/shard_map/ppermute | solution.py:113
  22.9 129.7 %all-gather.3.cloned.1.call-start = ((), (), s32[]{:S(2)}) async-start(), calls=%async_computation | async-start | bytes 2621440 | tf_op jit(solution)/shard_map/all_gather | solution.py:130
  35.4 19.0 %collective-permute-start.1 = (bf16[512,512]{1,0:T(8,128)(2,1)}, bf16[512,512]{1,0:T(8,128)(2,1)}, u32[]{:S(2)}, u32[]{:S(2)}) collective-permute-start(bf16[512,512]{1,0:T(8,128)(2,1)} %get-tuple-element.11), channel_id=1, source_target_pairs={{8,16},{12,20},{16,8},{20,12},{9,17},{13,21},{17,9},{21,13},{10,18... | collective-permute-start | bytes 1572872 | tf_op jit(solution)/shard_map/ppermute | solution.py:113
  38.9 21.8 %collective-permute-start.23 = (bf16[512,512]{1,0:T(8,128)(2,1)}, bf16[512,512]{1,0:T(8,128)(2,1)}, u32[]{:S(2)}, u32[]{:S(2)}) collective-permute-start(bf16[512,512]{1,0:T(8,128)(2,1)} %collective-permute-done.20), channel_id=1, source_target_pairs={{8,16},{12,20},{16,8},{20,12},{9,17},{13,21},{17,9},{21,13},{10,18... | collective-permute-start | bytes 1572872 | tf_op jit(solution)/shard_map/ppermute | solution.py:113
  49.6 22.5 %collective-permute-start.17 = (bf16[512,512]{1,0:T(8,128)(2,1)}, bf16[512,512]{1,0:T(8,128)(2,1)}, u32[]{:S(2)}, u32[]{:S(2)}) collective-permute-start(bf16[512,512]{1,0:T(8,128)(2,1)} %collective-permute-done.14), channel_id=1, source_target_pairs={{8,16},{12,20},{16,8},{20,12},{9,17},{13,21},{17,9},{21,13},{10,18... | collective-permute-start | bytes 1572872 | tf_op jit(solution)/shard_map/ppermute | solution.py:113
  52.8 31.2 %collective-permute-start.3 = (bf16[512,512]{1,0:T(8,128)(2,1)}, bf16[512,512]{1,0:T(8,128)(2,1)}, u32[]{:S(2)}, u32[]{:S(2)}) collective-permute-start(bf16[512,512]{1,0:T(8,128)(2,1)} %collective-permute-done), channel_id=1, source_target_pairs={{8,16},{12,20},{16,8},{20,12},{9,17},{13,21},{17,9},{21,13},{10,18... | collective-permute-start | bytes 1572872 | tf_op jit(solution)/shard_map/ppermute | solution.py:113
  59.4 23.2 %collective-permute-start.2 = (bf16[512,512]{1,0:T(8,128)(2,1)}, bf16[512,512]{1,0:T(8,128)(2,1)}, u32[]{:S(2)}, u32[]{:S(2)}) collective-permute-start(bf16[512,512]{1,0:T(8,128)(2,1)} %collective-permute-done.1), channel_id=1, source_target_pairs={{8,0},{12,4},{16,24},{20,28},{9,1},{13,5},{17,25},{21,29},{10,2},{... | collective-permute-start | bytes 1572872 | tf_op jit(solution)/shard_map/ppermute | solution.py:113
  60.7 33.2 %collective-permute-start.24 = (bf16[512,512]{1,0:T(8,128)(2,1)}, bf16[512,512]{1,0:T(8,128)(2,1)}, u32[]{:S(2)}, u32[]{:S(2)}) collective-permute-start(bf16[512,512]{1,0:T(8,128)(2,1)} %collective-permute-done.23), channel_id=1, source_target_pairs={{8,0},{12,4},{16,24},{20,28},{9,1},{13,5},{17,25},{21,29},{10,2},{... | collective-permute-start | bytes 1572872 | tf_op jit(solution)/shard_map/ppermute | solution.py:113
  71.4 24.0 %collective-permute-start.8 = (bf16[512,768]{1,0:T(8,128)(2,1)S(1)}, bf16[512,768]{1,0:T(8,128)(2,1)S(1)}, u32[]{:S(2)}, u32[]{:S(2)}) collective-permute-start(bf16[512,768]{1,0:T(8,128)(2,1)S(1)} %pad_maximum_fusion.1), channel_id=1, source_target_pairs={{8,16},{12,20},{16,8},{20,12},{9,17},{13,21},{17,9},{21,13},{10,18... | collective-permute-start | bytes 2359304 | tf_op jit(solution)/shard_map/ppermute | solution.py:113
  72.2 38.5 %collective-permute-start.7 = (bf16[512,768]{1,0:T(8,128)(2,1)S(1)}, bf16[512,768]{1,0:T(8,128)(2,1)S(1)}, u32[]{:S(2)}, u32[]{:S(2)}) collective-permute-start(bf16[512,768]{1,0:T(8,128)(2,1)S(1)} %pad_maximum_fusion.1), channel_id=1, source_target_pairs={{0,8},{4,12},{8,0},{12,4},{16,24},{20,28},{24,16},{28,20},{1,9},{5... | collective-permute-start | bytes 2359304 | tf_op jit(solution)/shard_map/ppermute | solution.py:113
  82.7 39.2 %collective-permute-start.18 = (bf16[512,512]{1,0:T(8,128)(2,1)}, bf16[512,512]{1,0:T(8,128)(2,1)S(1)}, u32[]{:S(2)}, u32[]{:S(2)}) collective-permute-start(bf16[512,512]{1,0:T(8,128)(2,1)} %collective-permute-done.17), channel_id=1, source_target_pairs={{8,0},{12,4},{16,24},{20,28},{9,1},{13,5},{17,25},{21,29},{10,2},{... | collective-permute-start | bytes 1572872 | tf_op jit(solution)/shard_map/ppermute | solution.py:113
  84.0 49.2 %collective-permute-start.4 = (bf16[512,512]{1,0:T(8,128)(2,1)}, bf16[512,512]{1,0:T(8,128)(2,1)S(1)}, u32[]{:S(2)}, u32[]{:S(2)}) collective-permute-start(bf16[512,512]{1,0:T(8,128)(2,1)} %collective-permute-done.3), channel_id=1, source_target_pairs={{8,0},{12,4},{16,24},{20,28},{9,1},{13,5},{17,25},{21,29},{10,2},{... | collective-permute-start | bytes 1572872 | tf_op jit(solution)/shard_map/ppermute | solution.py:113
  95.4 54.6 %collective-permute-start.9 = (bf16[512,768]{1,0:T(8,128)(2,1)S(1)}, bf16[512,768]{1,0:T(8,128)(2,1)S(1)}, u32[]{:S(2)}, u32[]{:S(2)}) collective-permute-start(bf16[512,768]{1,0:T(8,128)(2,1)S(1)} %collective-permute-done.8), channel_id=1, source_target_pairs={{8,0},{12,4},{16,24},{20,28},{9,1},{13,5},{17,25},{21,29},{10,2},{... | collective-permute-start | bytes 2359304 | tf_op jit(solution)/shard_map/ppermute | solution.py:113
  110.7 26.4 %collective-permute-start.10 = (bf16[512,768]{1,0:T(8,128)(2,1)S(1)}, bf16[512,768]{1,0:T(8,128)(2,1)}, u32[]{:S(2)}, u32[]{:S(2)}) collective-permute-start(bf16[512,768]{1,0:T(8,128)(2,1)S(1)} %collective-permute-done.7), channel_id=1, source_target_pairs={{8,16},{12,20},{16,8},{20,12},{9,17},{13,21},{17,9},{21,13},{10,18... | collective-permute-start | bytes 2359304 | tf_op jit(solution)/shard_map/ppermute | solution.py:113
  137.1 34.0 %collective-permute-start.11 = (bf16[512,768]{1,0:T(8,128)(2,1)}, bf16[512,768]{1,0:T(8,128)(2,1)}, u32[]{:S(2)}, u32[]{:S(2)}) collective-permute-start(bf16[512,768]{1,0:T(8,128)(2,1)} %collective-permute-done.10), channel_id=1, source_target_pairs={{8,0},{12,4},{16,24},{20,28},{9,1},{13,5},{17,25},{21,29},{10,2},{... | collective-permute-start | bytes 2359304 | tf_op jit(solution)/shard_map/ppermute | solution.py:113
  158.2 38.3 %collective-permute-start.25 = (bf16[512,512]{1,0:T(8,128)(2,1)S(1)}, bf16[512,512]{1,0:T(8,128)(2,1)S(1)}, u32[]{:S(2)}, u32[]{:S(2)}) collective-permute-start(bf16[512,512]{1,0:T(8,128)(2,1)S(1)} %fusion.2), channel_id=1, source_target_pairs={{0,4},{4,0},{8,12},{12,8},{16,20},{20,16},{24,28},{28,24},{1,5},{5... | collective-permute-start | bytes 1572872 | tf_op jit(solution)/shard_map/ppermute | solution.py:113
  163.8 38.8 %collective-permute-start.19 = (bf16[512,512]{1,0:T(8,128)(2,1)S(1)}, bf16[512,512]{1,0:T(8,128)(2,1)S(1)}, u32[]{:S(2)}, u32[]{:S(2)}) collective-permute-start(bf16[512,512]{1,0:T(8,128)(2,1)S(1)} %fusion.1), channel_id=1, source_target_pairs={{0,4},{4,0},{8,12},{12,8},{16,20},{20,16},{24,28},{28,24},{1,5},{5... | collective-permute-start | bytes 1572872 | tf_op jit(solution)/shard_map/ppermute | solution.py:113
  173.0 22.6 %collective-permute-start.12 = (f32[512,256]{1,0:T(8,128)S(1)}, f32[512,256]{1,0:T(8,128)S(1)}, u32[]{:S(2)}, u32[]{:S(2)}) collective-permute-start(f32[512,256]{1,0:T(8,128)S(1)} %slice.83), channel_id=1, source_target_pairs={{0,4},{4,0},{8,12},{12,8},{16,20},{20,16},{24,28},{28,24},{1,5},{5... | collective-permute-start | bytes 1572872 | tf_op jit(solution)/shard_map/ppermute | solution.py:113
  175.0 44.6 %collective-permute-start.6 = (bf16[512,512]{1,0:T(8,128)(2,1)S(1)}, bf16[512,512]{1,0:T(8,128)(2,1)S(1)}, u32[]{:S(2)}, u32[]{:S(2)}) collective-permute-start(bf16[512,512]{1,0:T(8,128)(2,1)S(1)} %fusion), channel_id=1, source_target_pairs={{0,4},{4,0},{8,12},{12,8},{16,20},{20,16},{24,28},{28,24},{1,5},{5... | collective-permute-start | bytes 1572872 | tf_op jit(solution)/shard_map/ppermute | solution.py:113
  177.8 35.8 %collective-permute-start.13 = (bf16[512,512]{1,0:T(8,128)(2,1)S(1)}, bf16[512,512]{1,0:T(8,128)(2,1)S(1)}, u32[]{:S(2)}, u32[]{:S(2)}) collective-permute-start(bf16[512,512]{1,0:T(8,128)(2,1)S(1)} %slice.139), channel_id=1, source_target_pairs={{0,4},{4,0},{8,12},{12,8},{16,20},{20,16},{24,28},{28,24},{1,5},{5... | collective-permute-start | bytes 1572872 | tf_op jit(solution)/shard_map/ppermute | solution.py:113
  (34 other events, 413.2 us)
Sparse Core Ops, SparseCore 0:
  23.0 15.6 all-gather.4
  40.2 22.5 all-gather.2

commit v2 on v1

v2 whole, which is shorter than its diff:
```python
import functools
import math

import jax
import jax.numpy as jnp
from jax import lax
from jax.experimental import pallas as pl
from jax.experimental.pallas import tpu as pltpu
from jax.sharding import PartitionSpec as P

KVH = 4
HD = 128


theta_base = 1000000.0
norm_eps = 1e-06

RUNS = (3, 2, 4, 3, 3, 1)


def doc_starts(lengths, count):
    doc_ends = jnp.cumsum(lengths)
    places = jnp.arange(count, dtype=jnp.int32)
    passed = (places[:, None] >= doc_ends[None, :]).astype(jnp.int32)
    return jnp.sum(passed * lengths[None, :], axis=1)


def rope_tables(positions):
    half_width = HD // 2
    frequency = jnp.exp(
        jnp.arange(half_width, dtype=jnp.float32) * (-2.0 * math.log(theta_base) / HD)
    )
    angles = positions.astype(jnp.float32)[:, None] * frequency[None, :]
    cosine, sine = jnp.cos(angles), jnp.sin(angles)
    return (
        jnp.concatenate([cosine, cosine], axis=1),
        jnp.concatenate([-sine, sine], axis=1),
    )


def norm_rope(raw, gain, cosine, sine, swap_halves):
    inv_rms = lax.rsqrt(jnp.mean(raw * raw, axis=-1, keepdims=True) + norm_eps)
    normed = raw * inv_rms * gain
    return (normed * cosine + swap_halves(normed) * sine).astype(jnp.bfloat16)


def attend_kernel(block, mine, other, keys, values, cosine, sine, starts, gain, out):
    rows, cols = mine.shape
    heads = [slice(low, low + HD) for low in range(0, cols, HD)]
    queries = [
        norm_rope(
            mine[:, at] + other[:, at].astype(jnp.float32), gain[...], cosine[...], sine[...],
            lambda n: pltpu.roll(n, HD // 2, 1),
        )
        for at in heads
    ]
    for first in range(0, rows, block):
        here, upto = slice(first, first + block), first + block
        col = lax.broadcasted_iota(jnp.int32, (block, upto), 1)
        row = lax.broadcasted_iota(jnp.int32, (block, upto), 0) + first
        allowed = (col >= starts[here, :]) & (col <= row)
        scores = [
            lax.dot_general(
                q[here], keys[:upto, :], (((1,), (1,)), ((), ())),
                preferred_element_type=jnp.float32,
            )
            for q in queries
        ]
        weights = [
            jnp.where(allowed, jnp.exp2(s * (HD**-0.5 * math.log2(math.e))), 0.0) for s in scores
        ]
        probs = [
            (w * (1.0 / jnp.sum(w, axis=-1, keepdims=True))).astype(jnp.bfloat16) for w in weights
        ]
        for at, p in zip(heads, probs, strict=True):
            mixed = jnp.dot(p, values[:upto, :], preferred_element_type=jnp.float32)
            out[here, at] = mixed.astype(out.dtype)


def attend(mine, other, keys, values, cosine, sine, starts, gain):
    rows, cols = mine.shape
    block = 128 if rows % 128 == 0 else rows
    heads = cols // HD
    step = max(n for n in range(1, 5) if heads % n == 0) * HD
    by_heads = pl.BlockSpec((rows, step), lambda h: (0, h))
    whole = lambda a: pl.BlockSpec(a.shape, lambda h: (0, 0))
    return pl.pallas_call(
        functools.partial(attend_kernel, block),
        grid=(cols // step,),
        out_shape=jax.ShapeDtypeStruct((rows, cols), jnp.bfloat16),
        in_specs=[by_heads, by_heads]
        + [whole(a) for a in (keys, values, cosine, sine, starts, gain)],
        out_specs=by_heads,
        compiler_params=pltpu.CompilerParams(vmem_limit_bytes=24 << 20),
        cost_estimate=pl.CostEstimate(flops=0, bytes_accessed=0, transcendentals=0),
        name="attend",
    )(mine, other, keys, values, cosine, sine, starts, gain)


def product_kernel(depth, windows, count, flag, tokens, *refs):
    out, arrays = refs[-1], refs[:-1]
    cols = out.shape[1]

    def add_up(which):
        total = jnp.zeros(out.shape, jnp.float32)
        for i, (at, low) in enumerate(which):
            total += jnp.dot(
                tokens[:, i * depth : (i + 1) * depth], arrays[at][:, low : low + cols],
                preferred_element_type=jnp.float32,
            )
        out[...] = total.astype(out.dtype)

    if len(windows) == count:
        add_up(windows)
    else:
        pl.when(flag[0] == 1)(lambda: add_up(windows[:count]))
        pl.when(flag[0] == 0)(lambda: add_up(windows[count:]))


def product(is_hub, tokens, cols, at_hub, at_leaf, dtype):
    rows, depth = tokens.shape[0], at_hub[0][0].shape[0]
    arrays, windows = [], []
    for array, low in [*at_hub, *(at_leaf or [])]:
        known = [i for i, a in enumerate(arrays) if a is array]
        if not known:
            arrays.append(array)
        windows.append((known[0] if known else len(arrays) - 1, low))
    block = 256 if rows % 256 == 0 else rows
    return pl.pallas_call(
        functools.partial(product_kernel, depth, tuple(windows), len(at_hub)),
        grid=(rows // block,),
        out_shape=jax.ShapeDtypeStruct((rows, cols), dtype),
        in_specs=[pl.BlockSpec(memory_space=pltpu.SMEM), pl.BlockSpec((block, tokens.shape[1]), lambda r: (r, 0))]
        + [pl.BlockSpec(p.shape, lambda r: (0, 0), pipeline_mode=pl.Buffered(1)) for p in arrays],
        out_specs=pl.BlockSpec((block, cols), lambda r: (r, 0)),
        compiler_params=pltpu.CompilerParams(vmem_limit_bytes=24 << 20),
        cost_estimate=pl.CostEstimate(flops=0, bytes_accessed=0, transcendentals=0),
        name="product",
    )(is_hub.astype(jnp.int32)[None], tokens, *arrays)


def kv_columns(kv_weight, head, n_head):
    if n_head == KVH:
        halves = kv_weight[:, :HD], kv_weight[:, HD:]
        has_keys = head < n_head // 2
        first = lax.ppermute(
            jnp.where(has_keys, *halves), "head",
            [(a, 2 * a) if 2 * a < n_head else (a, 2 * a - n_head + 1) for a in range(n_head)],
        )
        second = lax.ppermute(
            jnp.where(has_keys, *halves[::-1]), "head",
            [(a, 2 * a + 1) if 2 * a < n_head else (a, 2 * a - n_head) for a in range(n_head)],
        )
        even = head % 2 == 0
        return [jnp.where(even, first, second), jnp.where(even, second, first)]
    kv_all = lax.all_gather(kv_weight, "head", axis=1, tiled=True)
    kv_head = head * KVH // n_head
    return [
        lax.dynamic_slice_in_dim(kv_all, (part * KVH + kv_head) * HD, HD, 1) for part in range(2)
    ]


def after(value, *others):
    return lax.optimization_barrier((value, *others))[0]


def split_shares(heads, shares):
    total, bounds, sofar = sum(shares), [], 0
    for share in shares:
        bounds.append((sofar * heads // total * HD, (sofar + share) * heads // total * HD))
        sofar += share
    return bounds


def shards(tokens, q_weight, kv_weight, q_gain, k_gain, doc_lengths):
    rows, depth = tokens.shape[0], q_weight.shape[0]
    heads = q_weight.shape[1] // HD
    n_dp, n_head = lax.axis_size("dp"), lax.axis_size("head")
    n_line = n_dp // 2
    n_pairs = n_line // 2
    rank, head = lax.axis_index("dp"), lax.axis_index("head")
    spot, side = rank // 2, rank % 2
    pair = spot // 2

    hub_of = lambda g: 2 * g + 1 if 2 * g < n_pairs else 2 * g
    is_hub = spot % 2 == jnp.where(2 * pair < n_pairs, 1, 0)

    def on_line(moves):
        return [(2 * a + s, 2 * b + s) for a, b in moves for s in range(2)]

    swap = on_line([(a, a ^ 1) for a in range(n_line)])
    outward = on_line([(hub_of(g), hub_of(g) ^ 1) for g in range(n_pairs)])
    across = [(a, a ^ 1) for a in range(n_dp)]
    send = lambda value, moves: lax.ppermute(value, "dp", moves)

    def round_hubs(part):
        return [
            send(part, on_line([(hub_of(g), hub_of((g + s) % n_pairs)) for g in range(n_pairs)]))
            for s in range(1, n_pairs)
        ]

    def to_leaf(parts):
        return [send(part, outward) for part in parts]

    def woven(own, partners, hubs, leaves):
        return [own, partners] + [p for two in zip(hubs, leaves, strict=True) for p in two]

    order = [spot, spot ^ 1]
    for s in range(1, n_pairs):
        source = (pair - s + n_pairs) % n_pairs
        hub = 2 * source + jnp.where(2 * source < n_pairs, 1, 0)
        order += [hub, hub ^ 1]

    def features(block, of_side):
        return jnp.concatenate(
            [lax.dynamic_slice_in_dim(block, (2 * at + of_side) * depth, depth, 1) for at in order],
            axis=1,
        )

    def tables(of_rank):
        lengths = lax.dynamic_index_in_dim(doc_lengths, of_rank, 0, keepdims=False)
        starts = doc_starts(lengths, rows)
        return (*rope_tables(jnp.arange(rows, dtype=jnp.int32) - starts), starts[:, None])

    even = head % 2 == 0
    twins = [(a, a ^ 1) for a in range(n_head)]
    share = rows // 2
    part = lax.dynamic_slice_in_dim(tokens, head % 2 * share, share, 0)
    part = send(features(part, 1 - side), across)
    twin = lax.ppermute(part, "head", twins)
    beside_tokens = jnp.concatenate(
        [jnp.where(even, part, twin), jnp.where(even, twin, part)], axis=0
    )
    own_tokens = features(tokens, side)
    cosine, sine, starts = tables(rank)

    bounds = [b for b in split_shares(heads, RUNS) if b[0] < b[1]]
    count = len(bounds)
    widths = [high - low for low, high in bounds]
    with_kv = 1
    wides = [w + (2 * HD if k == with_kv else 0) for k, w in enumerate(widths)]
    owns = [q_weight[:, : bounds[0][1]]]
    first = send(owns[0], swap)
    kv_cols = kv_columns(after(kv_weight, owns[0]), head, n_head)
    owns.append(q_weight[:, bounds[1][0] : bounds[1][1]])
    late_weight = after(q_weight, first)
    owns += [late_weight[:, low:high] for low, high in bounds[2:]]
    owns[with_kv] = jnp.concatenate([owns[with_kv], *kv_cols], axis=1)
    cut = lambda k, where: where[0][:, where[1] : where[1] + wides[k]]
    joined = lambda blocks: jnp.concatenate(blocks, axis=1) if len(blocks) > 1 else blocks[0]

    got, hub_at, leaf_at = {}, {}, {}

    def go_round(k, *ties):
        blocks, taken = [], []
        if k + 2 < count:
            blocks.append(owns[k + 2])
            taken.append((hub_at, k + 2, 0))
        if 0 <= k + 1 < count:
            taken.append((leaf_at, k + 1, sum(b.shape[1] for b in blocks)))
            blocks.append(cut(k + 1, got[k + 1]))
        if blocks:
            moved = round_hubs(after(joined(blocks), *ties))
            for table, run, low in taken:
                table[run] = [(p, low) for p in moved]

    got[0] = (first, 0)
    go_round(-2)
    second = send(joined([after(owns[1], first, *[p for p, _ in hub_at[0]])] + owns[2:3]), swap)
    got[1], got[2] = (second, 0), (second, wides[1])
    go_round(-1)
    go_round(0)

    exchanged, sums, parts, computed = [first, second], [], [], {}
    keys = None
    for k in range(count):
        blocks = [owns[k + 3]] if k + 3 < count else []
        low = wides[k + 3] if blocks else 0
        blocks += [cut(k, w) for h, l in zip(hub_at[k], leaf_at[k], strict=True) for w in (h, l)]
        ties = [exchanged[-2]] + computed.get(k - 3, [])
        passed = send(after(joined(blocks), *ties), swap)
        exchanged.append(passed)
        if k + 3 < count:
            got[k + 3] = (passed, 0)
        if k + 1 < count:
            go_round(k + 1, exchanged[-2])
        wide = wides[k]
        at_leaf = [own_at for own_at in [(owns[k], 0), got[k]]]
        at_leaf += [(passed, low + i * wide) for i in range(2 * (n_pairs - 1))]
        pieces = woven((owns[k], 0), got[k], hub_at[k], leaf_at[k]), at_leaf
        theirs = product(
            is_hub, after(beside_tokens, *computed.get(k - 1, [])), wide, *pieces, jnp.float32 if k == with_kv else jnp.bfloat16
        )
        if k == with_kv:
            other_kv = send(theirs[:, widths[k] :], across)
            theirs = theirs[:, : widths[k]].astype(jnp.bfloat16)
        other = send(theirs, across)
        mine = product(is_hub, own_tokens, wide, *pieces, jnp.float32)
        if k == with_kv:
            kv = mine[:, widths[k] :] + other_kv
            mine = mine[:, : widths[k]]
            keys = norm_rope(
                kv[:, :HD], k_gain, cosine, sine,
                lambda n: jnp.concatenate([n[:, HD // 2 :], n[:, : HD // 2]], axis=1),
            )
            values = kv[:, HD:].astype(jnp.bfloat16)
        sums.append((mine, other))
        computed[k] = [mine]
        if keys is not None:
            late = 1
            while len(parts) < len(sums) - late:
                parts.append(
                    attend(*sums[len(parts)], keys, values, cosine, sine, starts, q_gain[None, :])
                )
                computed[k].append(parts[-1])
    parts.append(attend(*sums[-1], keys, values, cosine, sine, starts, q_gain[None, :]))
    return jnp.concatenate(parts, axis=1)


def solution(mesh):
    placed = (P("dp", None), P("dp", "head"), P("dp", "head"), P(), P(), P())
    return jax.shard_map(
        shards, mesh=mesh, in_specs=placed, out_specs=P("dp", "head"), check_vma=False
    )
```

time: 235 us -> 199 us (0.85)
  matrix products: 43.6 us -> 0 us
  waiting for transfers between devices: 95.7 us -> 73.4 us
  starting transfers between devices: 40.6 us -> 55.2 us
  between operations: 14.3 us -> 0.89 us
  Pallas kernels: 24.1 us -> 34.5 us
  local copies, waits for them, and re-layouts: 9.25 us -> 19.5 us
  other arithmetic: 6.56 us -> 14.4 us
    dot_general x32 -> x0, matrix products: 43.6 us -> none  [the longest x16 26.8 us: half_sums(): jnp.dot(t, w, preferred_element_type=jnp.float32)]
    ppermute x26 -> x23, waiting for transfers between devices: 95.6 us -> 72.5 us  [shards(): send = lambda value, moves: lax.ppermute(value, 'dp', moves)]
    pallas_call x4 -> x18, Pallas kernels: 24.1 us -> 34.5 us  [the longest x12 21.8 us: product(): pl.pallas_call(functools.partial(product_kernel, depth, tuple(windows), l...]
    ppermute x26 -> x23, starting transfers between devices: 40.6 us -> 50.2 us  [shards(): send = lambda value, moves: lax.ppermute(value, 'dp', moves)]
    slice x4 -> x22, local copies, waits for them, and re-layouts: 3.1 us -> 9.67 us  [the longest x3 4.13 us: shards(): owns += [late_weight[:, low:high] for low, high in bounds[2:]]]
    ppermute x0 -> x3, starting transfers between devices: none -> 5.02 us  [the longest x1 4.34 us: kv_columns(): lax.ppermute(jnp.where(has_keys, *halves[::-1]), 'head', [(a, 2 * a + 1)...]
    concatenate x3 -> x16, other arithmetic: 3.72 us -> 8.67 us  [the longest x12 5.47 us: shards(): jnp.concatenate(blocks, axis=1)]
    select_n x0 -> x3, other arithmetic: none -> 2.84 us  [the longest x1 1.68 us: shards(): jnp.where(even, part, twin)]
  transfers between devices with their start and end apart: 28 -> 26, of which waited for: 12 -> 8; matrix products, arithmetic and copies ran while one was open for 22% -> 13% of each run, Pallas kernels for 8% -> 16%
where the time goes in v2:
time: 199 us; the launch traced here: 198 us
  waiting for transfers between devices  73.4 us (37%)
  starting transfers between devices  55.2 us (28%)
  Pallas kernels  34.5 us (17%)
  local copies, waits for them, and re-layouts  19.5 us (10%)
  other arithmetic  14.4 us (7%)
    ppermute x23, waiting for transfers between devices, shards(): send = lambda value, moves: lax.ppermute(value, 'dp', moves)  72.5 us
    ppermute x23, starting transfers between devices, shards(): send = lambda value, moves: lax.ppermute(value, 'dp', moves)  50.2 us
    pallas_call x12, Pallas kernels, product(): pl.pallas_call(functools.partial(product_kernel, depth, tuple(windows), l...  21.8 us
    pallas_call x6, Pallas kernels, attend(): pl.pallas_call(functools.partial(attend_kernel, block), grid=(cols // ste...  12.8 us
    concatenate x12, other arithmetic, shards(): jnp.concatenate(blocks, axis=1)  5.47 us
    ppermute x1, starting transfers between devices, kv_columns(): lax.ppermute(jnp.where(has_keys, *halves[::-1]), 'head', [(a, 2 * a + 1)...  4.34 us
    slice x3, local copies, waits for them, and re-layouts, shards(): owns += [late_weight[:, low:high] for low, high in bounds[2:]]  4.13 us
    unnamed x63, local copies, waits for them, and re-layouts  4.02 us
  transfers between devices with their start and end apart: 26, of which 8 were waited for; matrix products, arithmetic and copies ran while one was open for 13% of the time, Pallas kernels for 16%

profile of v2, /device:TPU:0, one launch (start us, length us, event | category | flops | bytes accessed | tf_op | source)
XLA Modules:
  0.0 197.9 jit_solution(14900545075332114962)
XLA Ops:
  2.9 4.3 %collective-permute-start.3 = (bf16[512,128]{1,0:T(8,128)(2,1)S(1)}, bf16[512,128]{1,0:T(8,128)(2,1)S(1)}, u32[]{:S(2)}, u32[]{:S(2)}) collective-permute-start(bf16[512,128]{1,0:T(8,128)(2,1)S(1)} %get-tuple-element.69), channel_id=1, source_target_pairs={{0,1},{1,3},{2,0},{3,2},{4,5},{5,7},{6,4},{7,6},{8,9},{9,11},{10,8... | collective-permute-start | bytes 393224 | tf_op jit(solution)/shard_map/ppermute | solution.py:150
  11.5 6.8 %collective-permute-done.refs_1_ = bf16[512,384]{1,0:T(8,128)(2,1)S(1)} collective-permute-done((bf16[512,384]{1,0:T(8,128)(2,1)S(1)}, bf16[512,384]{1,0:T(8,128)(2,1)S(1)}, u32[]{:S(2)}, u32[]{:S(2)}) %collective-permute-start) | collective-permute-done | bytes 393248 | tf_op jit(solution)/shard_map/ppermute | solution.py:194
  20.9 3.2 %collective-permute-start.9 = (bf16[512,1024]{1,0:T(8,128)(2,1)}, bf16[512,1024]{1,0:T(8,128)(2,1)S(1)}, u32[]{:S(2)}, u32[]{:S(2)}) collective-permute-start(bf16[512,1024]{1,0:T(8,128)(2,1)} %pad_maximum_fusion.6), channel_id=1, source_target_pairs={{0,8},{4,12},{8,0},{12,4},{16,24},{20,28},{24,16},{28,20},{1,9},{5... | collective-permute-start | bytes 3145736 | tf_op jit(solution)/shard_map/ppermute | solution.py:194
  24.1 2.0 fusion.5
  30.5 16.3 %collective-permute-done.9.refs_1_ = bf16[512,1024]{1,0:T(8,128)(2,1)S(1)} collective-permute-done((bf16[512,1024]{1,0:T(8,128)(2,1)}, bf16[512,1024]{1,0:T(8,128)(2,1)S(1)}, u32[]{:S(2)}, u32[]{:S(2)}) %collective-permute-start.9) | collective-permute-done | bytes 1048608 | tf_op jit(solution)/shard_map/ppermute | solution.py:194
  49.7 1.9 fusion.6
  52.9 4.3 %collective-permute-start.5 = (bf16[512,1152]{1,0:T(8,128)(2,1)}, bf16[512,1152]{1,0:T(8,128)(2,1)}, u32[]{:S(2)}, u32[]{:S(2)}) collective-permute-start(bf16[512,1152]{1,0:T(8,128)(2,1)} %pad_maximum_fusion.3), channel_id=1, source_target_pairs={{0,8},{4,12},{8,0},{12,4},{16,24},{20,28},{24,16},{28,20},{1,9},{5... | collective-permute-start | bytes 3538952 | tf_op jit(solution)/shard_map/ppermute | solution.py:194
  61.7 16.9 %collective-permute-start.11 = (bf16[512,1408]{1,0:T(8,128)(2,1)}, bf16[512,1408]{1,0:T(8,128)(2,1)S(1)}, u32[]{:S(2)}, u32[]{:S(2)}) collective-permute-start(bf16[512,1408]{1,0:T(8,128)(2,1)} %pad_maximum_fusion.2), channel_id=1, source_target_pairs={{0,8},{4,12},{8,0},{12,4},{16,24},{20,28},{24,16},{28,20},{1,9},{5... | collective-permute-start | bytes 4325384 | tf_op jit(solution)/shard_map/ppermute | solution.py:194
  90.0 2.7 %product.13 = bf16[512,384]{1,0:T(8,128)(2,1)S(1)} custom-call(s32[1]{0:T(128)} %bitcast.flag, bf16[512,2048]{1,0:T(8,128)(2,1)S(1)} %pad_maximum_fusion.1.tokens, bf16[512,384]{1,0:T(8,128)(2,1)S(1)} %copy-done.19, bf16[512,384]{1,0:T(8,128)(2,1)S(1)} %copy-done.14, bf16[512,384]{1,0:T(8,128)(2,1)S(1)} %copy-done.17, bf16[512,896]{1,0:T(8,128)(2,1)S(1)} %copy-done.1, ...), custom_call_target="tpu_custom_call" | custom-call | tf_op jit(solution)/shard_map/product/pallas_call | solution.py:129
  94.3 2.7 %product.12.mine = f32[512,384]{1,0:T(8,128)S(1)} custom-call(s32[1]{0:T(128)} %bitcast.flag, bf16[512,2048]{1,0:T(8,128)(2,1)S(1)} %pad_maximum_fusion.tokens, bf16[512,384]{1,0:T(8,128)(2,1)S(1)} %copy-done.19, bf16[512,384]{1,0:T(8,128)(2,1)S(1)} %copy-done.14, bf16[512,384]{1,0:T(8,128)(2,1)S(1)} %copy-done.17, bf16[512,896]{1,0:T(8,128)(2,1)S(1)} %copy-done.1, ...), custom_call_target="tpu_custom_call" | custom-call | tf_op jit(solution)/shard_map/product/pallas_call | solution.py:129
  97.0 15.3 %collective-permute-done.11.refs_4_.refs_1_ = bf16[512,1408]{1,0:T(8,128)(2,1)S(1)} collective-permute-done((bf16[512,1408]{1,0:T(8,128)(2,1)}, bf16[512,1408]{1,0:T(8,128)(2,1)S(1)}, u32[]{:S(2)}, u32[]{:S(2)}) %collective-permute-start.11) | collective-permute-done | bytes 1441824 | tf_op jit(solution)/shard_map/ppermute | solution.py:194
  115.5 3.9 %collective-permute-start.15 = (bf16[512,1152]{1,0:T(8,128)(2,1)S(1)}, bf16[512,1152]{1,0:T(8,128)(2,1)S(1)}, u32[]{:S(2)}, u32[]{:S(2)}) collective-permute-start(bf16[512,1152]{1,0:T(8,128)(2,1)S(1)} %pad_maximum_fusion.4), channel_id=1, source_target_pairs={{0,8},{4,12},{8,0},{12,4},{16,24},{20,28},{24,16},{28,20},{1,9},{5... | collective-permute-start | bytes 3538952 | tf_op jit(solution)/shard_map/ppermute | solution.py:194
  119.6 3.7 %collective-permute-start.18 = (bf16[512,768]{1,0:T(8,128)(2,1)S(1)}, bf16[512,768]{1,0:T(8,128)(2,1)S(1)}, u32[]{:S(2)}, u32[]{:S(2)}) collective-permute-start(bf16[512,768]{1,0:T(8,128)(2,1)S(1)} %pad_maximum_fusion.11), channel_id=1, source_target_pairs={{0,8},{4,12},{8,0},{12,4},{16,24},{20,28},{24,16},{28,20},{1,9},{5... | collective-permute-start | bytes 2359304 | tf_op jit(solution)/shard_map/ppermute | solution.py:194
  127.6 2.3 %attend.6 = bf16[512,384]{1,0:T(8,128)(2,1)S(1)} custom-call(f32[512,384]{1,0:T(8,128)S(1)} %product.12.mine, bf16[512,384]{1,0:T(8,128)(2,1)S(1)} %collective-permute-done.8.other, bf16[512,128]{1,0:T(8,128)(2,1)S(1)} %get-tuple-element.41.keys, bf16[512,128]{1,0:T(8,128)(2,1)S(1)} %slice.159.values, f32[512,128]{1,0:T(8,128)S(1)} %get-tuple-element.63.cosine, ...), custom_call_target="tpu_custom_call" | custom-call | tf_op jit(solution)/shard_map/attend/pallas_call | solution.py:87
  130.0 16.3 %collective-permute-done.15.refs_4_.refs_1_ = bf16[512,1152]{1,0:T(8,128)(2,1)S(1)} collective-permute-done((bf16[512,1152]{1,0:T(8,128)(2,1)S(1)}, bf16[512,1152]{1,0:T(8,128)(2,1)S(1)}, u32[]{:S(2)}, u32[]{:S(2)}) %collective-permute-start.15) | collective-permute-done | bytes 1179680 | tf_op jit(solution)/shard_map/ppermute | solution.py:194
  146.3 2.0 %collective-permute-start.21 = (bf16[512,768]{1,0:T(8,128)(2,1)S(1)}, bf16[512,768]{1,0:T(8,128)(2,1)S(1)}, u32[]{:S(2)}, u32[]{:S(2)}) collective-permute-start(bf16[512,768]{1,0:T(8,128)(2,1)S(1)} %pad_maximum_fusion.12), channel_id=1, source_target_pairs={{0,8},{4,12},{8,0},{12,4},{16,24},{20,28},{24,16},{28,20},{1,9},{5... | collective-permute-start | bytes 2359304 | tf_op jit(solution)/shard_map/ppermute | solution.py:194
  154.2 11.9 %collective-permute-done.13.other = bf16[512,256]{1,0:T(8,128)(2,1)S(1)} collective-permute-done((bf16[512,256]{1,0:T(8,128)(2,1)S(1)}, bf16[512,256]{1,0:T(8,128)(2,1)S(1)}, u32[]{:S(2)}, u32[]{:S(2)}) %collective-permute-start.13) | collective-permute-done | bytes 262176 | tf_op jit(solution)/shard_map/ppermute | solution.py:194
  167.7 2.7 %product.19 = bf16[512,384]{1,0:T(8,128)(2,1)S(1)} custom-call(s32[1]{0:T(128)} %bitcast.flag, bf16[512,2048]{1,0:T(8,128)(2,1)S(1)} %pad_maximum_fusion.1.tokens, bf16[512,384]{1,0:T(8,128)(2,1)S(1)} %copy-done.8, bf16[512,1152]{1,0:T(8,128)(2,1)} %collective-permute-done.5.refs_4_.refs_1_, bf16[512,896]{1,0:T(8,128)(2,1)S(1)} %copy-done.3, ...), custom_call_target="tpu_custom_call" | custom-call | tf_op jit(solution)/shard_map/product/pallas_call | solution.py:129
  172.2 2.7 %product.18.mine = f32[512,384]{1,0:T(8,128)S(1)} custom-call(s32[1]{0:T(128)} %bitcast.flag, bf16[512,2048]{1,0:T(8,128)(2,1)S(1)} %pad_maximum_fusion.tokens, bf16[512,384]{1,0:T(8,128)(2,1)S(1)} %copy-done.8, bf16[512,1152]{1,0:T(8,128)(2,1)} %collective-permute-done.5.refs_4_.refs_1_, bf16[512,896]{1,0:T(8,128)(2,1)S(1)} %copy-done.3, ...), custom_call_target="tpu_custom_call" | custom-call | tf_op jit(solution)/shard_map/product/pallas_call | solution.py:129
  174.9 2.9 %attend.8 = bf16[512,512]{1,0:T(8,128)(2,1)S(1)} custom-call(f32[512,512]{1,0:T(8,128)S(1)} %product.16.mine, bf16[512,512]{1,0:T(8,128)(2,1)S(1)} %collective-permute-done.16.other, bf16[512,128]{1,0:T(8,128)(2,1)S(1)} %get-tuple-element.41.keys, bf16[512,128]{1,0:T(8,128)(2,1)S(1)} %slice.159.values, f32[512,128]{1,0:T(8,128)S(1)} %get-tuple-element.63.cosine, ...), custom_call_target="tpu_custom_call" | custom-call | tf_op jit(solution)/shard_map/attend/pallas_call | solution.py:87
  180.0 2.1 %collective-permute-done.19.other = bf16[512,384]{1,0:T(8,128)(2,1)S(1)} collective-permute-done((bf16[512,384]{1,0:T(8,128)(2,1)S(1)}, bf16[512,384]{1,0:T(8,128)(2,1)S(1)}, u32[]{:S(2)}, u32[]{:S(2)}) %collective-permute-start.19) | collective-permute-done | bytes 393248 | tf_op jit(solution)/shard_map/ppermute | solution.py:194
  182.2 2.3 %attend.9 = bf16[512,384]{1,0:T(8,128)(2,1)S(1)} custom-call(f32[512,384]{1,0:T(8,128)S(1)} %product.18.mine, bf16[512,384]{1,0:T(8,128)(2,1)S(1)} %collective-permute-done.19.other, bf16[512,128]{1,0:T(8,128)(2,1)S(1)} %get-tuple-element.41.keys, bf16[512,128]{1,0:T(8,128)(2,1)S(1)} %slice.159.values, f32[512,128]{1,0:T(8,128)S(1)} %get-tuple-element.63.cosine, ...), custom_call_target="tpu_custom_call" | custom-call | tf_op jit(solution)/shard_map/attend/pallas_call | solution.py:87
  188.5 3.6 %collective-permute-done.25.other = bf16[512,128]{1,0:T(8,128)(2,1)S(1)} collective-permute-done((bf16[512,128]{1,0:T(8,128)(2,1)S(1)}, bf16[512,128]{1,0:T(8,128)(2,1)S(1)}, u32[]{:S(2)}, u32[]{:S(2)}) %collective-permute-start.25) | collective-permute-done | bytes 131104 | tf_op jit(solution)/shard_map/ppermute | solution.py:194
  193.5 2.3 %attend.10 = bf16[512,384]{1,0:T(8,128)(2,1)S(1)} custom-call(f32[512,384]{1,0:T(8,128)S(1)} %product.20.mine, bf16[512,384]{1,0:T(8,128)(2,1)S(1)} %collective-permute-done.22.other, bf16[512,128]{1,0:T(8,128)(2,1)S(1)} %get-tuple-element.41.keys, bf16[512,128]{1,0:T(8,128)(2,1)S(1)} %slice.159.values, f32[512,128]{1,0:T(8,128)S(1)} %get-tuple-element.63.cosine, ...), custom_call_target="tpu_custom_call" | custom-call | tf_op jit(solution)/shard_map/attend/pallas_call | solution.py:87
  (169 shorter events, 61.5 us)
Async XLA Ops:
  2.2 8.3 %collective-permute-start.2 = (bf16[512,128]{1,0:T(8,128)(2,1)S(1)}, bf16[512,128]{1,0:T(8,128)(2,1)S(1)}, u32[]{:S(2)}, u32[]{:S(2)}) collective-permute-start(bf16[512,128]{1,0:T(8,128)(2,1)S(1)} %get-tuple-element.68), channel_id=1, source_target_pairs={{0,0},{1,2},{2,1},{3,3},{4,4},{5,6},{6,5},{7,7},{8,8},{9,10},{10,9... | collective-permute-start | bytes 393224 | tf_op jit(solution)/shard_map/ppermute | solution.py:146
  2.9 8.5 %collective-permute-start.3 = (bf16[512,128]{1,0:T(8,128)(2,1)S(1)}, bf16[512,128]{1,0:T(8,128)(2,1)S(1)}, u32[]{:S(2)}, u32[]{:S(2)}) collective-permute-start(bf16[512,128]{1,0:T(8,128)(2,1)S(1)} %get-tuple-element.69), channel_id=1, source_target_pairs={{0,1},{1,3},{2,0},{3,2},{4,5},{5,7},{6,4},{7,6},{8,9},{9,11},{10,8... | collective-permute-start | bytes 393224 | tf_op jit(solution)/shard_map/ppermute | solution.py:150
  7.2 11.1 %collective-permute-start = (bf16[512,384]{1,0:T(8,128)(2,1)S(1)}, bf16[512,384]{1,0:T(8,128)(2,1)S(1)}, u32[]{:S(2)}, u32[]{:S(2)}) collective-permute-start(bf16[512,384]{1,0:T(8,128)(2,1)S(1)} %slice.95.refs_0_), channel_id=1, source_target_pairs={{0,8},{4,12},{8,0},{12,4},{16,24},{20,28},{24,16},{28,20},{1,9},{5... | collective-permute-start | bytes 1179656 | tf_op jit(solution)/shard_map/ppermute | solution.py:194
  8.8 10.8 %collective-permute-start.1 = (bf16[512,384]{1,0:T(8,128)(2,1)S(1)}, bf16[512,384]{1,0:T(8,128)(2,1)S(1)}, u32[]{:S(2)}, u32[]{:S(2)}) collective-permute-start(bf16[512,384]{1,0:T(8,128)(2,1)S(1)} %slice.95.refs_0_), channel_id=1, source_target_pairs={{8,16},{12,20},{16,8},{20,12},{9,17},{13,21},{17,9},{21,13},{10,18... | collective-permute-start | bytes 1179656 | tf_op jit(solution)/shard_map/ppermute | solution.py:194
  20.9 26.0 %collective-permute-start.9 = (bf16[512,1024]{1,0:T(8,128)(2,1)}, bf16[512,1024]{1,0:T(8,128)(2,1)S(1)}, u32[]{:S(2)}, u32[]{:S(2)}) collective-permute-start(bf16[512,1024]{1,0:T(8,128)(2,1)} %pad_maximum_fusion.6), channel_id=1, source_target_pairs={{0,8},{4,12},{8,0},{12,4},{16,24},{20,28},{24,16},{28,20},{1,9},{5... | collective-permute-start | bytes 3145736 | tf_op jit(solution)/shard_map/ppermute | solution.py:194
  27.2 32.0 %collective-permute-start.6 = (bf16[256,2048]{1,0:T(8,128)(2,1)}, bf16[256,2048]{1,0:T(8,128)(2,1)}, u32[]{:S(2)}, u32[]{:S(2)}) collective-permute-start(bf16[256,2048]{1,0:T(8,128)(2,1)} %pad_maximum_fusion.5), channel_id=1, source_target_pairs={{0,4},{4,0},{8,12},{12,8},{16,20},{20,16},{24,28},{28,24},{1,5},{5... | collective-permute-start | bytes 3145736 | tf_op jit(solution)/shard_map/ppermute | solution.py:194
  29.8 21.8 %collective-permute-start.4 = (bf16[512,896]{1,0:T(8,128)(2,1)S(1)}, bf16[512,896]{1,0:T(8,128)(2,1)S(1)}, u32[]{:S(2)}, u32[]{:S(2)}) collective-permute-start(bf16[512,896]{1,0:T(8,128)(2,1)S(1)} %pad_maximum_fusion.8), channel_id=1, source_target_pairs={{8,16},{12,20},{16,8},{20,12},{9,17},{13,21},{17,9},{21,13},{10,18... | collective-permute-start | bytes 2752520 | tf_op jit(solution)/shard_map/ppermute | solution.py:194
  48.9 10.3 %collective-permute-start.10 = (bf16[512,1024]{1,0:T(8,128)(2,1)}, bf16[512,1024]{1,0:T(8,128)(2,1)S(1)}, u32[]{:S(2)}, u32[]{:S(2)}) collective-permute-start(bf16[512,1024]{1,0:T(8,128)(2,1)} %pad_maximum_fusion.7), channel_id=1, source_target_pairs={{8,16},{12,20},{16,8},{20,12},{9,17},{13,21},{17,9},{21,13},{10,18... | collective-permute-start | bytes 3145736 | tf_op jit(solution)/shard_map/ppermute | solution.py:194
  52.9 31.6 %collective-permute-start.5 = (bf16[512,1152]{1,0:T(8,128)(2,1)}, bf16[512,1152]{1,0:T(8,128)(2,1)}, u32[]{:S(2)}, u32[]{:S(2)}) collective-permute-start(bf16[512,1152]{1,0:T(8,128)(2,1)} %pad_maximum_fusion.3), channel_id=1, source_target_pairs={{0,8},{4,12},{8,0},{12,4},{16,24},{20,28},{24,16},{28,20},{1,9},{5... | collective-permute-start | bytes 3538952 | tf_op jit(solution)/shard_map/ppermute | solution.py:194
  59.1 27.3 %collective-permute-start.7 = (bf16[256,2048]{1,0:T(8,128)(2,1)}, bf16[256,2048]{1,0:T(8,128)(2,1)}, u32[]{:S(2)}, u32[]{:S(2)}) collective-permute-start(bf16[256,2048]{1,0:T(8,128)(2,1)} %collective-permute-done.6), channel_id=1, source_target_pairs={{0,1},{1,0},{2,3},{3,2},{4,5},{5,4},{6,7},{7,6},{8,9},{9,8},{10,11... | collective-permute-start | bytes 3145736 | tf_op jit(solution)/shard_map/ppermute | solution.py:230
  61.7 50.6 %collective-permute-start.11 = (bf16[512,1408]{1,0:T(8,128)(2,1)}, bf16[512,1408]{1,0:T(8,128)(2,1)S(1)}, u32[]{:S(2)}, u32[]{:S(2)}) collective-permute-start(bf16[512,1408]{1,0:T(8,128)(2,1)} %pad_maximum_fusion.2), channel_id=1, source_target_pairs={{0,8},{4,12},{8,0},{12,4},{16,24},{20,28},{24,16},{28,20},{1,9},{5... | collective-permute-start | bytes 4325384 | tf_op jit(solution)/shard_map/ppermute | solution.py:194
  85.7 33.7 %collective-permute-start.17 = (bf16[512,768]{1,0:T(8,128)(2,1)S(1)}, bf16[512,768]{1,0:T(8,128)(2,1)S(1)}, u32[]{:S(2)}, u32[]{:S(2)}) collective-permute-start(bf16[512,768]{1,0:T(8,128)(2,1)S(1)} %pad_maximum_fusion.10), channel_id=1, source_target_pairs={{8,16},{12,20},{16,8},{20,12},{9,17},{13,21},{17,9},{21,13},{10,18... | collective-permute-start | bytes 2359304 | tf_op jit(solution)/shard_map/ppermute | solution.py:194
  92.7 34.7 %collective-permute-start.8 = (bf16[512,384]{1,0:T(8,128)(2,1)S(1)}, bf16[512,384]{1,0:T(8,128)(2,1)S(1)}, u32[]{:S(2)}, u32[]{:S(2)}) collective-permute-start(bf16[512,384]{1,0:T(8,128)(2,1)S(1)} %product.13), channel_id=1, source_target_pairs={{0,4},{4,0},{8,12},{12,8},{16,20},{20,16},{24,28},{28,24},{1,5},{5... | collective-permute-start | bytes 1179656 | tf_op jit(solution)/shard_map/ppermute | solution.py:194
  113.8 12.0 %collective-permute-start.12 = (f32[512,256]{1,0:T(8,128)S(1)}, f32[512,256]{1,0:T(8,128)S(1)}, u32[]{:S(2)}, u32[]{:S(2)}) collective-permute-start(f32[512,256]{1,0:T(8,128)S(1)} %slice.131), channel_id=1, source_target_pairs={{0,4},{4,0},{8,12},{12,8},{16,20},{20,16},{24,28},{28,24},{1,5},{5... | collective-permute-start | bytes 1572872 | tf_op jit(solution)/shard_map/ppermute | solution.py:194
  115.5 30.8 %collective-permute-start.15 = (bf16[512,1152]{1,0:T(8,128)(2,1)S(1)}, bf16[512,1152]{1,0:T(8,128)(2,1)S(1)}, u32[]{:S(2)}, u32[]{:S(2)}) collective-permute-start(bf16[512,1152]{1,0:T(8,128)(2,1)S(1)} %pad_maximum_fusion.4), channel_id=1, source_target_pairs={{0,8},{4,12},{8,0},{12,4},{16,24},{20,28},{24,16},{28,20},{1,9},{5... | collective-permute-start | bytes 3538952 | tf_op jit(solution)/shard_map/ppermute | solution.py:194
  119.6 48.1 %collective-permute-start.18 = (bf16[512,768]{1,0:T(8,128)(2,1)S(1)}, bf16[512,768]{1,0:T(8,128)(2,1)S(1)}, u32[]{:S(2)}, u32[]{:S(2)}) collective-permute-start(bf16[512,768]{1,0:T(8,128)(2,1)S(1)} %pad_maximum_fusion.11), channel_id=1, source_target_pairs={{0,8},{4,12},{8,0},{12,4},{16,24},{20,28},{24,16},{28,20},{1,9},{5... | collective-permute-start | bytes 2359304 | tf_op jit(solution)/shard_map/ppermute | solution.py:194
  146.3 31.5 %collective-permute-start.21 = (bf16[512,768]{1,0:T(8,128)(2,1)S(1)}, bf16[512,768]{1,0:T(8,128)(2,1)S(1)}, u32[]{:S(2)}, u32[]{:S(2)}) collective-permute-start(bf16[512,768]{1,0:T(8,128)(2,1)S(1)} %pad_maximum_fusion.12), channel_id=1, source_target_pairs={{0,8},{4,12},{8,0},{12,4},{16,24},{20,28},{24,16},{28,20},{1,9},{5... | collective-permute-start | bytes 2359304 | tf_op jit(solution)/shard_map/ppermute | solution.py:194
  149.8 25.1 %collective-permute-start.16 = (bf16[512,512]{1,0:T(8,128)(2,1)S(1)}, bf16[512,512]{1,0:T(8,128)(2,1)S(1)}, u32[]{:S(2)}, u32[]{:S(2)}) collective-permute-start(bf16[512,512]{1,0:T(8,128)(2,1)S(1)} %product.17), channel_id=1, source_target_pairs={{0,4},{4,0},{8,12},{12,8},{16,20},{20,16},{24,28},{28,24},{1,5},{5... | collective-permute-start | bytes 1572872 | tf_op jit(solution)/shard_map/ppermute | solution.py:194
  151.4 14.7 %collective-permute-start.13 = (bf16[512,256]{1,0:T(8,128)(2,1)S(1)}, bf16[512,256]{1,0:T(8,128)(2,1)S(1)}, u32[]{:S(2)}, u32[]{:S(2)}) collective-permute-start(bf16[512,256]{1,0:T(8,128)(2,1)S(1)} %slice.158), channel_id=1, source_target_pairs={{0,4},{4,0},{8,12},{12,8},{16,20},{20,16},{24,28},{28,24},{1,5},{5... | collective-permute-start | bytes 786440 | tf_op jit(solution)/shard_map/ppermute | solution.py:194
  152.0 20.0 %collective-permute-start.23 = (bf16[512,128]{1,0:T(8,128)(2,1)S(1)}, bf16[512,128]{1,0:T(8,128)(2,1)S(1)}, u32[]{:S(2)}, u32[]{:S(2)}) collective-permute-start(bf16[512,128]{1,0:T(8,128)(2,1)S(1)} %slice.147), channel_id=1, source_target_pairs={{8,16},{12,20},{16,8},{20,12},{9,17},{13,21},{17,9},{21,13},{10,18... | collective-permute-start | bytes 393224 | tf_op jit(solution)/shard_map/ppermute | solution.py:194
  170.5 11.7 %collective-permute-start.19 = (bf16[512,384]{1,0:T(8,128)(2,1)S(1)}, bf16[512,384]{1,0:T(8,128)(2,1)S(1)}, u32[]{:S(2)}, u32[]{:S(2)}) collective-permute-start(bf16[512,384]{1,0:T(8,128)(2,1)S(1)} %product.19), channel_id=1, source_target_pairs={{0,4},{4,0},{8,12},{12,8},{16,20},{20,16},{24,28},{28,24},{1,5},{5... | collective-permute-start | bytes 1179656 | tf_op jit(solution)/shard_map/ppermute | solution.py:194
  172.1 13.9 %collective-permute-start.24 = (bf16[512,256]{1,0:T(8,128)(2,1)S(1)}, bf16[512,256]{1,0:T(8,128)(2,1)S(1)}, u32[]{:S(2)}, u32[]{:S(2)}) collective-permute-start(bf16[512,256]{1,0:T(8,128)(2,1)S(1)} %pad_maximum_fusion.17), channel_id=1, source_target_pairs={{0,8},{4,12},{8,0},{12,4},{16,24},{20,28},{24,16},{28,20},{1,9},{5... | collective-permute-start | bytes 786440 | tf_op jit(solution)/shard_map/ppermute | solution.py:194
  179.4 14.2 %collective-permute-start.22 = (bf16[512,384]{1,0:T(8,128)(2,1)S(1)}, bf16[512,384]{1,0:T(8,128)(2,1)S(1)}, u32[]{:S(2)}, u32[]{:S(2)}) collective-permute-start(bf16[512,384]{1,0:T(8,128)(2,1)S(1)} %product.21), channel_id=1, source_target_pairs={{0,4},{4,0},{8,12},{12,8},{16,20},{20,16},{24,28},{28,24},{1,5},{5... | collective-permute-start | bytes 1179656 | tf_op jit(solution)/shard_map/ppermute | solution.py:194
  187.1 5.0 %collective-permute-start.25 = (bf16[512,128]{1,0:T(8,128)(2,1)S(1)}, bf16[512,128]{1,0:T(8,128)(2,1)S(1)}, u32[]{:S(2)}, u32[]{:S(2)}) collective-permute-start(bf16[512,128]{1,0:T(8,128)(2,1)S(1)} %product.23), channel_id=1, source_target_pairs={{0,4},{4,0},{8,12},{12,8},{16,20},{20,16},{24,28},{28,24},{1,5},{5... | collective-permute-start | bytes 393224 | tf_op jit(solution)/shard_map/ppermute | solution.py:194
  (34 other events, 251.5 us)

commit v3 on v2

--- a/solution.py
+++ b/solution.py
@@ -15,7 +15,7 @@
 theta_base = 1000000.0
 norm_eps = 1e-06
 
-RUNS = (3, 2, 4, 3, 3, 1)
+RUNS = (4, 3, 4, 4, 1)
 
 
 def doc_starts(lengths, count):
@@ -25,17 +25,15 @@
     return jnp.sum(passed * lengths[None, :], axis=1)
 
 
-def rope_tables(positions):
+def rope_tables(positions, starts):
     half_width = HD // 2
     frequency = jnp.exp(
         jnp.arange(half_width, dtype=jnp.float32) * (-2.0 * math.log(theta_base) / HD)
     )
     angles = positions.astype(jnp.float32)[:, None] * frequency[None, :]
     cosine, sine = jnp.cos(angles), jnp.sin(angles)
-    return (
-        jnp.concatenate([cosine, cosine], axis=1),
-        jnp.concatenate([-sine, sine], axis=1),
-    )
+    wide_starts = jnp.broadcast_to(starts.astype(jnp.float32)[:, None], (starts.shape[0], HD))
+    return jnp.concatenate([cosine, cosine, -sine, sine, wide_starts], axis=1)
 
 
 def norm_rope(raw, gain, cosine, sine, swap_halves):
@@ -44,13 +42,14 @@
     return (normed * cosine + swap_halves(normed) * sine).astype(jnp.bfloat16)
 
 
-def attend_kernel(block, mine, other, keys, values, cosine, sine, starts, gain, out):
+def attend_kernel(block, mine, other, keys_values, tables, gain, out):
     rows, cols = mine.shape
     heads = [slice(low, low + HD) for low in range(0, cols, HD)]
+    keys, values = keys_values.at[:, :HD], keys_values.at[:, HD:]
     queries = [
         norm_rope(
-            mine[:, at] + other[:, at].astype(jnp.float32), gain[...], cosine[...], sine[...],
-            lambda n: pltpu.roll(n, HD // 2, 1),
+            mine[:, at] + other[:, at].astype(jnp.float32), gain[...], tables[:, :HD],
+            tables[:, HD : 2 * HD], lambda n: pltpu.roll(n, HD // 2, 1),
         )
         for at in heads
     ]
@@ -58,7 +57,8 @@
         here, upto = slice(first, first + block), first + block
         col = lax.broadcasted_iota(jnp.int32, (block, upto), 1)
         row = lax.broadcasted_iota(jnp.int32, (block, upto), 0) + first
-        allowed = (col >= starts[here, :]) & (col <= row)
+        starts = tables[here, 2 * HD : 2 * HD + 1].astype(jnp.int32)
+        allowed = (col >= starts) & (col <= row)
         scores = [
             lax.dot_general(
                 q[here], keys[:upto, :], (((1,), (1,)), ((), ())),
@@ -77,7 +77,7 @@
             out[here, at] = mixed.astype(out.dtype)
 
 
-def attend(mine, other, keys, values, cosine, sine, starts, gain):
+def attend(mine, other, keys_values, tables, gain):
     rows, cols = mine.shape
     block = 128 if rows % 128 == 0 else rows
     heads = cols // HD
@@ -88,55 +88,79 @@
         functools.partial(attend_kernel, block),
         grid=(cols // step,),
         out_shape=jax.ShapeDtypeStruct((rows, cols), jnp.bfloat16),
-        in_specs=[by_heads, by_heads]
-        + [whole(a) for a in (keys, values, cosine, sine, starts, gain)],
+        in_specs=[by_heads, by_heads] + [whole(a) for a in (keys_values, tables, gain)],
         out_specs=by_heads,
         compiler_params=pltpu.CompilerParams(vmem_limit_bytes=24 << 20),
         cost_estimate=pl.CostEstimate(flops=0, bytes_accessed=0, transcendentals=0),
         name="attend",
-    )(mine, other, keys, values, cosine, sine, starts, gain)
-
-
-def product_kernel(depth, windows, count, flag, tokens, *refs):
-    out, arrays = refs[-1], refs[:-1]
-    cols = out.shape[1]
-
-    def add_up(which):
-        total = jnp.zeros(out.shape, jnp.float32)
-        for i, (at, low) in enumerate(which):
-            total += jnp.dot(
-                tokens[:, i * depth : (i + 1) * depth], arrays[at][:, low : low + cols],
-                preferred_element_type=jnp.float32,
-            )
-        out[...] = total.astype(out.dtype)
-
-    if len(windows) == count:
-        add_up(windows)
-    else:
-        pl.when(flag[0] == 1)(lambda: add_up(windows[:count]))
-        pl.when(flag[0] == 0)(lambda: add_up(windows[count:]))
-
-
-def product(is_hub, tokens, cols, at_hub, at_leaf, dtype):
-    rows, depth = tokens.shape[0], at_hub[0][0].shape[0]
+    )(mine, other, keys_values, tables, gain)
+
+
+def product_kernel(windows, count, sides, flag, *refs):
+    tokens, arrays, outs = refs[:sides], refs[sides : -sides - 3], refs[-sides - 3 : -3]
+    features, weights, arrived = refs[-3:]
+    depth, cols = weights.shape[1:]
+    rows = tokens[0].shape[0]
+    block = 256 if rows % 256 == 0 else rows
+
+    def rows_of(which, i):
+        at, low = which[i]
+        return pltpu.make_async_copy(
+            arrays[at].at[:, pl.ds(low, cols)], weights.at[i], arrived.at[sides, i]
+        )
+
+    def features_of(side, i):
+        return pltpu.make_async_copy(
+            tokens[side].at[:, pl.ds(i * depth, depth)], features.at[side, i], arrived.at[side, i]
+        )
+
+    def start_all(which):
+        for i in range(count):
+            rows_of(which, i).start()
+            for side in range(sides):
+                features_of(side, i).start()
+
+    pl.when(flag[0] == 1)(lambda: start_all(windows[:count]))
+    pl.when(flag[0] == 0)(lambda: start_all(windows[count:]))
+    for i in range(count):
+        rows_of(windows, i).wait()
+        for side in range(sides):
+            features_of(side, i).wait()
+    for side in range(sides):
+        for r in range(rows // block):
+            here = pl.ds(r * block, block)
+            total = jnp.zeros((block, cols), jnp.float32)
+            for i in range(count):
+                total += jnp.dot(
+                    features[side, i, here, :], weights[i], preferred_element_type=jnp.float32
+                )
+            outs[side][here, :] = total.astype(outs[side].dtype)
+
+
+def product(is_hub, tokens, cols, at_hub, at_leaf, dtypes):
+    (rows, width), depth, sides = tokens[0].shape, at_hub[0][0].shape[0], len(tokens)
+    count = len(at_hub)
     arrays, windows = [], []
-    for array, low in [*at_hub, *(at_leaf or [])]:
+    for array, low in [*at_hub, *at_leaf]:
         known = [i for i, a in enumerate(arrays) if a is array]
         if not known:
             arrays.append(array)
         windows.append((known[0] if known else len(arrays) - 1, low))
-    block = 256 if rows % 256 == 0 else rows
     return pl.pallas_call(
-        functools.partial(product_kernel, depth, tuple(windows), len(at_hub)),
-        grid=(rows // block,),
-        out_shape=jax.ShapeDtypeStruct((rows, cols), dtype),
-        in_specs=[pl.BlockSpec(memory_space=pltpu.SMEM), pl.BlockSpec((block, tokens.shape[1]), lambda r: (r, 0))]
-        + [pl.BlockSpec(p.shape, lambda r: (0, 0), pipeline_mode=pl.Buffered(1)) for p in arrays],
-        out_specs=pl.BlockSpec((block, cols), lambda r: (r, 0)),
-        compiler_params=pltpu.CompilerParams(vmem_limit_bytes=24 << 20),
+        functools.partial(product_kernel, tuple(windows), count, sides),
+        out_shape=[jax.ShapeDtypeStruct((rows, cols), dtype) for dtype in dtypes],
+        in_specs=[pl.BlockSpec(memory_space=pltpu.SMEM)]
+        + [pl.BlockSpec(memory_space=pl.ANY)] * (sides + len(arrays)),
+        out_specs=[pl.BlockSpec(memory_space=pltpu.VMEM)] * sides,
+        scratch_shapes=[
+            pltpu.VMEM((sides, count, rows, depth), jnp.bfloat16),
+            pltpu.VMEM((count, depth, cols), jnp.bfloat16),
+            pltpu.SemaphoreType.DMA((sides + 1, count)),
+        ],
+        compiler_params=pltpu.CompilerParams(vmem_limit_bytes=20 << 20),
         cost_estimate=pl.CostEstimate(flops=0, bytes_accessed=0, transcendentals=0),
         name="product",
-    )(is_hub.astype(jnp.int32)[None], tokens, *arrays)
+    )(is_hub.astype(jnp.int32)[None], *tokens, *arrays)
 
 
 def kv_columns(kv_weight, head, n_head):
@@ -220,27 +244,28 @@
     def tables(of_rank):
         lengths = lax.dynamic_index_in_dim(doc_lengths, of_rank, 0, keepdims=False)
         starts = doc_starts(lengths, rows)
-        return (*rope_tables(jnp.arange(rows, dtype=jnp.int32) - starts), starts[:, None])
+        return rope_tables(jnp.arange(rows, dtype=jnp.int32) - starts, starts)
 
     even = head % 2 == 0
+    own_first = q_weight[:, : split_shares(heads, RUNS)[0][1]]
+    first = send(own_first, swap)
     twins = [(a, a ^ 1) for a in range(n_head)]
     share = rows // 2
     part = lax.dynamic_slice_in_dim(tokens, head % 2 * share, share, 0)
-    part = send(features(part, 1 - side), across)
+    part = send(features(after(part, first), 1 - side), across)
     twin = lax.ppermute(part, "head", twins)
     beside_tokens = jnp.concatenate(
         [jnp.where(even, part, twin), jnp.where(even, twin, part)], axis=0
     )
     own_tokens = features(tokens, side)
-    cosine, sine, starts = tables(rank)
+    own_tables = tables(rank)
 
     bounds = [b for b in split_shares(heads, RUNS) if b[0] < b[1]]
     count = len(bounds)
     widths = [high - low for low, high in bounds]
     with_kv = 1
     wides = [w + (2 * HD if k == with_kv else 0) for k, w in enumerate(widths)]
-    owns = [q_weight[:, : bounds[0][1]]]
-    first = send(owns[0], swap)
+    owns = [own_first]
     kv_cols = kv_columns(after(kv_weight, owns[0]), head, n_head)
     owns.append(q_weight[:, bounds[1][0] : bounds[1][1]])
     late_weight = after(q_weight, first)
@@ -251,69 +276,70 @@
 
     got, hub_at, leaf_at = {}, {}, {}
 
-    def go_round(k, *ties):
-        blocks, taken = [], []
-        if k + 2 < count:
-            blocks.append(owns[k + 2])
-            taken.append((hub_at, k + 2, 0))
-        if 0 <= k + 1 < count:
-            taken.append((leaf_at, k + 1, sum(b.shape[1] for b in blocks)))
-            blocks.append(cut(k + 1, got[k + 1]))
-        if blocks:
-            moved = round_hubs(after(joined(blocks), *ties))
-            for table, run, low in taken:
-                table[run] = [(p, low) for p in moved]
+    def go_round(own_runs, leaf_run, *ties):
+        runs = [(hub_at, k, (owns[k], 0)) for k in own_runs if k < count]
+        if leaf_run is not None and leaf_run < count:
+            runs.append((leaf_at, leaf_run, got[leaf_run]))
+        if runs:
+            moved = round_hubs(after(joined([cut(k, where) for _, k, where in runs]), *ties))
+            low = 0
+            for table, k, _ in runs:
+                table[k] = [(p, low) for p in moved]
+                low += wides[k]
 
     got[0] = (first, 0)
-    go_round(-2)
-    second = send(joined([after(owns[1], first, *[p for p, _ in hub_at[0]])] + owns[2:3]), swap)
-    got[1], got[2] = (second, 0), (second, wides[1])
-    go_round(-1)
-    go_round(0)
-
-    exchanged, sums, parts, computed = [first, second], [], [], {}
+    go_round([0], None)
+    arrived = lambda table, k: [p for p, _ in table.get(k, [])]
+    second = send(joined([after(owns[1], first, *arrived(hub_at, 0))] + owns[2:4]), swap)
+    for k in range(1, min(4, count)):
+        got[k] = (second, sum(wides[1:k]))
+    go_round([], 0)
+    go_round([1, 2], None, *arrived(leaf_at, 0))
+    go_round([], 1)
+    go_round([3], 2, *arrived(leaf_at, 1))
+
+    exchanged, sums, parts, computed = [first, second], [], [], []
     keys = None
     for k in range(count):
-        blocks = [owns[k + 3]] if k + 3 < count else []
-        low = wides[k + 3] if blocks else 0
+        blocks = [owns[k + 4]] if k + 4 < count else []
+        low = wides[k + 4] if blocks else 0
         blocks += [cut(k, w) for h, l in zip(hub_at[k], leaf_at[k], strict=True) for w in (h, l)]
-        ties = [exchanged[-2]] + computed.get(k - 3, [])
+        ties = exchanged[-1:] + computed[: max(0, k - 1)][-1:]
         passed = send(after(joined(blocks), *ties), swap)
         exchanged.append(passed)
-        if k + 3 < count:
-            got[k + 3] = (passed, 0)
-        if k + 1 < count:
-            go_round(k + 1, exchanged[-2])
+        if k + 4 < count:
+            got[k + 4] = (passed, 0)
+        go_round([k + 4], k + 3, *arrived(leaf_at, k + 2))
         wide = wides[k]
         at_leaf = [own_at for own_at in [(owns[k], 0), got[k]]]
         at_leaf += [(passed, low + i * wide) for i in range(2 * (n_pairs - 1))]
         pieces = woven((owns[k], 0), got[k], hub_at[k], leaf_at[k]), at_leaf
-        theirs = product(
-            is_hub, after(beside_tokens, *computed.get(k - 1, [])), wide, *pieces, jnp.float32 if k == with_kv else jnp.bfloat16
+        done = parts[: max(0, k - 2 + (k + 1 == count))][-2:]
+        theirs, mine = product(
+            is_hub, (after(beside_tokens, *computed[-1:], *done), own_tokens), wide, *pieces,
+            (jnp.float32 if k == with_kv else jnp.bfloat16, jnp.float32),
         )
         if k == with_kv:
             other_kv = send(theirs[:, widths[k] :], across)
             theirs = theirs[:, : widths[k]].astype(jnp.bfloat16)
         other = send(theirs, across)
-        mine = product(is_hub, own_tokens, wide, *pieces, jnp.float32)
         if k == with_kv:
             kv = mine[:, widths[k] :] + other_kv
             mine = mine[:, : widths[k]]
             keys = norm_rope(
-                kv[:, :HD], k_gain, cosine, sine,
+                kv[:, :HD], k_gain, own_tables[:, :HD], own_tables[:, HD : 2 * HD],
                 lambda n: jnp.concatenate([n[:, HD // 2 :], n[:, : HD // 2]], axis=1),
             )
-            values = kv[:, HD:].astype(jnp.bfloat16)
+            keys_values = jnp.concatenate([keys, kv[:, HD:].astype(jnp.bfloat16)], axis=1)
         sums.append((mine, other))
-        computed[k] = [mine]
+        computed.append(mine)
         if keys is not None:
             late = 1
             while len(parts) < len(sums) - late:
                 parts.append(
-                    attend(*sums[len(parts)], keys, values, cosine, sine, starts, q_gain[None, :])
+                    attend(*sums[len(parts)], keys_values, own_tables, q_gain[None, :])
                 )
-                computed[k].append(parts[-1])
-    parts.append(attend(*sums[-1], keys, values, cosine, sine, starts, q_gain[None, :]))
+    parts.append(attend(*sums[-1], keys_values, own_tables, q_gain[None, :]))
     return jnp.concatenate(parts, axis=1)
 
 

time: 199 us -> 188 us (0.945)
  starting transfers between devices: 55.2 us -> 35.5 us
  local copies, waits for them, and re-layouts: 19.5 us -> 26.5 us
  Pallas kernels: 34.5 us -> 31.1 us
  waiting for transfers between devices: 73.4 us -> 76.8 us
  other arithmetic: 14.4 us -> 16.6 us
    ppermute x23 -> x21, starting transfers between devices: 50.2 us -> 31.9 us  [shards(): send = lambda value, moves: lax.ppermute(value, 'dp', moves)]
    pallas_call x12 -> x5, Pallas kernels: 21.8 us -> 18.7 us  [product(): pl.pallas_call(functools.partial(product_kernel, tuple(windows), count, s...]
    concatenate x12 -> x9, other arithmetic: 5.47 us -> 8.46 us  [shards(): jnp.concatenate(blocks, axis=1)]
    unnamed x63 -> x88, local copies, waits for them, and re-layouts: 4.02 us -> 6.37 us
    ppermute x1, waiting for transfers between devices: 0.94 us -> 3.14 us  [kv_columns(): lax.ppermute(jnp.where(has_keys, *halves[::-1]), 'head', [(a, 2 * a + 1)...]
    ppermute x23 -> x21, waiting for transfers between devices: 72.5 us -> 73.7 us  [shards(): send = lambda value, moves: lax.ppermute(value, 'dp', moves)]
    pallas_call x6 -> x5, Pallas kernels: 12.8 us -> 12.4 us  [attend(): pl.pallas_call(functools.partial(attend_kernel, block), grid=(cols // ste...]
  transfers between devices with their start and end apart: 26 -> 24, of which waited for: 8 -> 9; matrix products, arithmetic and copies ran while one was open for 13% -> 17% of each run, Pallas kernels for 16% -> 15%
where the time goes in v3:
time: 188 us; the launch traced here: 187 us
  waiting for transfers between devices  76.8 us (41%)
  starting transfers between devices  35.5 us (19%)
  Pallas kernels  31.1 us (17%)
  local copies, waits for them, and re-layouts  26.5 us (14%)
  other arithmetic  16.6 us (9%)
    ppermute x21, waiting for transfers between devices, shards(): send = lambda value, moves: lax.ppermute(value, 'dp', moves)  73.7 us
    ppermute x21, starting transfers between devices, shards(): send = lambda value, moves: lax.ppermute(value, 'dp', moves)  31.9 us
    pallas_call x5, Pallas kernels, product(): pl.pallas_call(functools.partial(product_kernel, tuple(windows), count, s...  18.7 us
    pallas_call x5, Pallas kernels, attend(): pl.pallas_call(functools.partial(attend_kernel, block), grid=(cols // ste...  12.4 us
    concatenate x9, other arithmetic, shards(): jnp.concatenate(blocks, axis=1)  8.46 us
    unnamed x88, local copies, waits for them, and re-layouts  6.37 us
    slice x10, local copies, waits for them, and re-layouts, shards(): cut = lambda k, where: where[0][:, where[1]:where[1] + wides[k]]  3.94 us
  transfers between devices with their start and end apart: 24, of which 9 were waited for; matrix products, arithmetic and copies ran while one was open for 17% of the time, Pallas kernels for 15%

profile of v3, /device:TPU:0, one launch (start us, length us, event | category | flops | bytes accessed | tf_op | source)
XLA Modules:
  0.0 187.4 jit_solution(10030329662050444926)
XLA Ops:
  1.1 3.1 %collective-permute-start = (bf16[512,512]{1,0:T(8,128)(2,1)S(1)}, bf16[512,512]{1,0:T(8,128)(2,1)S(1)}, u32[]{:S(2)}, u32[]{:S(2)}) collective-permute-start(bf16[512,512]{1,0:T(8,128)(2,1)S(1)} %slice.84.refs_2_), channel_id=1, source_target_pairs={{0,8},{4,12},{8,0},{12,4},{16,24},{20,28},{24,16},{28,20},{1,9},{5... | collective-permute-start | bytes 1572872 | tf_op jit(solution)/shard_map/ppermute | solution.py:218
  6.5 2.9 %collective-permute-start.6 = (bf16[512,128]{1,0:T(8,128)(2,1)S(1)}, bf16[512,128]{1,0:T(8,128)(2,1)S(1)}, u32[]{:S(2)}, u32[]{:S(2)}) collective-permute-start(bf16[512,128]{1,0:T(8,128)(2,1)S(1)} %get-tuple-element.80), channel_id=1, source_target_pairs={{0,1},{1,3},{2,0},{3,2},{4,5},{5,7},{6,4},{7,6},{8,9},{9,11},{10,8... | collective-permute-start | bytes 393224 | tf_op jit(solution)/shard_map/ppermute | solution.py:174
  10.5 3.1 %collective-permute-done.6 = bf16[512,128]{1,0:T(8,128)(2,1)S(1)} collective-permute-done((bf16[512,128]{1,0:T(8,128)(2,1)S(1)}, bf16[512,128]{1,0:T(8,128)(2,1)S(1)}, u32[]{:S(2)}, u32[]{:S(2)}) %collective-permute-start.6) | collective-permute-done | bytes 131104 | tf_op jit(solution)/shard_map/ppermute | solution.py:174
  13.8 2.3 %collective-permute-done.refs_3_ = bf16[512,512]{1,0:T(8,128)(2,1)S(1)} collective-permute-done((bf16[512,512]{1,0:T(8,128)(2,1)S(1)}, bf16[512,512]{1,0:T(8,128)(2,1)S(1)}, u32[]{:S(2)}, u32[]{:S(2)}) %collective-permute-start) | collective-permute-done | bytes 524320 | tf_op jit(solution)/shard_map/ppermute | solution.py:218
  19.2 4.6 %collective-permute-start.7 = (bf16[512,1664]{1,0:T(8,128)(2,1)}, bf16[512,1664]{1,0:T(8,128)(2,1)S(1)}, u32[]{:S(2)}, u32[]{:S(2)}) collective-permute-start(bf16[512,1664]{1,0:T(8,128)(2,1)} %pad_maximum_fusion.2), channel_id=1, source_target_pairs={{0,8},{4,12},{8,0},{12,4},{16,24},{20,28},{24,16},{28,20},{1,9},{5... | collective-permute-start | bytes 5111816 | tf_op jit(solution)/shard_map/ppermute | solution.py:218
  35.4 2.4 %pad_maximum_fusion.4 = bf16[512,1152]{1,0:T(8,128)(2,1)} fusion(bf16[512,512]{1,0:T(8,128)(2,1)} %copy-done.20, bf16[512,512]{1,0:T(8,128)(2,1)} %copy-done.18, bf16[512,128]{1,0:T(8,128)(2,1)S(1)} %slice.85.refs_2_), kind=kLoop, calls=%fused_computation.4 | loop fusion | flops 3538944 | bytes 2359296 | tf_op jit(solution)/shard_map/concatenate | solution.py:275
  37.8 22.6 %collective-permute-done.7.refs_3_ = bf16[512,1664]{1,0:T(8,128)(2,1)S(1)} collective-permute-done((bf16[512,1664]{1,0:T(8,128)(2,1)}, bf16[512,1664]{1,0:T(8,128)(2,1)S(1)}, u32[]{:S(2)}, u32[]{:S(2)}) %collective-permute-start.7) | collective-permute-done | bytes 1703968 | tf_op jit(solution)/shard_map/ppermute | solution.py:218
  60.3 1.7 collective-permute-start.8
  65.1 1.8 copy-done.3
  68.2 18.6 %collective-permute-done.8.refs_6_.refs_3_ = bf16[512,1152]{1,0:T(8,128)(2,1)} collective-permute-done((bf16[512,1152]{1,0:T(8,128)(2,1)}, bf16[512,1152]{1,0:T(8,128)(2,1)}, u32[]{:S(2)}, u32[]{:S(2)}) %collective-permute-start.8) | collective-permute-done | bytes 1179680 | tf_op jit(solution)/shard_map/ppermute | solution.py:218
  93.0 4.0 %product.5 = (bf16[512,512]{1,0:T(8,128)(2,1)S(1)}, f32[512,512]{1,0:T(8,128)S(1)}) custom-call(s32[1]{0:T(128)} %bitcast.flag, bf16[512,2048]{1,0:T(8,128)(2,1)S(1)} %pad_maximum_fusion.refs_0_, bf16[512,2048]{1,0:T(8,128)(2,1)S(1)} %pad_maximum_fusion.1.refs_1_, bf16[512,512]{1,0:T(8,128)(2,1)S(1)} %copy-done.17, bf16[512,512]{1,0:T(8,128)(2,1)S(1)} %copy-done.31, ...), custom_call_target="tpu_custom_call" | custom-call | tf_op jit(solution)/shard_map/product/pallas_call | solution.py:149
  100.7 14.8 %collective-permute-done.12.refs_6_ = bf16[512,1280]{1,0:T(8,128)(2,1)S(1)} collective-permute-done((bf16[512,1280]{1,0:T(8,128)(2,1)S(1)}, bf16[512,1280]{1,0:T(8,128)(2,1)S(1)}, u32[]{:S(2)}, u32[]{:S(2)}) %collective-permute-start.12) | collective-permute-done | bytes 1310752 | tf_op jit(solution)/shard_map/ppermute | solution.py:218
  117.3 4.5 %product.6 = (f32[512,640]{1,0:T(8,128)S(1)}, f32[512,640]{1,0:T(8,128)S(1)}) custom-call(s32[1]{0:T(128)} %bitcast.flag, bf16[512,2048]{1,0:T(8,128)(2,1)S(1)} %pad_maximum_fusion.refs_0_, bf16[512,2048]{1,0:T(8,128)(2,1)S(1)} %pad_maximum_fusion.1.refs_1_, bf16[512,640]{1,0:T(8,128)(2,1)S(1)} %copy-done.11, bf16[512,1664]{1,0:T(8,128)(2,1)S(1)} %copy-done.3, ...), custom_call_target="tpu_custom_call" | custom-call | tf_op jit(solution)/shard_map/product/pallas_call | solution.py:149
  124.2 1.9 %fusion.2 = (f32[512,64]{1,0:T(8,128)}, f32[512,64]{1,0:T(8,128)}, f32[512,64]{1,0:T(8,128)}) fusion(f32[64]{0:T(128)S(1)} %multiply_exponential_fusion, f32[512]{0:T(512)S(1)} %get-tuple-element.87), kind=kLoop, calls=%fused_computation.31 | loop fusion | flops 65536 | bytes 395520 | tf_op jit(solution)/shard_map/neg | solution.py:36
  141.1 4.2 %product.7 = (bf16[512,512]{1,0:T(8,128)(2,1)S(1)}, f32[512,512]{1,0:T(8,128)S(1)}) custom-call(s32[1]{0:T(128)} %bitcast.flag, bf16[512,2048]{1,0:T(8,128)(2,1)S(1)} %copy-done.1, bf16[512,2048]{1,0:T(8,128)(2,1)S(1)} %pad_maximum_fusion.1.refs_1_, bf16[512,512]{1,0:T(8,128)(2,1)S(1)} %copy-done.15, bf16[512,1664]{1,0:T(8,128)(2,1)S(1)} %copy-done.4, ...), custom_call_target="tpu_custom_call" | custom-call | tf_op jit(solution)/shard_map/product/pallas_call | solution.py:149
  149.0 2.9 %attend.5 = bf16[512,512]{1,0:T(8,128)(2,1)S(1)} custom-call(f32[512,512]{1,0:T(8,128)S(1)} %copy-done.28, bf16[512,512]{1,0:T(8,128)(2,1)S(1)} %collective-permute-done.9.other, bf16[512,256]{1,0:T(8,128)(2,1)S(1)} %pad_maximum_fusion.12.keys_values, f32[512,384]{1,0:T(8,128)S(1)} %concatenate.71.tables, f32[1,128]{1,0:T(1,128)S(1)} %bitcast.6), custom_call_target="tpu_custom_call" | custom-call | tf_op jit(solution)/shard_map/attend/pallas_call | solution.py:87
  151.9 8.7 %collective-permute-done.19.refs_6_ = bf16[512,1024]{1,0:T(8,128)(2,1)S(1)} collective-permute-done((bf16[512,1024]{1,0:T(8,128)(2,1)S(1)}, bf16[512,1024]{1,0:T(8,128)(2,1)S(1)}, u32[]{:S(2)}, u32[]{:S(2)}) %collective-permute-start.19) | collective-permute-done | bytes 1048608 | tf_op jit(solution)/shard_map/ppermute | solution.py:218
  160.6 3.3 %product.8 = (bf16[512,512]{1,0:T(8,128)(2,1)S(1)}, f32[512,512]{1,0:T(8,128)S(1)}) custom-call(s32[1]{0:T(128)} %bitcast.flag, bf16[512,2048]{1,0:T(8,128)(2,1)S(1)} %copy-done.1, bf16[512,2048]{1,0:T(8,128)(2,1)S(1)} %pad_maximum_fusion.1.refs_1_, bf16[512,512]{1,0:T(8,128)(2,1)S(1)} %copy-done.13, bf16[512,1664]{1,0:T(8,128)(2,1)S(1)} %copy-done.4, ...), custom_call_target="tpu_custom_call" | custom-call | tf_op jit(solution)/shard_map/product/pallas_call | solution.py:149
  165.5 2.6 %collective-permute-start.22 = (bf16[512,256]{1,0:T(8,128)(2,1)S(1)}, bf16[512,256]{1,0:T(8,128)(2,1)S(1)}, u32[]{:S(2)}, u32[]{:S(2)}) collective-permute-start(bf16[512,256]{1,0:T(8,128)(2,1)S(1)} %pad_maximum_fusion.13), channel_id=1, source_target_pairs={{0,8},{4,12},{8,0},{12,4},{16,24},{20,28},{24,16},{28,20},{1,9},{5... | collective-permute-start | bytes 786440 | tf_op jit(solution)/shard_map/ppermute | solution.py:218
  168.1 2.3 %attend.6 = bf16[512,384]{1,0:T(8,128)(2,1)S(1)} custom-call(f32[512,384]{1,0:T(8,128)S(1)} %slice.99.mine, bf16[512,384]{1,0:T(8,128)(2,1)S(1)} %collective-permute-done.14.other, bf16[512,256]{1,0:T(8,128)(2,1)S(1)} %pad_maximum_fusion.12.keys_values, f32[512,384]{1,0:T(8,128)S(1)} %concatenate.71.tables, f32[1,128]{1,0:T(1,128)S(1)} %bitcast.7), custom_call_target="tpu_custom_call" | custom-call | tf_op jit(solution)/shard_map/attend/pallas_call | solution.py:87
  170.5 2.9 %attend.7 = bf16[512,512]{1,0:T(8,128)(2,1)S(1)} custom-call(f32[512,512]{1,0:T(8,128)S(1)} %get-tuple-element.47.mine, bf16[512,512]{1,0:T(8,128)(2,1)S(1)} %collective-permute-done.17.other, bf16[512,256]{1,0:T(8,128)(2,1)S(1)} %pad_maximum_fusion.12.keys_values, f32[512,384]{1,0:T(8,128)S(1)} %concatenate.71.tables, f32[1,128]{1,0:T(1,128)S(1)} %bitcast.8), custom_call_target="tpu_custom_call" | custom-call | tf_op jit(solution)/shard_map/attend/pallas_call | solution.py:87
  173.4 2.6 %product.9 = (bf16[512,128]{1,0:T(8,128)(2,1)S(1)}, f32[512,128]{1,0:T(8,128)S(1)}) custom-call(s32[1]{0:T(128)} %bitcast.flag, bf16[512,2048]{1,0:T(8,128)(2,1)S(1)} %copy-done.1, bf16[512,2048]{1,0:T(8,128)(2,1)S(1)} %pad_maximum_fusion.1.refs_1_, bf16[512,128]{1,0:T(8,128)(2,1)S(1)} %copy-done.24, ...), custom_call_target="tpu_custom_call" | custom-call | tf_op jit(solution)/shard_map/product/pallas_call | solution.py:149
  176.8 4.3 %collective-permute-done.23.other = bf16[512,128]{1,0:T(8,128)(2,1)S(1)} collective-permute-done((bf16[512,128]{1,0:T(8,128)(2,1)S(1)}, bf16[512,128]{1,0:T(8,128)(2,1)S(1)}, u32[]{:S(2)}, u32[]{:S(2)}) %collective-permute-start.23) | collective-permute-done | bytes 131104 | tf_op jit(solution)/shard_map/ppermute | solution.py:218
  182.4 2.9 %attend.8 = bf16[512,512]{1,0:T(8,128)(2,1)S(1)} custom-call(f32[512,512]{1,0:T(8,128)S(1)} %get-tuple-element.52.mine, bf16[512,512]{1,0:T(8,128)(2,1)S(1)} %collective-permute-done.20.other, bf16[512,256]{1,0:T(8,128)(2,1)S(1)} %pad_maximum_fusion.12.keys_values, f32[512,384]{1,0:T(8,128)S(1)} %concatenate.71.tables, f32[1,128]{1,0:T(1,128)S(1)} %bitcast.10), custom_call_target="tpu_custom_call" | custom-call | tf_op jit(solution)/shard_map/attend/pallas_call | solution.py:87
  (178 shorter events, 61.4 us)
Async XLA Ops:
  1.1 15.0 %collective-permute-start = (bf16[512,512]{1,0:T(8,128)(2,1)S(1)}, bf16[512,512]{1,0:T(8,128)(2,1)S(1)}, u32[]{:S(2)}, u32[]{:S(2)}) collective-permute-start(bf16[512,512]{1,0:T(8,128)(2,1)S(1)} %slice.84.refs_2_), channel_id=1, source_target_pairs={{0,8},{4,12},{8,0},{12,4},{16,24},{20,28},{24,16},{28,20},{1,9},{5... | collective-permute-start | bytes 1572872 | tf_op jit(solution)/shard_map/ppermute | solution.py:218
  4.2 11.9 %collective-permute-start.3 = (bf16[512,512]{1,0:T(8,128)(2,1)S(1)}, bf16[512,512]{1,0:T(8,128)(2,1)S(1)}, u32[]{:S(2)}, u32[]{:S(2)}) collective-permute-start(bf16[512,512]{1,0:T(8,128)(2,1)S(1)} %slice.84.refs_2_), channel_id=1, source_target_pairs={{8,16},{12,20},{16,8},{20,12},{9,17},{13,21},{17,9},{21,13},{10,18... | collective-permute-start | bytes 1572872 | tf_op jit(solution)/shard_map/ppermute | solution.py:218
  5.9 4.6 %collective-permute-start.5 = (bf16[512,128]{1,0:T(8,128)(2,1)S(1)}, bf16[512,128]{1,0:T(8,128)(2,1)S(1)}, u32[]{:S(2)}, u32[]{:S(2)}) collective-permute-start(bf16[512,128]{1,0:T(8,128)(2,1)S(1)} %get-tuple-element.79), channel_id=1, source_target_pairs={{0,0},{1,2},{2,1},{3,3},{4,4},{5,6},{6,5},{7,7},{8,8},{9,10},{10,9... | collective-permute-start | bytes 393224 | tf_op jit(solution)/shard_map/ppermute | solution.py:170
  6.5 7.1 %collective-permute-start.6 = (bf16[512,128]{1,0:T(8,128)(2,1)S(1)}, bf16[512,128]{1,0:T(8,128)(2,1)S(1)}, u32[]{:S(2)}, u32[]{:S(2)}) collective-permute-start(bf16[512,128]{1,0:T(8,128)(2,1)S(1)} %get-tuple-element.80), channel_id=1, source_target_pairs={{0,1},{1,3},{2,0},{3,2},{4,5},{5,7},{6,4},{7,6},{8,9},{9,11},{10,8... | collective-permute-start | bytes 393224 | tf_op jit(solution)/shard_map/ppermute | solution.py:174
  19.2 41.1 %collective-permute-start.7 = (bf16[512,1664]{1,0:T(8,128)(2,1)}, bf16[512,1664]{1,0:T(8,128)(2,1)S(1)}, u32[]{:S(2)}, u32[]{:S(2)}) collective-permute-start(bf16[512,1664]{1,0:T(8,128)(2,1)} %pad_maximum_fusion.2), channel_id=1, source_target_pairs={{0,8},{4,12},{8,0},{12,4},{16,24},{20,28},{24,16},{28,20},{1,9},{5... | collective-permute-start | bytes 5111816 | tf_op jit(solution)/shard_map/ppermute | solution.py:218
  25.2 6.8 %collective-permute-start.4 = (bf16[512,512]{1,0:T(8,128)(2,1)S(1)}, bf16[512,512]{1,0:T(8,128)(2,1)S(1)}, u32[]{:S(2)}, u32[]{:S(2)}) collective-permute-start(bf16[512,512]{1,0:T(8,128)(2,1)S(1)} %collective-permute-done.refs_3_), channel_id=1, source_target_pairs={{8,16},{12,20},{16,8},{20,12},{9,17},{13,21},{17,9},{21,13},{10,18... | collective-permute-start | bytes 1572872 | tf_op jit(solution)/shard_map/ppermute | solution.py:218
  28.4 35.4 %collective-permute-start.1 = (bf16[256,2048]{1,0:T(8,128)(2,1)}, bf16[256,2048]{1,0:T(8,128)(2,1)}, u32[]{:S(2)}, u32[]{:S(2)}) collective-permute-start(bf16[256,2048]{1,0:T(8,128)(2,1)} %pad_maximum_fusion.6), channel_id=1, source_target_pairs={{0,4},{4,0},{8,12},{12,8},{16,20},{20,16},{24,28},{28,24},{1,5},{5... | collective-permute-start | bytes 3145736 | tf_op jit(solution)/shard_map/ppermute | solution.py:218
  32.8 32.3 %collective-permute-start.10 = (bf16[512,1152]{1,0:T(8,128)(2,1)}, bf16[512,1152]{1,0:T(8,128)(2,1)S(1)}, u32[]{:S(2)}, u32[]{:S(2)}) collective-permute-start(bf16[512,1152]{1,0:T(8,128)(2,1)} %pad_maximum_fusion.5), channel_id=1, source_target_pairs={{8,16},{12,20},{16,8},{20,12},{9,17},{13,21},{17,9},{21,13},{10,18... | collective-permute-start | bytes 3538952 | tf_op jit(solution)/shard_map/ppermute | solution.py:218
  60.3 26.5 %collective-permute-start.8 = (bf16[512,1152]{1,0:T(8,128)(2,1)}, bf16[512,1152]{1,0:T(8,128)(2,1)}, u32[]{:S(2)}, u32[]{:S(2)}) collective-permute-start(bf16[512,1152]{1,0:T(8,128)(2,1)} %pad_maximum_fusion.4), channel_id=1, source_target_pairs={{0,8},{4,12},{8,0},{12,4},{16,24},{20,28},{24,16},{28,20},{1,9},{5... | collective-permute-start | bytes 3538952 | tf_op jit(solution)/shard_map/ppermute | solution.py:218
  63.9 25.3 %collective-permute-start.2 = (bf16[256,2048]{1,0:T(8,128)(2,1)}, bf16[256,2048]{1,0:T(8,128)(2,1)S(1)}, u32[]{:S(2)}, u32[]{:S(2)}) collective-permute-start(bf16[256,2048]{1,0:T(8,128)(2,1)} %collective-permute-done.1), channel_id=1, source_target_pairs={{0,1},{1,0},{2,3},{3,2},{4,5},{5,4},{6,7},{7,6},{8,9},{9,8},{10,11... | collective-permute-start | bytes 3145736 | tf_op jit(solution)/shard_map/ppermute | solution.py:256
  64.0 3.2 %collective-permute-start.11 = (bf16[512,640]{1,0:T(8,128)(2,1)S(1)}, bf16[512,640]{1,0:T(8,128)(2,1)S(1)}, u32[]{:S(2)}, u32[]{:S(2)}) collective-permute-start(bf16[512,640]{1,0:T(8,128)(2,1)S(1)} %slice.110), channel_id=1, source_target_pairs={{8,16},{12,20},{16,8},{20,12},{9,17},{13,21},{17,9},{21,13},{10,18... | collective-permute-start | bytes 1966088 | tf_op jit(solution)/shard_map/ppermute | solution.py:218
  67.2 29.9 %collective-permute-start.15 = (bf16[512,1024]{1,0:T(8,128)(2,1)S(1)}, bf16[512,1024]{1,0:T(8,128)(2,1)S(1)}, u32[]{:S(2)}, u32[]{:S(2)}) collective-permute-start(bf16[512,1024]{1,0:T(8,128)(2,1)S(1)} %pad_maximum_fusion.7), channel_id=1, source_target_pairs={{8,16},{12,20},{16,8},{20,12},{9,17},{13,21},{17,9},{21,13},{10,18... | collective-permute-start | bytes 3145736 | tf_op jit(solution)/shard_map/ppermute | solution.py:218
  86.8 28.7 %collective-permute-start.12 = (bf16[512,1280]{1,0:T(8,128)(2,1)S(1)}, bf16[512,1280]{1,0:T(8,128)(2,1)S(1)}, u32[]{:S(2)}, u32[]{:S(2)}) collective-permute-start(bf16[512,1280]{1,0:T(8,128)(2,1)S(1)} %pad_maximum_fusion.3), channel_id=1, source_target_pairs={{0,8},{4,12},{8,0},{12,4},{16,24},{20,28},{24,16},{28,20},{1,9},{5... | collective-permute-start | bytes 3932168 | tf_op jit(solution)/shard_map/ppermute | solution.py:218
  97.1 32.9 %collective-permute-start.18 = (bf16[512,640]{1,0:T(8,128)(2,1)}, bf16[512,640]{1,0:T(8,128)(2,1)}, u32[]{:S(2)}, u32[]{:S(2)}) collective-permute-start(bf16[512,640]{1,0:T(8,128)(2,1)} %pad_maximum_fusion.11), channel_id=1, source_target_pairs={{8,16},{12,20},{16,8},{20,12},{9,17},{13,21},{17,9},{21,13},{10,18... | collective-permute-start | bytes 1966088 | tf_op jit(solution)/shard_map/ppermute | solution.py:218
  115.5 23.6 %collective-permute-start.16 = (bf16[512,1024]{1,0:T(8,128)(2,1)}, bf16[512,1024]{1,0:T(8,128)(2,1)}, u32[]{:S(2)}, u32[]{:S(2)}) collective-permute-start(bf16[512,1024]{1,0:T(8,128)(2,1)} %pad_maximum_fusion.8), channel_id=1, source_target_pairs={{0,8},{4,12},{8,0},{12,4},{16,24},{20,28},{24,16},{28,20},{1,9},{5... | collective-permute-start | bytes 3145736 | tf_op jit(solution)/shard_map/ppermute | solution.py:218
  122.7 15.2 %collective-permute-start.13 = (f32[512,256]{1,0:T(8,128)}, f32[512,256]{1,0:T(8,128)}, u32[]{:S(2)}, u32[]{:S(2)}) collective-permute-start(f32[512,256]{1,0:T(8,128)} %slice.94), channel_id=1, source_target_pairs={{0,4},{4,0},{8,12},{12,8},{16,20},{20,16},{24,28},{28,24},{1,5},{5... | collective-permute-start | bytes 1572872 | tf_op jit(solution)/shard_map/ppermute | solution.py:218
  128.5 20.5 %collective-permute-start.9 = (bf16[512,512]{1,0:T(8,128)(2,1)S(1)}, bf16[512,512]{1,0:T(8,128)(2,1)S(1)}, u32[]{:S(2)}, u32[]{:S(2)}) collective-permute-start(bf16[512,512]{1,0:T(8,128)(2,1)S(1)} %copy-done.34), channel_id=1, source_target_pairs={{0,4},{4,0},{8,12},{12,8},{16,20},{20,16},{24,28},{28,24},{1,5},{5... | collective-permute-start | bytes 1572872 | tf_op jit(solution)/shard_map/ppermute | solution.py:218
  130.1 35.4 %collective-permute-start.21 = (bf16[512,128]{1,0:T(8,128)(2,1)S(1)}, bf16[512,128]{1,0:T(8,128)(2,1)S(1)}, u32[]{:S(2)}, u32[]{:S(2)}) collective-permute-start(bf16[512,128]{1,0:T(8,128)(2,1)S(1)} %slice.123), channel_id=1, source_target_pairs={{8,16},{12,20},{16,8},{20,12},{9,17},{13,21},{17,9},{21,13},{10,18... | collective-permute-start | bytes 393224 | tf_op jit(solution)/shard_map/ppermute | solution.py:218
  135.5 32.6 %collective-permute-start.14 = (bf16[512,384]{1,0:T(8,128)(2,1)S(1)}, bf16[512,384]{1,0:T(8,128)(2,1)S(1)}, u32[]{:S(2)}, u32[]{:S(2)}) collective-permute-start(bf16[512,384]{1,0:T(8,128)(2,1)S(1)} %slice.134), channel_id=1, source_target_pairs={{0,4},{4,0},{8,12},{12,8},{16,20},{20,16},{24,28},{28,24},{1,5},{5... | collective-permute-start | bytes 1179656 | tf_op jit(solution)/shard_map/ppermute | solution.py:218
  139.2 21.4 %collective-permute-start.19 = (bf16[512,1024]{1,0:T(8,128)(2,1)S(1)}, bf16[512,1024]{1,0:T(8,128)(2,1)S(1)}, u32[]{:S(2)}, u32[]{:S(2)}) collective-permute-start(bf16[512,1024]{1,0:T(8,128)(2,1)S(1)} %pad_maximum_fusion.9), channel_id=1, source_target_pairs={{0,8},{4,12},{8,0},{12,4},{16,24},{20,28},{24,16},{28,20},{1,9},{5... | collective-permute-start | bytes 3145736 | tf_op jit(solution)/shard_map/ppermute | solution.py:218
  145.4 25.1 %collective-permute-start.17 = (bf16[512,512]{1,0:T(8,128)(2,1)S(1)}, bf16[512,512]{1,0:T(8,128)(2,1)S(1)}, u32[]{:S(2)}, u32[]{:S(2)}) collective-permute-start(bf16[512,512]{1,0:T(8,128)(2,1)S(1)} %get-tuple-element.48), channel_id=1, source_target_pairs={{0,4},{4,0},{8,12},{12,8},{16,20},{20,16},{24,28},{28,24},{1,5},{5... | collective-permute-start | bytes 1572872 | tf_op jit(solution)/shard_map/ppermute | solution.py:218
  163.9 18.6 %collective-permute-start.20 = (bf16[512,512]{1,0:T(8,128)(2,1)S(1)}, bf16[512,512]{1,0:T(8,128)(2,1)S(1)}, u32[]{:S(2)}, u32[]{:S(2)}) collective-permute-start(bf16[512,512]{1,0:T(8,128)(2,1)S(1)} %get-tuple-element.53), channel_id=1, source_target_pairs={{0,4},{4,0},{8,12},{12,8},{16,20},{20,16},{24,28},{28,24},{1,5},{5... | collective-permute-start | bytes 1572872 | tf_op jit(solution)/shard_map/ppermute | solution.py:218
  165.5 7.9 %collective-permute-start.22 = (bf16[512,256]{1,0:T(8,128)(2,1)S(1)}, bf16[512,256]{1,0:T(8,128)(2,1)S(1)}, u32[]{:S(2)}, u32[]{:S(2)}) collective-permute-start(bf16[512,256]{1,0:T(8,128)(2,1)S(1)} %pad_maximum_fusion.13), channel_id=1, source_target_pairs={{0,8},{4,12},{8,0},{12,4},{16,24},{20,28},{24,16},{28,20},{1,9},{5... | collective-permute-start | bytes 786440 | tf_op jit(solution)/shard_map/ppermute | solution.py:218
  176.0 5.0 %collective-permute-start.23 = (bf16[512,128]{1,0:T(8,128)(2,1)S(1)}, bf16[512,128]{1,0:T(8,128)(2,1)S(1)}, u32[]{:S(2)}, u32[]{:S(2)}) collective-permute-start(bf16[512,128]{1,0:T(8,128)(2,1)S(1)} %get-tuple-element.58), channel_id=1, source_target_pairs={{0,4},{4,0},{8,12},{12,8},{16,20},{20,16},{24,28},{28,24},{1,5},{5... | collective-permute-start | bytes 393224 | tf_op jit(solution)/shard_map/ppermute | solution.py:218
  (44 other events, 295.6 us)

commit v4 on v3

--- a/solution.py
+++ b/solution.py
@@ -122,15 +122,15 @@
 
     pl.when(flag[0] == 1)(lambda: start_all(windows[:count]))
     pl.when(flag[0] == 0)(lambda: start_all(windows[count:]))
-    for i in range(count):
-        rows_of(windows, i).wait()
-        for side in range(sides):
-            features_of(side, i).wait()
     for side in range(sides):
-        for r in range(rows // block):
-            here = pl.ds(r * block, block)
+        for r in range(0, rows, block):
+            here = pl.ds(r, block)
             total = jnp.zeros((block, cols), jnp.float32)
             for i in range(count):
+                if r == 0:
+                    features_of(side, i).wait()
+                    if side == 0:
+                        rows_of(windows, i).wait()
                 total += jnp.dot(
                     features[side, i, here, :], weights[i], preferred_element_type=jnp.float32
                 )
@@ -252,7 +252,7 @@
     twins = [(a, a ^ 1) for a in range(n_head)]
     share = rows // 2
     part = lax.dynamic_slice_in_dim(tokens, head % 2 * share, share, 0)
-    part = send(features(after(part, first), 1 - side), across)
+    part = send(features(part, 1 - side), across)
     twin = lax.ppermute(part, "head", twins)
     beside_tokens = jnp.concatenate(
         [jnp.where(even, part, twin), jnp.where(even, twin, part)], axis=0
@@ -290,7 +290,7 @@
     got[0] = (first, 0)
     go_round([0], None)
     arrived = lambda table, k: [p for p, _ in table.get(k, [])]
-    second = send(joined([after(owns[1], first, *arrived(hub_at, 0))] + owns[2:4]), swap)
+    second = send(joined(owns[1:4]), swap)
     for k in range(1, min(4, count)):
         got[k] = (second, sum(wides[1:k]))
     go_round([], 0)
@@ -311,7 +311,7 @@
             got[k + 4] = (passed, 0)
         go_round([k + 4], k + 3, *arrived(leaf_at, k + 2))
         wide = wides[k]
-        at_leaf = [own_at for own_at in [(owns[k], 0), got[k]]]
+        at_leaf = [(owns[k], 0), got[k]]
         at_leaf += [(passed, low + i * wide) for i in range(2 * (n_pairs - 1))]
         pieces = woven((owns[k], 0), got[k], hub_at[k], leaf_at[k]), at_leaf
         done = parts[: max(0, k - 2 + (k + 1 == count))][-2:]
@@ -334,12 +334,12 @@
         sums.append((mine, other))
         computed.append(mine)
         if keys is not None:
-            late = 1
-            while len(parts) < len(sums) - late:
+            while len(parts) < len(sums) - 1:
                 parts.append(
                     attend(*sums[len(parts)], keys_values, own_tables, q_gain[None, :])
                 )
-    parts.append(attend(*sums[-1], keys_values, own_tables, q_gain[None, :]))
+    last, other = sums[-1]
+    parts.append(attend(after(last, *parts[-1:]), other, keys_values, own_tables, q_gain[None, :]))
     return jnp.concatenate(parts, axis=1)
 
 

time: 188 us -> 194 us (1.032)
  starting transfers between devices: 35.5 us -> 42.3 us
  local copies, waits for them, and re-layouts: 26.5 us -> 22.9 us
  other arithmetic: 16.6 us -> 19.6 us
  waiting for transfers between devices: 76.8 us -> 74.1 us
    ppermute x21, starting transfers between devices: 31.9 us -> 38.7 us  [shards(): send = lambda value, moves: lax.ppermute(value, 'dp', moves)]
    unnamed x88 -> x74, local copies, waits for them, and re-layouts: 6.37 us -> 2.6 us
    ppermute x21, waiting for transfers between devices: 73.7 us -> 71.1 us  [shards(): send = lambda value, moves: lax.ppermute(value, 'dp', moves)]
    slice x3 -> x4, local copies, waits for them, and re-layouts: 3.51 us -> 0.93 us  [shards(): owns += [late_weight[:, low:high] for low, high in bounds[2:]]]
    slice x10 -> x9, local copies, waits for them, and re-layouts: 3.94 us -> 5.91 us  [shards(): cut = lambda k, where: where[0][:, where[1]:where[1] + wides[k]]]
  transfers between devices with their start and end apart: 24 -> 24, of which waited for: 9 -> 10; matrix products, arithmetic and copies ran while one was open for 17% -> 19% of each run, Pallas kernels for 15% -> 16%
where the time goes in v4:
time: 194 us; the launch traced here: 193 us
  waiting for transfers between devices  74.1 us (38%)
  starting transfers between devices  42.3 us (22%)
  Pallas kernels  32.9 us (17%)
  local copies, waits for them, and re-layouts  22.9 us (12%)
  other arithmetic  19.6 us (10%)
    ppermute x21, waiting for transfers between devices, shards(): send = lambda value, moves: lax.ppermute(value, 'dp', moves)  71.1 us
    ppermute x21, starting transfers between devices, shards(): send = lambda value, moves: lax.ppermute(value, 'dp', moves)  38.7 us
    pallas_call x5, Pallas kernels, product(): pl.pallas_call(functools.partial(product_kernel, tuple(windows), count, s...  20.6 us
    pallas_call x5, Pallas kernels, attend(): pl.pallas_call(functools.partial(attend_kernel, block), grid=(cols // ste...  12.3 us
    concatenate x9, other arithmetic, shards(): jnp.concatenate(blocks, axis=1)  9.39 us
    slice x9, local copies, waits for them, and re-layouts, shards(): cut = lambda k, where: where[0][:, where[1]:where[1] + wides[k]]  5.91 us
  transfers between devices with their start and end apart: 24, of which 10 were waited for; matrix products, arithmetic and copies ran while one was open for 19% of the time, Pallas kernels for 16%

profile of v4, /device:TPU:0, one launch (start us, length us, event | category | flops | bytes accessed | tf_op | source)
XLA Modules:
  0.0 192.6 jit_solution(11912578406019590961)
XLA Ops:
  1.9 3.0 %collective-permute-start.2 = (bf16[512,512]{1,0:T(8,128)(2,1)}, bf16[512,512]{1,0:T(8,128)(2,1)S(1)}, u32[]{:S(2)}, u32[]{:S(2)}) collective-permute-start(bf16[512,512]{1,0:T(8,128)(2,1)} %slice.84.refs_2_), channel_id=1, source_target_pairs={{0,8},{4,12},{8,0},{12,4},{16,24},{20,28},{24,16},{28,20},{1,9},{5... | collective-permute-start | bytes 1572872 | tf_op jit(solution)/shard_map/ppermute | solution.py:218
  6.6 2.9 %collective-permute-start.6 = (bf16[512,128]{1,0:T(8,128)(2,1)S(1)}, bf16[512,128]{1,0:T(8,128)(2,1)S(1)}, u32[]{:S(2)}, u32[]{:S(2)}) collective-permute-start(bf16[512,128]{1,0:T(8,128)(2,1)S(1)} %get-tuple-element.78), channel_id=1, source_target_pairs={{0,1},{1,3},{2,0},{3,2},{4,5},{5,7},{6,4},{7,6},{8,9},{9,11},{10,8... | collective-permute-start | bytes 393224 | tf_op jit(solution)/shard_map/ppermute | solution.py:174
  10.6 3.0 %collective-permute-done.6 = bf16[512,128]{1,0:T(8,128)(2,1)S(1)} collective-permute-done((bf16[512,128]{1,0:T(8,128)(2,1)S(1)}, bf16[512,128]{1,0:T(8,128)(2,1)S(1)}, u32[]{:S(2)}, u32[]{:S(2)}) %collective-permute-start.6) | collective-permute-done | bytes 131104 | tf_op jit(solution)/shard_map/ppermute | solution.py:174
  13.7 3.3 %collective-permute-done.2.refs_3_ = bf16[512,512]{1,0:T(8,128)(2,1)S(1)} collective-permute-done((bf16[512,512]{1,0:T(8,128)(2,1)}, bf16[512,512]{1,0:T(8,128)(2,1)S(1)}, u32[]{:S(2)}, u32[]{:S(2)}) %collective-permute-start.2) | collective-permute-done | bytes 524320 | tf_op jit(solution)/shard_map/ppermute | solution.py:218
  32.8 14.5 %collective-permute-done = bf16[256,2048]{1,0:T(8,128)(2,1)} collective-permute-done((bf16[256,2048]{1,0:T(8,128)(2,1)}, bf16[256,2048]{1,0:T(8,128)(2,1)}, u32[]{:S(2)}, u32[]{:S(2)}) %collective-permute-start) | collective-permute-done | bytes 1048608 | tf_op jit(solution)/shard_map/ppermute | solution.py:218
  47.3 2.2 %pad_maximum_fusion.4 = bf16[512,1152]{1,0:T(8,128)(2,1)} fusion(bf16[512,512]{1,0:T(8,128)(2,1)S(1)} %copy-done.15, bf16[512,512]{1,0:T(8,128)(2,1)} %collective-permute-done.3.refs_4_, bf16[512,128]{1,0:T(8,128)(2,1)S(1)} %slice.85.refs_2_), kind=kLoop, calls=%fused_computation.4 | loop fusion | flops 3538944 | bytes 2359296 | tf_op jit(solution)/shard_map/concatenate | solution.py:275
  49.5 7.5 %collective-permute-done.7.refs_3_ = bf16[512,1664]{1,0:T(8,128)(2,1)S(1)} collective-permute-done((bf16[512,1664]{1,0:T(8,128)(2,1)}, bf16[512,1664]{1,0:T(8,128)(2,1)S(1)}, u32[]{:S(2)}, u32[]{:S(2)}) %collective-permute-start.7) | collective-permute-done | bytes 1703968 | tf_op jit(solution)/shard_map/ppermute | solution.py:218
  57.0 3.8 %collective-permute-start.8 = (bf16[512,1152]{1,0:T(8,128)(2,1)}, bf16[512,1152]{1,0:T(8,128)(2,1)}, u32[]{:S(2)}, u32[]{:S(2)}) collective-permute-start(bf16[512,1152]{1,0:T(8,128)(2,1)} %pad_maximum_fusion.4), channel_id=1, source_target_pairs={{0,8},{4,12},{8,0},{12,4},{16,24},{20,28},{24,16},{28,20},{1,9},{5... | collective-permute-start | bytes 3538952 | tf_op jit(solution)/shard_map/ppermute | solution.py:218
  70.3 17.4 %collective-permute-done.8.refs_6_.refs_3_ = bf16[512,1152]{1,0:T(8,128)(2,1)} collective-permute-done((bf16[512,1152]{1,0:T(8,128)(2,1)}, bf16[512,1152]{1,0:T(8,128)(2,1)}, u32[]{:S(2)}, u32[]{:S(2)}) %collective-permute-start.8) | collective-permute-done | bytes 1179680 | tf_op jit(solution)/shard_map/ppermute | solution.py:218
  87.7 11.3 %collective-permute-start.12 = (bf16[512,1280]{1,0:T(8,128)(2,1)S(1)}, bf16[512,1280]{1,0:T(8,128)(2,1)S(1)}, u32[]{:S(2)}, u32[]{:S(2)}) collective-permute-start(bf16[512,1280]{1,0:T(8,128)(2,1)S(1)} %pad_maximum_fusion.3), channel_id=1, source_target_pairs={{0,8},{4,12},{8,0},{12,4},{16,24},{20,28},{24,16},{28,20},{1,9},{5... | collective-permute-start | bytes 3932168 | tf_op jit(solution)/shard_map/ppermute | solution.py:218
  102.9 4.0 %product.5 = (bf16[512,512]{1,0:T(8,128)(2,1)S(1)}, f32[512,512]{1,0:T(8,128)S(1)}) custom-call(s32[1]{0:T(128)} %bitcast.flag, bf16[512,2048]{1,0:T(8,128)(2,1)S(1)} %pad_maximum_fusion.refs_0_, bf16[512,2048]{1,0:T(8,128)(2,1)S(1)} %pad_maximum_fusion.1.refs_1_, bf16[512,512]{1,0:T(8,128)(2,1)} %slice.84.refs_2_, bf16[512,512]{1,0:T(8,128)(2,1)S(1)} %copy-done.23, ...), custom_call_target="tpu_custom_call" | custom-call | tf_op jit(solution)/shard_map/product/pallas_call | solution.py:149
  110.6 15.2 %collective-permute-done.12.refs_6_ = bf16[512,1280]{1,0:T(8,128)(2,1)S(1)} collective-permute-done((bf16[512,1280]{1,0:T(8,128)(2,1)S(1)}, bf16[512,1280]{1,0:T(8,128)(2,1)S(1)}, u32[]{:S(2)}, u32[]{:S(2)}) %collective-permute-start.12) | collective-permute-done | bytes 1310752 | tf_op jit(solution)/shard_map/ppermute | solution.py:218
  127.7 5.5 %product.6 = (f32[512,640]{1,0:T(8,128)S(1)}, f32[512,640]{1,0:T(8,128)S(1)}) custom-call(s32[1]{0:T(128)} %bitcast.flag, bf16[512,2048]{1,0:T(8,128)(2,1)S(1)} %pad_maximum_fusion.refs_0_, bf16[512,2048]{1,0:T(8,128)(2,1)S(1)} %pad_maximum_fusion.1.refs_1_, bf16[512,640]{1,0:T(8,128)(2,1)S(1)} %pad_maximum_fusion.10.refs_2_, ...), custom_call_target="tpu_custom_call" | custom-call | tf_op jit(solution)/shard_map/product/pallas_call | solution.py:149
  146.8 2.6 %collective-permute-done.13 = f32[512,256]{1,0:T(8,128)} collective-permute-done((f32[512,256]{1,0:T(8,128)}, f32[512,256]{1,0:T(8,128)}, u32[]{:S(2)}, u32[]{:S(2)}) %collective-permute-start.13) | collective-permute-done | bytes 524320 | tf_op jit(solution)/shard_map/ppermute | solution.py:218
  151.3 4.0 %product.7 = (bf16[512,512]{1,0:T(8,128)(2,1)S(1)}, f32[512,512]{1,0:T(8,128)S(1)}) custom-call(s32[1]{0:T(128)} %bitcast.flag, bf16[512,2048]{1,0:T(8,128)(2,1)S(1)} %copy-done.1, bf16[512,2048]{1,0:T(8,128)(2,1)S(1)} %pad_maximum_fusion.1.refs_1_, bf16[512,512]{1,0:T(8,128)(2,1)S(1)} %copy-done.13, bf16[512,1664]{1,0:T(8,128)(2,1)S(1)} %copy-done.4, ...), custom_call_target="tpu_custom_call" | custom-call | tf_op jit(solution)/shard_map/product/pallas_call | solution.py:149
  156.2 4.3 %collective-permute-done.9.other = bf16[512,512]{1,0:T(8,128)(2,1)S(1)} collective-permute-done((bf16[512,512]{1,0:T(8,128)(2,1)}, bf16[512,512]{1,0:T(8,128)(2,1)S(1)}, u32[]{:S(2)}, u32[]{:S(2)}) %collective-permute-start.9) | collective-permute-done | bytes 524320 | tf_op jit(solution)/shard_map/ppermute | solution.py:218
  160.5 2.9 %attend.5 = bf16[512,512]{1,0:T(8,128)(2,1)S(1)} custom-call(f32[512,512]{1,0:T(8,128)S(1)} %copy-done.20, bf16[512,512]{1,0:T(8,128)(2,1)S(1)} %collective-permute-done.9.other, bf16[512,256]{1,0:T(8,128)(2,1)S(1)} %pad_maximum_fusion.12.keys_values, f32[512,384]{1,0:T(8,128)S(1)} %concatenate.72.tables, f32[1,128]{1,0:T(1,128)S(1)} %bitcast.6), custom_call_target="tpu_custom_call" | custom-call | tf_op jit(solution)/shard_map/attend/pallas_call | solution.py:87
  163.4 5.8 %collective-permute-done.19.refs_6_ = bf16[512,1024]{1,0:T(8,128)(2,1)S(1)} collective-permute-done((bf16[512,1024]{1,0:T(8,128)(2,1)S(1)}, bf16[512,1024]{1,0:T(8,128)(2,1)S(1)}, u32[]{:S(2)}, u32[]{:S(2)}) %collective-permute-start.19) | collective-permute-done | bytes 1048608 | tf_op jit(solution)/shard_map/ppermute | solution.py:218
  169.2 3.8 %product.8 = (bf16[512,512]{1,0:T(8,128)(2,1)S(1)}, f32[512,512]{1,0:T(8,128)S(1)}) custom-call(s32[1]{0:T(128)} %bitcast.flag, bf16[512,2048]{1,0:T(8,128)(2,1)S(1)} %copy-done.1, bf16[512,2048]{1,0:T(8,128)(2,1)S(1)} %pad_maximum_fusion.1.refs_1_, bf16[512,512]{1,0:T(8,128)(2,1)S(1)} %copy-done.11, bf16[512,1664]{1,0:T(8,128)(2,1)S(1)} %copy-done.4, ...), custom_call_target="tpu_custom_call" | custom-call | tf_op jit(solution)/shard_map/product/pallas_call | solution.py:149
  174.7 2.1 %collective-permute-start.22 = (bf16[512,256]{1,0:T(8,128)(2,1)S(1)}, bf16[512,256]{1,0:T(8,128)(2,1)S(1)}, u32[]{:S(2)}, u32[]{:S(2)}) collective-permute-start(bf16[512,256]{1,0:T(8,128)(2,1)S(1)} %pad_maximum_fusion.13), channel_id=1, source_target_pairs={{0,8},{4,12},{8,0},{12,4},{16,24},{20,28},{24,16},{28,20},{1,9},{5... | collective-permute-start | bytes 786440 | tf_op jit(solution)/shard_map/ppermute | solution.py:218
  176.7 2.3 %attend.6 = bf16[512,384]{1,0:T(8,128)(2,1)S(1)} custom-call(f32[512,384]{1,0:T(8,128)S(1)} %slice.99.mine, bf16[512,384]{1,0:T(8,128)(2,1)S(1)} %collective-permute-done.14.other, bf16[512,256]{1,0:T(8,128)(2,1)S(1)} %pad_maximum_fusion.12.keys_values, f32[512,384]{1,0:T(8,128)S(1)} %concatenate.72.tables, f32[1,128]{1,0:T(1,128)S(1)} %bitcast.7), custom_call_target="tpu_custom_call" | custom-call | tf_op jit(solution)/shard_map/attend/pallas_call | solution.py:87
  179.2 2.9 %attend.7 = bf16[512,512]{1,0:T(8,128)(2,1)S(1)} custom-call(f32[512,512]{1,0:T(8,128)S(1)} %get-tuple-element.44.mine, bf16[512,512]{1,0:T(8,128)(2,1)S(1)} %collective-permute-done.17.other, bf16[512,256]{1,0:T(8,128)(2,1)S(1)} %pad_maximum_fusion.12.keys_values, f32[512,384]{1,0:T(8,128)S(1)} %concatenate.72.tables, f32[1,128]{1,0:T(1,128)S(1)} %bitcast.8), custom_call_target="tpu_custom_call" | custom-call | tf_op jit(solution)/shard_map/attend/pallas_call | solution.py:87
  182.1 3.4 %product.9 = (bf16[512,128]{1,0:T(8,128)(2,1)S(1)}, f32[512,128]{1,0:T(8,128)S(1)}) custom-call(s32[1]{0:T(128)} %bitcast.flag, bf16[512,2048]{1,0:T(8,128)(2,1)S(1)} %copy-done.1, bf16[512,2048]{1,0:T(8,128)(2,1)S(1)} %pad_maximum_fusion.1.refs_1_, bf16[512,128]{1,0:T(8,128)(2,1)S(1)} %slice.85.refs_2_, ...), custom_call_target="tpu_custom_call" | custom-call | tf_op jit(solution)/shard_map/product/pallas_call | solution.py:149
  186.9 2.9 %attend.8 = bf16[512,512]{1,0:T(8,128)(2,1)S(1)} custom-call(f32[512,512]{1,0:T(8,128)S(1)} %get-tuple-element.49.mine, bf16[512,512]{1,0:T(8,128)(2,1)S(1)} %collective-permute-done.20.other, bf16[512,256]{1,0:T(8,128)(2,1)S(1)} %pad_maximum_fusion.12.keys_values, f32[512,384]{1,0:T(8,128)S(1)} %concatenate.72.tables, f32[1,128]{1,0:T(1,128)S(1)} %bitcast.9), custom_call_target="tpu_custom_call" | custom-call | tf_op jit(solution)/shard_map/attend/pallas_call | solution.py:87
  (163 shorter events, 61.5 us)
Async XLA Ops:
  1.9 15.2 %collective-permute-start.2 = (bf16[512,512]{1,0:T(8,128)(2,1)}, bf16[512,512]{1,0:T(8,128)(2,1)S(1)}, u32[]{:S(2)}, u32[]{:S(2)}) collective-permute-start(bf16[512,512]{1,0:T(8,128)(2,1)} %slice.84.refs_2_), channel_id=1, source_target_pairs={{0,8},{4,12},{8,0},{12,4},{16,24},{20,28},{24,16},{28,20},{1,9},{5... | collective-permute-start | bytes 1572872 | tf_op jit(solution)/shard_map/ppermute | solution.py:218
  5.9 4.7 %collective-permute-start.5 = (bf16[512,128]{1,0:T(8,128)(2,1)S(1)}, bf16[512,128]{1,0:T(8,128)(2,1)S(1)}, u32[]{:S(2)}, u32[]{:S(2)}) collective-permute-start(bf16[512,128]{1,0:T(8,128)(2,1)S(1)} %get-tuple-element.77), channel_id=1, source_target_pairs={{0,0},{1,2},{2,1},{3,3},{4,4},{5,6},{6,5},{7,7},{8,8},{9,10},{10,9... | collective-permute-start | bytes 393224 | tf_op jit(solution)/shard_map/ppermute | solution.py:170
  6.6 7.1 %collective-permute-start.6 = (bf16[512,128]{1,0:T(8,128)(2,1)S(1)}, bf16[512,128]{1,0:T(8,128)(2,1)S(1)}, u32[]{:S(2)}, u32[]{:S(2)}) collective-permute-start(bf16[512,128]{1,0:T(8,128)(2,1)S(1)} %get-tuple-element.78), channel_id=1, source_target_pairs={{0,1},{1,3},{2,0},{3,2},{4,5},{5,7},{6,4},{7,6},{8,9},{9,11},{10,8... | collective-permute-start | bytes 393224 | tf_op jit(solution)/shard_map/ppermute | solution.py:174
  18.4 38.6 %collective-permute-start.7 = (bf16[512,1664]{1,0:T(8,128)(2,1)}, bf16[512,1664]{1,0:T(8,128)(2,1)S(1)}, u32[]{:S(2)}, u32[]{:S(2)}) collective-permute-start(bf16[512,1664]{1,0:T(8,128)(2,1)} %pad_maximum_fusion.2), channel_id=1, source_target_pairs={{0,8},{4,12},{8,0},{12,4},{16,24},{20,28},{24,16},{28,20},{1,9},{5... | collective-permute-start | bytes 5111816 | tf_op jit(solution)/shard_map/ppermute | solution.py:218
  23.2 24.1 %collective-permute-start = (bf16[256,2048]{1,0:T(8,128)(2,1)}, bf16[256,2048]{1,0:T(8,128)(2,1)}, u32[]{:S(2)}, u32[]{:S(2)}) collective-permute-start(bf16[256,2048]{1,0:T(8,128)(2,1)} %pad_maximum_fusion.6), channel_id=1, source_target_pairs={{0,4},{4,0},{8,12},{12,8},{16,20},{20,16},{24,28},{28,24},{1,5},{5... | collective-permute-start | bytes 3145736 | tf_op jit(solution)/shard_map/ppermute | solution.py:218
  24.8 22.5 %collective-permute-start.3 = (bf16[512,512]{1,0:T(8,128)(2,1)}, bf16[512,512]{1,0:T(8,128)(2,1)}, u32[]{:S(2)}, u32[]{:S(2)}) collective-permute-start(bf16[512,512]{1,0:T(8,128)(2,1)} %slice.84.refs_2_), channel_id=1, source_target_pairs={{8,16},{12,20},{16,8},{20,12},{9,17},{13,21},{17,9},{21,13},{10,18... | collective-permute-start | bytes 1572872 | tf_op jit(solution)/shard_map/ppermute | solution.py:218
  26.2 2.8 %collective-permute-start.4 = (bf16[512,512]{1,0:T(8,128)(2,1)S(1)}, bf16[512,512]{1,0:T(8,128)(2,1)S(1)}, u32[]{:S(2)}, u32[]{:S(2)}) collective-permute-start(bf16[512,512]{1,0:T(8,128)(2,1)S(1)} %collective-permute-done.2.refs_3_), channel_id=1, source_target_pairs={{8,16},{12,20},{16,8},{20,12},{9,17},{13,21},{17,9},{21,13},{10,18... | collective-permute-start | bytes 1572872 | tf_op jit(solution)/shard_map/ppermute | solution.py:218
  29.8 38.3 %collective-permute-start.10 = (bf16[512,1152]{1,0:T(8,128)(2,1)}, bf16[512,1152]{1,0:T(8,128)(2,1)S(1)}, u32[]{:S(2)}, u32[]{:S(2)}) collective-permute-start(bf16[512,1152]{1,0:T(8,128)(2,1)} %pad_maximum_fusion.5), channel_id=1, source_target_pairs={{8,16},{12,20},{16,8},{20,12},{9,17},{13,21},{17,9},{21,13},{10,18... | collective-permute-start | bytes 3538952 | tf_op jit(solution)/shard_map/ppermute | solution.py:218
  47.3 51.7 %collective-permute-start.1 = (bf16[256,2048]{1,0:T(8,128)(2,1)}, bf16[256,2048]{1,0:T(8,128)(2,1)}, u32[]{:S(2)}, u32[]{:S(2)}) collective-permute-start(bf16[256,2048]{1,0:T(8,128)(2,1)} %collective-permute-done), channel_id=1, source_target_pairs={{0,1},{1,0},{2,3},{3,2},{4,5},{5,4},{6,7},{7,6},{8,9},{9,8},{10,11... | collective-permute-start | bytes 3145736 | tf_op jit(solution)/shard_map/ppermute | solution.py:256
  57.0 30.7 %collective-permute-start.8 = (bf16[512,1152]{1,0:T(8,128)(2,1)}, bf16[512,1152]{1,0:T(8,128)(2,1)}, u32[]{:S(2)}, u32[]{:S(2)}) collective-permute-start(bf16[512,1152]{1,0:T(8,128)(2,1)} %pad_maximum_fusion.4), channel_id=1, source_target_pairs={{0,8},{4,12},{8,0},{12,4},{16,24},{20,28},{24,16},{28,20},{1,9},{5... | collective-permute-start | bytes 3538952 | tf_op jit(solution)/shard_map/ppermute | solution.py:218
  63.1 5.3 %collective-permute-start.11 = (bf16[512,640]{1,0:T(8,128)(2,1)}, bf16[512,640]{1,0:T(8,128)(2,1)}, u32[]{:S(2)}, u32[]{:S(2)}) collective-permute-start(bf16[512,640]{1,0:T(8,128)(2,1)} %slice.110), channel_id=1, source_target_pairs={{8,16},{12,20},{16,8},{20,12},{9,17},{13,21},{17,9},{21,13},{10,18... | collective-permute-start | bytes 1966088 | tf_op jit(solution)/shard_map/ppermute | solution.py:218
  68.4 38.5 %collective-permute-start.15 = (bf16[512,1024]{1,0:T(8,128)(2,1)S(1)}, bf16[512,1024]{1,0:T(8,128)(2,1)S(1)}, u32[]{:S(2)}, u32[]{:S(2)}) collective-permute-start(bf16[512,1024]{1,0:T(8,128)(2,1)S(1)} %pad_maximum_fusion.7), channel_id=1, source_target_pairs={{8,16},{12,20},{16,8},{20,12},{9,17},{13,21},{17,9},{21,13},{10,18... | collective-permute-start | bytes 3145736 | tf_op jit(solution)/shard_map/ppermute | solution.py:218
  87.7 38.0 %collective-permute-start.12 = (bf16[512,1280]{1,0:T(8,128)(2,1)S(1)}, bf16[512,1280]{1,0:T(8,128)(2,1)S(1)}, u32[]{:S(2)}, u32[]{:S(2)}) collective-permute-start(bf16[512,1280]{1,0:T(8,128)(2,1)S(1)} %pad_maximum_fusion.3), channel_id=1, source_target_pairs={{0,8},{4,12},{8,0},{12,4},{16,24},{20,28},{24,16},{28,20},{1,9},{5... | collective-permute-start | bytes 3932168 | tf_op jit(solution)/shard_map/ppermute | solution.py:218
  106.9 34.6 %collective-permute-start.18 = (bf16[512,640]{1,0:T(8,128)(2,1)}, bf16[512,640]{1,0:T(8,128)(2,1)}, u32[]{:S(2)}, u32[]{:S(2)}) collective-permute-start(bf16[512,640]{1,0:T(8,128)(2,1)} %pad_maximum_fusion.11), channel_id=1, source_target_pairs={{8,16},{12,20},{16,8},{20,12},{9,17},{13,21},{17,9},{21,13},{10,18... | collective-permute-start | bytes 1966088 | tf_op jit(solution)/shard_map/ppermute | solution.py:218
  125.7 24.9 %collective-permute-start.16 = (bf16[512,1024]{1,0:T(8,128)(2,1)}, bf16[512,1024]{1,0:T(8,128)(2,1)}, u32[]{:S(2)}, u32[]{:S(2)}) collective-permute-start(bf16[512,1024]{1,0:T(8,128)(2,1)} %pad_maximum_fusion.8), channel_id=1, source_target_pairs={{0,8},{4,12},{8,0},{12,4},{16,24},{20,28},{24,16},{28,20},{1,9},{5... | collective-permute-start | bytes 3145736 | tf_op jit(solution)/shard_map/ppermute | solution.py:218
  134.2 15.2 %collective-permute-start.13 = (f32[512,256]{1,0:T(8,128)}, f32[512,256]{1,0:T(8,128)}, u32[]{:S(2)}, u32[]{:S(2)}) collective-permute-start(f32[512,256]{1,0:T(8,128)} %slice.94), channel_id=1, source_target_pairs={{0,4},{4,0},{8,12},{12,8},{16,20},{20,16},{24,28},{28,24},{1,5},{5... | collective-permute-start | bytes 1572872 | tf_op jit(solution)/shard_map/ppermute | solution.py:218
  139.1 21.4 %collective-permute-start.9 = (bf16[512,512]{1,0:T(8,128)(2,1)}, bf16[512,512]{1,0:T(8,128)(2,1)S(1)}, u32[]{:S(2)}, u32[]{:S(2)}) collective-permute-start(bf16[512,512]{1,0:T(8,128)(2,1)} %copy-done.25), channel_id=1, source_target_pairs={{0,4},{4,0},{8,12},{12,8},{16,20},{20,16},{24,28},{28,24},{1,5},{5... | collective-permute-start | bytes 1572872 | tf_op jit(solution)/shard_map/ppermute | solution.py:218
  141.5 33.1 %collective-permute-start.21 = (bf16[512,128]{1,0:T(8,128)(2,1)S(1)}, bf16[512,128]{1,0:T(8,128)(2,1)S(1)}, u32[]{:S(2)}, u32[]{:S(2)}) collective-permute-start(bf16[512,128]{1,0:T(8,128)(2,1)S(1)} %slice.123), channel_id=1, source_target_pairs={{8,16},{12,20},{16,8},{20,12},{9,17},{13,21},{17,9},{21,13},{10,18... | collective-permute-start | bytes 393224 | tf_op jit(solution)/shard_map/ppermute | solution.py:218
  146.1 30.6 %collective-permute-start.14 = (bf16[512,384]{1,0:T(8,128)(2,1)S(1)}, bf16[512,384]{1,0:T(8,128)(2,1)S(1)}, u32[]{:S(2)}, u32[]{:S(2)}) collective-permute-start(bf16[512,384]{1,0:T(8,128)(2,1)S(1)} %slice.134), channel_id=1, source_target_pairs={{0,4},{4,0},{8,12},{12,8},{16,20},{20,16},{24,28},{28,24},{1,5},{5... | collective-permute-start | bytes 1179656 | tf_op jit(solution)/shard_map/ppermute | solution.py:218
  150.6 18.5 %collective-permute-start.19 = (bf16[512,1024]{1,0:T(8,128)(2,1)S(1)}, bf16[512,1024]{1,0:T(8,128)(2,1)S(1)}, u32[]{:S(2)}, u32[]{:S(2)}) collective-permute-start(bf16[512,1024]{1,0:T(8,128)(2,1)S(1)} %pad_maximum_fusion.9), channel_id=1, source_target_pairs={{0,8},{4,12},{8,0},{12,4},{16,24},{20,28},{24,16},{28,20},{1,9},{5... | collective-permute-start | bytes 3145736 | tf_op jit(solution)/shard_map/ppermute | solution.py:218
  155.3 23.9 %collective-permute-start.17 = (bf16[512,512]{1,0:T(8,128)(2,1)S(1)}, bf16[512,512]{1,0:T(8,128)(2,1)S(1)}, u32[]{:S(2)}, u32[]{:S(2)}) collective-permute-start(bf16[512,512]{1,0:T(8,128)(2,1)S(1)} %get-tuple-element.45), channel_id=1, source_target_pairs={{0,4},{4,0},{8,12},{12,8},{16,20},{20,16},{24,28},{28,24},{1,5},{5... | collective-permute-start | bytes 1572872 | tf_op jit(solution)/shard_map/ppermute | solution.py:218
  172.9 14.0 %collective-permute-start.20 = (bf16[512,512]{1,0:T(8,128)(2,1)S(1)}, bf16[512,512]{1,0:T(8,128)(2,1)S(1)}, u32[]{:S(2)}, u32[]{:S(2)}) collective-permute-start(bf16[512,512]{1,0:T(8,128)(2,1)S(1)} %get-tuple-element.50), channel_id=1, source_target_pairs={{0,4},{4,0},{8,12},{12,8},{16,20},{20,16},{24,28},{28,24},{1,5},{5... | collective-permute-start | bytes 1572872 | tf_op jit(solution)/shard_map/ppermute | solution.py:218
  174.7 7.4 %collective-permute-start.22 = (bf16[512,256]{1,0:T(8,128)(2,1)S(1)}, bf16[512,256]{1,0:T(8,128)(2,1)S(1)}, u32[]{:S(2)}, u32[]{:S(2)}) collective-permute-start(bf16[512,256]{1,0:T(8,128)(2,1)S(1)} %pad_maximum_fusion.13), channel_id=1, source_target_pairs={{0,8},{4,12},{8,0},{12,4},{16,24},{20,28},{24,16},{28,20},{1,9},{5... | collective-permute-start | bytes 786440 | tf_op jit(solution)/shard_map/ppermute | solution.py:218
  185.5 5.0 %collective-permute-start.23 = (bf16[512,128]{1,0:T(8,128)(2,1)S(1)}, bf16[512,128]{1,0:T(8,128)(2,1)S(1)}, u32[]{:S(2)}, u32[]{:S(2)}) collective-permute-start(bf16[512,128]{1,0:T(8,128)(2,1)S(1)} %get-tuple-element.56), channel_id=1, source_target_pairs={{0,4},{4,0},{8,12},{12,8},{16,20},{20,16},{24,28},{28,24},{1,5},{5... | collective-permute-start | bytes 393224 | tf_op jit(solution)/shard_map/ppermute | solution.py:218
  (37 other events, 278.6 us)

commit v5 on v4

--- a/solution.py
+++ b/solution.py
@@ -252,7 +252,7 @@
     twins = [(a, a ^ 1) for a in range(n_head)]
     share = rows // 2
     part = lax.dynamic_slice_in_dim(tokens, head % 2 * share, share, 0)
-    part = send(features(part, 1 - side), across)
+    part = send(features(after(part), 1 - side), across)
     twin = lax.ppermute(part, "head", twins)
     beside_tokens = jnp.concatenate(
         [jnp.where(even, part, twin), jnp.where(even, twin, part)], axis=0
@@ -290,7 +290,7 @@
     got[0] = (first, 0)
     go_round([0], None)
     arrived = lambda table, k: [p for p, _ in table.get(k, [])]
-    second = send(joined(owns[1:4]), swap)
+    second = send(joined([after(owns[1])] + owns[2:4]), swap)
     for k in range(1, min(4, count)):
         got[k] = (second, sum(wides[1:k]))
     go_round([], 0)

time: 194 us -> 183 us (0.943)
  starting transfers between devices: 42.3 us -> 33.2 us
  other arithmetic: 19.6 us -> 15.4 us
  waiting for transfers between devices: 74.1 us -> 76.8 us
    ppermute x21, starting transfers between devices: 38.7 us -> 29.6 us  [shards(): send = lambda value, moves: lax.ppermute(value, 'dp', moves)]
    ppermute x21, waiting for transfers between devices: 71.1 us -> 75.1 us  [shards(): send = lambda value, moves: lax.ppermute(value, 'dp', moves)]
    concatenate x9, other arithmetic: 9.39 us -> 7.41 us  [shards(): jnp.concatenate(blocks, axis=1)]
    unnamed x74 -> x82, local copies, waits for them, and re-layouts: 2.6 us -> 3.88 us
  transfers between devices with their start and end apart: 24 -> 24, of which waited for: 10 -> 9; matrix products, arithmetic and copies ran while one was open for 19% -> 18% of each run, Pallas kernels for 16% -> 17%
where the time goes in v5:
time: 183 us; the launch traced here: 182 us
  waiting for transfers between devices  76.8 us (42%)
  starting transfers between devices  33.2 us (18%)
  Pallas kernels  32.8 us (18%)
  local copies, waits for them, and re-layouts  23.2 us (13%)
  other arithmetic  15.4 us (8%)
    ppermute x21, waiting for transfers between devices, shards(): send = lambda value, moves: lax.ppermute(value, 'dp', moves)  75.1 us
    ppermute x21, starting transfers between devices, shards(): send = lambda value, moves: lax.ppermute(value, 'dp', moves)  29.6 us
    pallas_call x5, Pallas kernels, product(): pl.pallas_call(functools.partial(product_kernel, tuple(windows), count, s...  20.4 us
    pallas_call x5, Pallas kernels, attend(): pl.pallas_call(functools.partial(attend_kernel, block), grid=(cols // ste...  12.4 us
    concatenate x9, other arithmetic, shards(): jnp.concatenate(blocks, axis=1)  7.41 us
    slice x9, local copies, waits for them, and re-layouts, shards(): cut = lambda k, where: where[0][:, where[1]:where[1] + wides[k]]  3.98 us
    unnamed x82, local copies, waits for them, and re-layouts  3.88 us
  transfers between devices with their start and end apart: 24, of which 9 were waited for; matrix products, arithmetic and copies ran while one was open for 18% of the time, Pallas kernels for 17%

profile of v5, /device:TPU:0, one launch (start us, length us, event | category | flops | bytes accessed | tf_op | source)
XLA Modules:
  0.0 182.3 jit_solution(15722066581970068790)
XLA Ops:
  0.0 1.9 %slice.84.refs_2_ = bf16[512,512]{1,0:T(8,128)(2,1)} slice(bf16[512,2048]{1,0:T(8,128)(2,1)} %param.7), slice={[0:512], [0:512]} | slice | bytes 1048576 | tf_op jit(solution)/shard_map/slice | solution.py:250
  1.9 3.0 %collective-permute-start.2 = (bf16[512,512]{1,0:T(8,128)(2,1)}, bf16[512,512]{1,0:T(8,128)(2,1)S(1)}, u32[]{:S(2)}, u32[]{:S(2)}) collective-permute-start(bf16[512,512]{1,0:T(8,128)(2,1)} %slice.84.refs_2_), channel_id=1, source_target_pairs={{0,8},{4,12},{8,0},{12,4},{16,24},{20,28},{24,16},{28,20},{1,9},{5... | collective-permute-start | bytes 1572872 | tf_op jit(solution)/shard_map/ppermute | solution.py:218
  6.6 2.9 %collective-permute-start.6 = (bf16[512,128]{1,0:T(8,128)(2,1)S(1)}, bf16[512,128]{1,0:T(8,128)(2,1)S(1)}, u32[]{:S(2)}, u32[]{:S(2)}) collective-permute-start(bf16[512,128]{1,0:T(8,128)(2,1)S(1)} %get-tuple-element.78), channel_id=1, source_target_pairs={{0,1},{1,3},{2,0},{3,2},{4,5},{5,7},{6,4},{7,6},{8,9},{9,11},{10,8... | collective-permute-start | bytes 393224 | tf_op jit(solution)/shard_map/ppermute | solution.py:174
  13.8 3.3 %collective-permute-done.2.refs_3_ = bf16[512,512]{1,0:T(8,128)(2,1)S(1)} collective-permute-done((bf16[512,512]{1,0:T(8,128)(2,1)}, bf16[512,512]{1,0:T(8,128)(2,1)S(1)}, u32[]{:S(2)}, u32[]{:S(2)}) %collective-permute-start.2) | collective-permute-done | bytes 524320 | tf_op jit(solution)/shard_map/ppermute | solution.py:218
  18.4 1.7 collective-permute-start.7
  33.3 23.7 %collective-permute-done.7.refs_3_ = bf16[512,1664]{1,0:T(8,128)(2,1)S(1)} collective-permute-done((bf16[512,1664]{1,0:T(8,128)(2,1)}, bf16[512,1664]{1,0:T(8,128)(2,1)S(1)}, u32[]{:S(2)}, u32[]{:S(2)}) %collective-permute-start.7) | collective-permute-done | bytes 1703968 | tf_op jit(solution)/shard_map/ppermute | solution.py:218
  64.2 19.0 %collective-permute-done.8.refs_6_.refs_3_ = bf16[512,1152]{1,0:T(8,128)(2,1)S(1)} collective-permute-done((bf16[512,1152]{1,0:T(8,128)(2,1)S(1)}, bf16[512,1152]{1,0:T(8,128)(2,1)S(1)}, u32[]{:S(2)}, u32[]{:S(2)}) %collective-permute-start.8) | collective-permute-done | bytes 1179680 | tf_op jit(solution)/shard_map/ppermute | solution.py:218
  83.2 5.0 %collective-permute-start.12 = (bf16[512,1280]{1,0:T(8,128)(2,1)S(1)}, bf16[512,1280]{1,0:T(8,128)(2,1)S(1)}, u32[]{:S(2)}, u32[]{:S(2)}) collective-permute-start(bf16[512,1280]{1,0:T(8,128)(2,1)S(1)} %pad_maximum_fusion.3), channel_id=1, source_target_pairs={{0,8},{4,12},{8,0},{12,4},{16,24},{20,28},{24,16},{28,20},{1,9},{5... | collective-permute-start | bytes 3932168 | tf_op jit(solution)/shard_map/ppermute | solution.py:218
  92.0 4.0 %product.5 = (bf16[512,512]{1,0:T(8,128)(2,1)}, f32[512,512]{1,0:T(8,128)S(1)}) custom-call(s32[1]{0:T(128)} %bitcast.flag, bf16[512,2048]{1,0:T(8,128)(2,1)S(1)} %pad_maximum_fusion.refs_0_, bf16[512,2048]{1,0:T(8,128)(2,1)S(1)} %pad_maximum_fusion.1.refs_1_, bf16[512,512]{1,0:T(8,128)(2,1)} %slice.84.refs_2_, bf16[512,512]{1,0:T(8,128)(2,1)S(1)} %copy-done.26, ...), custom_call_target="tpu_custom_call" | custom-call | tf_op jit(solution)/shard_map/product/pallas_call | solution.py:149
  99.7 15.3 %collective-permute-done.12.refs_6_ = bf16[512,1280]{1,0:T(8,128)(2,1)S(1)} collective-permute-done((bf16[512,1280]{1,0:T(8,128)(2,1)S(1)}, bf16[512,1280]{1,0:T(8,128)(2,1)S(1)}, u32[]{:S(2)}, u32[]{:S(2)}) %collective-permute-start.12) | collective-permute-done | bytes 1310752 | tf_op jit(solution)/shard_map/ppermute | solution.py:218
  115.0 2.0 %collective-permute-start.16 = (bf16[512,1024]{1,0:T(8,128)(2,1)}, bf16[512,1024]{1,0:T(8,128)(2,1)}, u32[]{:S(2)}, u32[]{:S(2)}) collective-permute-start(bf16[512,1024]{1,0:T(8,128)(2,1)} %pad_maximum_fusion.8), channel_id=1, source_target_pairs={{0,8},{4,12},{8,0},{12,4},{16,24},{20,28},{24,16},{28,20},{1,9},{5... | collective-permute-start | bytes 3145736 | tf_op jit(solution)/shard_map/ppermute | solution.py:218
  117.0 5.5 %product.6 = (f32[512,640]{1,0:T(8,128)S(1)}, f32[512,640]{1,0:T(8,128)S(1)}) custom-call(s32[1]{0:T(128)} %bitcast.flag, bf16[512,2048]{1,0:T(8,128)(2,1)S(1)} %pad_maximum_fusion.refs_0_, bf16[512,2048]{1,0:T(8,128)(2,1)S(1)} %pad_maximum_fusion.1.refs_1_, bf16[512,640]{1,0:T(8,128)(2,1)S(1)} %copy-done.11, bf16[512,1664]{1,0:T(8,128)(2,1)S(1)} %copy-done.3, ...), custom_call_target="tpu_custom_call" | custom-call | tf_op jit(solution)/shard_map/product/pallas_call | solution.py:149
  124.0 1.8 fusion.2
  135.7 2.9 %collective-permute-done.13 = f32[512,256]{1,0:T(8,128)} collective-permute-done((f32[512,256]{1,0:T(8,128)}, f32[512,256]{1,0:T(8,128)}, u32[]{:S(2)}, u32[]{:S(2)}) %collective-permute-start.13) | collective-permute-done | bytes 524320 | tf_op jit(solution)/shard_map/ppermute | solution.py:218
  140.5 4.0 %product.7 = (bf16[512,512]{1,0:T(8,128)(2,1)S(1)}, f32[512,512]{1,0:T(8,128)S(1)}) custom-call(s32[1]{0:T(128)} %bitcast.flag, bf16[512,2048]{1,0:T(8,128)(2,1)S(1)} %copy-done.1, bf16[512,2048]{1,0:T(8,128)(2,1)S(1)} %pad_maximum_fusion.1.refs_1_, bf16[512,512]{1,0:T(8,128)(2,1)S(1)} %copy-done.17, bf16[512,1664]{1,0:T(8,128)(2,1)S(1)} %copy-done.4, ...), custom_call_target="tpu_custom_call" | custom-call | tf_op jit(solution)/shard_map/product/pallas_call | solution.py:149
  145.9 3.8 %collective-permute-done.9.other = bf16[512,512]{1,0:T(8,128)(2,1)S(1)} collective-permute-done((bf16[512,512]{1,0:T(8,128)(2,1)}, bf16[512,512]{1,0:T(8,128)(2,1)S(1)}, u32[]{:S(2)}, u32[]{:S(2)}) %collective-permute-start.9) | collective-permute-done | bytes 524320 | tf_op jit(solution)/shard_map/ppermute | solution.py:218
  149.8 2.9 %attend.5 = bf16[512,512]{1,0:T(8,128)(2,1)S(1)} custom-call(f32[512,512]{1,0:T(8,128)S(1)} %copy-done.23, bf16[512,512]{1,0:T(8,128)(2,1)S(1)} %collective-permute-done.9.other, bf16[512,256]{1,0:T(8,128)(2,1)S(1)} %pad_maximum_fusion.12.keys_values, f32[512,384]{1,0:T(8,128)S(1)} %concatenate.71.tables, f32[1,128]{1,0:T(1,128)S(1)} %bitcast.6), custom_call_target="tpu_custom_call" | custom-call | tf_op jit(solution)/shard_map/attend/pallas_call | solution.py:87
  152.7 6.3 %collective-permute-done.19.refs_6_ = bf16[512,1024]{1,0:T(8,128)(2,1)S(1)} collective-permute-done((bf16[512,1024]{1,0:T(8,128)(2,1)S(1)}, bf16[512,1024]{1,0:T(8,128)(2,1)S(1)}, u32[]{:S(2)}, u32[]{:S(2)}) %collective-permute-start.19) | collective-permute-done | bytes 1048608 | tf_op jit(solution)/shard_map/ppermute | solution.py:218
  158.9 3.9 %product.8 = (bf16[512,512]{1,0:T(8,128)(2,1)S(1)}, f32[512,512]{1,0:T(8,128)S(1)}) custom-call(s32[1]{0:T(128)} %bitcast.flag, bf16[512,2048]{1,0:T(8,128)(2,1)S(1)} %copy-done.1, bf16[512,2048]{1,0:T(8,128)(2,1)S(1)} %pad_maximum_fusion.1.refs_1_, bf16[512,512]{1,0:T(8,128)(2,1)S(1)} %copy-done.15, bf16[512,1664]{1,0:T(8,128)(2,1)S(1)} %copy-done.4, ...), custom_call_target="tpu_custom_call" | custom-call | tf_op jit(solution)/shard_map/product/pallas_call | solution.py:149
  164.9 1.8 %collective-permute-start.22 = (bf16[512,256]{1,0:T(8,128)(2,1)S(1)}, bf16[512,256]{1,0:T(8,128)(2,1)S(1)}, u32[]{:S(2)}, u32[]{:S(2)}) collective-permute-start(bf16[512,256]{1,0:T(8,128)(2,1)S(1)} %pad_maximum_fusion.13), channel_id=1, source_target_pairs={{0,8},{4,12},{8,0},{12,4},{16,24},{20,28},{24,16},{28,20},{1,9},{5... | collective-permute-start | bytes 786440 | tf_op jit(solution)/shard_map/ppermute | solution.py:218
  166.7 2.3 %attend.6 = bf16[512,384]{1,0:T(8,128)(2,1)S(1)} custom-call(f32[512,384]{1,0:T(8,128)S(1)} %slice.99.mine, bf16[512,384]{1,0:T(8,128)(2,1)S(1)} %collective-permute-done.14.other, bf16[512,256]{1,0:T(8,128)(2,1)S(1)} %pad_maximum_fusion.12.keys_values, f32[512,384]{1,0:T(8,128)S(1)} %concatenate.71.tables, f32[1,128]{1,0:T(1,128)S(1)} %bitcast.7), custom_call_target="tpu_custom_call" | custom-call | tf_op jit(solution)/shard_map/attend/pallas_call | solution.py:87
  169.2 2.9 %attend.7 = bf16[512,512]{1,0:T(8,128)(2,1)S(1)} custom-call(f32[512,512]{1,0:T(8,128)S(1)} %get-tuple-element.44.mine, bf16[512,512]{1,0:T(8,128)(2,1)S(1)} %collective-permute-done.17.other, bf16[512,256]{1,0:T(8,128)(2,1)S(1)} %pad_maximum_fusion.12.keys_values, f32[512,384]{1,0:T(8,128)S(1)} %concatenate.71.tables, f32[1,128]{1,0:T(1,128)S(1)} %bitcast.8), custom_call_target="tpu_custom_call" | custom-call | tf_op jit(solution)/shard_map/attend/pallas_call | solution.py:87
  172.1 3.0 %product.9 = (bf16[512,128]{1,0:T(8,128)(2,1)S(1)}, f32[512,128]{1,0:T(8,128)S(1)}) custom-call(s32[1]{0:T(128)} %bitcast.flag, bf16[512,2048]{1,0:T(8,128)(2,1)S(1)} %copy-done.1, bf16[512,2048]{1,0:T(8,128)(2,1)S(1)} %pad_maximum_fusion.1.refs_1_, bf16[512,128]{1,0:T(8,128)(2,1)S(1)} %slice.85.refs_2_, bf16[512,1152]{1,0:T(8,128)(2,1)S(1)} %copy-done.13, ...), custom_call_target="tpu_custom_call" | custom-call | tf_op jit(solution)/shard_map/product/pallas_call | solution.py:149
  176.4 2.9 %attend.8 = bf16[512,512]{1,0:T(8,128)(2,1)S(1)} custom-call(f32[512,512]{1,0:T(8,128)S(1)} %get-tuple-element.49.mine, bf16[512,512]{1,0:T(8,128)(2,1)S(1)} %collective-permute-done.20.other, bf16[512,256]{1,0:T(8,128)(2,1)S(1)} %pad_maximum_fusion.12.keys_values, f32[512,384]{1,0:T(8,128)S(1)} %concatenate.71.tables, f32[1,128]{1,0:T(1,128)S(1)} %bitcast.9), custom_call_target="tpu_custom_call" | custom-call | tf_op jit(solution)/shard_map/attend/pallas_call | solution.py:87
  (172 shorter events, 55.6 us)
Async XLA Ops:
  1.9 15.2 %collective-permute-start.2 = (bf16[512,512]{1,0:T(8,128)(2,1)}, bf16[512,512]{1,0:T(8,128)(2,1)S(1)}, u32[]{:S(2)}, u32[]{:S(2)}) collective-permute-start(bf16[512,512]{1,0:T(8,128)(2,1)} %slice.84.refs_2_), channel_id=1, source_target_pairs={{0,8},{4,12},{8,0},{12,4},{16,24},{20,28},{24,16},{28,20},{1,9},{5... | collective-permute-start | bytes 1572872 | tf_op jit(solution)/shard_map/ppermute | solution.py:218
  5.9 6.1 %collective-permute-start.5 = (bf16[512,128]{1,0:T(8,128)(2,1)S(1)}, bf16[512,128]{1,0:T(8,128)(2,1)S(1)}, u32[]{:S(2)}, u32[]{:S(2)}) collective-permute-start(bf16[512,128]{1,0:T(8,128)(2,1)S(1)} %get-tuple-element.77), channel_id=1, source_target_pairs={{0,0},{1,2},{2,1},{3,3},{4,4},{5,6},{6,5},{7,7},{8,8},{9,10},{10,9... | collective-permute-start | bytes 393224 | tf_op jit(solution)/shard_map/ppermute | solution.py:170
  6.6 7.1 %collective-permute-start.6 = (bf16[512,128]{1,0:T(8,128)(2,1)S(1)}, bf16[512,128]{1,0:T(8,128)(2,1)S(1)}, u32[]{:S(2)}, u32[]{:S(2)}) collective-permute-start(bf16[512,128]{1,0:T(8,128)(2,1)S(1)} %get-tuple-element.78), channel_id=1, source_target_pairs={{0,1},{1,3},{2,0},{3,2},{4,5},{5,7},{6,4},{7,6},{8,9},{9,11},{10,8... | collective-permute-start | bytes 393224 | tf_op jit(solution)/shard_map/ppermute | solution.py:174
  9.5 22.5 %collective-permute-start.3 = (bf16[512,512]{1,0:T(8,128)(2,1)}, bf16[512,512]{1,0:T(8,128)(2,1)}, u32[]{:S(2)}, u32[]{:S(2)}) collective-permute-start(bf16[512,512]{1,0:T(8,128)(2,1)} %slice.84.refs_2_), channel_id=1, source_target_pairs={{8,16},{12,20},{16,8},{20,12},{9,17},{13,21},{17,9},{21,13},{10,18... | collective-permute-start | bytes 1572872 | tf_op jit(solution)/shard_map/ppermute | solution.py:218
  18.4 38.6 %collective-permute-start.7 = (bf16[512,1664]{1,0:T(8,128)(2,1)}, bf16[512,1664]{1,0:T(8,128)(2,1)S(1)}, u32[]{:S(2)}, u32[]{:S(2)}) collective-permute-start(bf16[512,1664]{1,0:T(8,128)(2,1)} %pad_maximum_fusion.2), channel_id=1, source_target_pairs={{0,8},{4,12},{8,0},{12,4},{16,24},{20,28},{24,16},{28,20},{1,9},{5... | collective-permute-start | bytes 5111816 | tf_op jit(solution)/shard_map/ppermute | solution.py:218
  24.1 36.1 %collective-permute-start = (bf16[256,2048]{1,0:T(8,128)(2,1)}, bf16[256,2048]{1,0:T(8,128)(2,1)}, u32[]{:S(2)}, u32[]{:S(2)}) collective-permute-start(bf16[256,2048]{1,0:T(8,128)(2,1)} %pad_maximum_fusion.6), channel_id=1, source_target_pairs={{0,4},{4,0},{8,12},{12,8},{16,20},{20,16},{24,28},{28,24},{1,5},{5... | collective-permute-start | bytes 3145736 | tf_op jit(solution)/shard_map/ppermute | solution.py:218
  25.7 2.8 %collective-permute-start.4 = (bf16[512,512]{1,0:T(8,128)(2,1)S(1)}, bf16[512,512]{1,0:T(8,128)(2,1)S(1)}, u32[]{:S(2)}, u32[]{:S(2)}) collective-permute-start(bf16[512,512]{1,0:T(8,128)(2,1)S(1)} %collective-permute-done.2.refs_3_), channel_id=1, source_target_pairs={{8,16},{12,20},{16,8},{20,12},{9,17},{13,21},{17,9},{21,13},{10,18... | collective-permute-start | bytes 1572872 | tf_op jit(solution)/shard_map/ppermute | solution.py:218
  29.3 32.2 %collective-permute-start.10 = (bf16[512,1152]{1,0:T(8,128)(2,1)}, bf16[512,1152]{1,0:T(8,128)(2,1)S(1)}, u32[]{:S(2)}, u32[]{:S(2)}) collective-permute-start(bf16[512,1152]{1,0:T(8,128)(2,1)} %pad_maximum_fusion.5), channel_id=1, source_target_pairs={{8,16},{12,20},{16,8},{20,12},{9,17},{13,21},{17,9},{21,13},{10,18... | collective-permute-start | bytes 3538952 | tf_op jit(solution)/shard_map/ppermute | solution.py:218
  57.0 26.2 %collective-permute-start.8 = (bf16[512,1152]{1,0:T(8,128)(2,1)S(1)}, bf16[512,1152]{1,0:T(8,128)(2,1)S(1)}, u32[]{:S(2)}, u32[]{:S(2)}) collective-permute-start(bf16[512,1152]{1,0:T(8,128)(2,1)S(1)} %pad_maximum_fusion.4), channel_id=1, source_target_pairs={{0,8},{4,12},{8,0},{12,4},{16,24},{20,28},{24,16},{28,20},{1,9},{5... | collective-permute-start | bytes 3538952 | tf_op jit(solution)/shard_map/ppermute | solution.py:218
  60.2 28.1 %collective-permute-start.1 = (bf16[256,2048]{1,0:T(8,128)(2,1)}, bf16[256,2048]{1,0:T(8,128)(2,1)S(1)}, u32[]{:S(2)}, u32[]{:S(2)}) collective-permute-start(bf16[256,2048]{1,0:T(8,128)(2,1)} %collective-permute-done), channel_id=1, source_target_pairs={{0,1},{1,0},{2,3},{3,2},{4,5},{5,4},{6,7},{7,6},{8,9},{9,8},{10,11... | collective-permute-start | bytes 3145736 | tf_op jit(solution)/shard_map/ppermute | solution.py:256
  60.4 2.9 %collective-permute-start.11 = (bf16[512,640]{1,0:T(8,128)(2,1)S(1)}, bf16[512,640]{1,0:T(8,128)(2,1)S(1)}, u32[]{:S(2)}, u32[]{:S(2)}) collective-permute-start(bf16[512,640]{1,0:T(8,128)(2,1)S(1)} %slice.110), channel_id=1, source_target_pairs={{8,16},{12,20},{16,8},{20,12},{9,17},{13,21},{17,9},{21,13},{10,18... | collective-permute-start | bytes 1966088 | tf_op jit(solution)/shard_map/ppermute | solution.py:218
  63.4 32.6 %collective-permute-start.15 = (bf16[512,1024]{1,0:T(8,128)(2,1)S(1)}, bf16[512,1024]{1,0:T(8,128)(2,1)S(1)}, u32[]{:S(2)}, u32[]{:S(2)}) collective-permute-start(bf16[512,1024]{1,0:T(8,128)(2,1)S(1)} %pad_maximum_fusion.7), channel_id=1, source_target_pairs={{8,16},{12,20},{16,8},{20,12},{9,17},{13,21},{17,9},{21,13},{10,18... | collective-permute-start | bytes 3145736 | tf_op jit(solution)/shard_map/ppermute | solution.py:218
  83.2 31.7 %collective-permute-start.12 = (bf16[512,1280]{1,0:T(8,128)(2,1)S(1)}, bf16[512,1280]{1,0:T(8,128)(2,1)S(1)}, u32[]{:S(2)}, u32[]{:S(2)}) collective-permute-start(bf16[512,1280]{1,0:T(8,128)(2,1)S(1)} %pad_maximum_fusion.3), channel_id=1, source_target_pairs={{0,8},{4,12},{8,0},{12,4},{16,24},{20,28},{24,16},{28,20},{1,9},{5... | collective-permute-start | bytes 3932168 | tf_op jit(solution)/shard_map/ppermute | solution.py:218
  96.0 34.5 %collective-permute-start.18 = (bf16[512,640]{1,0:T(8,128)(2,1)}, bf16[512,640]{1,0:T(8,128)(2,1)}, u32[]{:S(2)}, u32[]{:S(2)}) collective-permute-start(bf16[512,640]{1,0:T(8,128)(2,1)} %pad_maximum_fusion.11), channel_id=1, source_target_pairs={{8,16},{12,20},{16,8},{20,12},{9,17},{13,21},{17,9},{21,13},{10,18... | collective-permute-start | bytes 1966088 | tf_op jit(solution)/shard_map/ppermute | solution.py:218
  115.0 24.9 %collective-permute-start.16 = (bf16[512,1024]{1,0:T(8,128)(2,1)}, bf16[512,1024]{1,0:T(8,128)(2,1)}, u32[]{:S(2)}, u32[]{:S(2)}) collective-permute-start(bf16[512,1024]{1,0:T(8,128)(2,1)} %pad_maximum_fusion.8), channel_id=1, source_target_pairs={{0,8},{4,12},{8,0},{12,4},{16,24},{20,28},{24,16},{28,20},{1,9},{5... | collective-permute-start | bytes 3145736 | tf_op jit(solution)/shard_map/ppermute | solution.py:218
  123.5 15.2 %collective-permute-start.13 = (f32[512,256]{1,0:T(8,128)}, f32[512,256]{1,0:T(8,128)}, u32[]{:S(2)}, u32[]{:S(2)}) collective-permute-start(f32[512,256]{1,0:T(8,128)} %slice.94), channel_id=1, source_target_pairs={{0,4},{4,0},{8,12},{12,8},{16,20},{20,16},{24,28},{28,24},{1,5},{5... | collective-permute-start | bytes 1572872 | tf_op jit(solution)/shard_map/ppermute | solution.py:218
  128.1 21.7 %collective-permute-start.9 = (bf16[512,512]{1,0:T(8,128)(2,1)}, bf16[512,512]{1,0:T(8,128)(2,1)S(1)}, u32[]{:S(2)}, u32[]{:S(2)}) collective-permute-start(bf16[512,512]{1,0:T(8,128)(2,1)} %get-tuple-element.35), channel_id=1, source_target_pairs={{0,4},{4,0},{8,12},{12,8},{16,20},{20,16},{24,28},{28,24},{1,5},{5... | collective-permute-start | bytes 1572872 | tf_op jit(solution)/shard_map/ppermute | solution.py:218
  130.5 34.3 %collective-permute-start.21 = (bf16[512,128]{1,0:T(8,128)(2,1)S(1)}, bf16[512,128]{1,0:T(8,128)(2,1)S(1)}, u32[]{:S(2)}, u32[]{:S(2)}) collective-permute-start(bf16[512,128]{1,0:T(8,128)(2,1)S(1)} %slice.123), channel_id=1, source_target_pairs={{8,16},{12,20},{16,8},{20,12},{9,17},{13,21},{17,9},{21,13},{10,18... | collective-permute-start | bytes 393224 | tf_op jit(solution)/shard_map/ppermute | solution.py:218
  135.1 31.6 %collective-permute-start.14 = (bf16[512,384]{1,0:T(8,128)(2,1)S(1)}, bf16[512,384]{1,0:T(8,128)(2,1)S(1)}, u32[]{:S(2)}, u32[]{:S(2)}) collective-permute-start(bf16[512,384]{1,0:T(8,128)(2,1)S(1)} %slice.134), channel_id=1, source_target_pairs={{0,4},{4,0},{8,12},{12,8},{16,20},{20,16},{24,28},{28,24},{1,5},{5... | collective-permute-start | bytes 1179656 | tf_op jit(solution)/shard_map/ppermute | solution.py:218
  139.9 19.0 %collective-permute-start.19 = (bf16[512,1024]{1,0:T(8,128)(2,1)S(1)}, bf16[512,1024]{1,0:T(8,128)(2,1)S(1)}, u32[]{:S(2)}, u32[]{:S(2)}) collective-permute-start(bf16[512,1024]{1,0:T(8,128)(2,1)S(1)} %pad_maximum_fusion.9), channel_id=1, source_target_pairs={{0,8},{4,12},{8,0},{12,4},{16,24},{20,28},{24,16},{28,20},{1,9},{5... | collective-permute-start | bytes 3145736 | tf_op jit(solution)/shard_map/ppermute | solution.py:218
  144.5 24.7 %collective-permute-start.17 = (bf16[512,512]{1,0:T(8,128)(2,1)S(1)}, bf16[512,512]{1,0:T(8,128)(2,1)S(1)}, u32[]{:S(2)}, u32[]{:S(2)}) collective-permute-start(bf16[512,512]{1,0:T(8,128)(2,1)S(1)} %get-tuple-element.45), channel_id=1, source_target_pairs={{0,4},{4,0},{8,12},{12,8},{16,20},{20,16},{24,28},{28,24},{1,5},{5... | collective-permute-start | bytes 1572872 | tf_op jit(solution)/shard_map/ppermute | solution.py:218
  162.9 13.5 %collective-permute-start.20 = (bf16[512,512]{1,0:T(8,128)(2,1)S(1)}, bf16[512,512]{1,0:T(8,128)(2,1)S(1)}, u32[]{:S(2)}, u32[]{:S(2)}) collective-permute-start(bf16[512,512]{1,0:T(8,128)(2,1)S(1)} %get-tuple-element.50), channel_id=1, source_target_pairs={{0,4},{4,0},{8,12},{12,8},{16,20},{20,16},{24,28},{28,24},{1,5},{5... | collective-permute-start | bytes 1572872 | tf_op jit(solution)/shard_map/ppermute | solution.py:218
  164.9 7.2 %collective-permute-start.22 = (bf16[512,256]{1,0:T(8,128)(2,1)S(1)}, bf16[512,256]{1,0:T(8,128)(2,1)S(1)}, u32[]{:S(2)}, u32[]{:S(2)}) collective-permute-start(bf16[512,256]{1,0:T(8,128)(2,1)S(1)} %pad_maximum_fusion.13), channel_id=1, source_target_pairs={{0,8},{4,12},{8,0},{12,4},{16,24},{20,28},{24,16},{28,20},{1,9},{5... | collective-permute-start | bytes 786440 | tf_op jit(solution)/shard_map/ppermute | solution.py:218
  175.2 5.0 %collective-permute-start.23 = (bf16[512,128]{1,0:T(8,128)(2,1)S(1)}, bf16[512,128]{1,0:T(8,128)(2,1)S(1)}, u32[]{:S(2)}, u32[]{:S(2)}) collective-permute-start(bf16[512,128]{1,0:T(8,128)(2,1)S(1)} %get-tuple-element.56), channel_id=1, source_target_pairs={{0,4},{4,0},{8,12},{12,8},{16,20},{20,16},{24,28},{28,24},{1,5},{5... | collective-permute-start | bytes 393224 | tf_op jit(solution)/shard_map/ppermute | solution.py:218
  (41 other events, 273.6 us)

commit v6 on v5

--- a/solution.py
+++ b/solution.py
@@ -90,14 +90,16 @@
         out_shape=jax.ShapeDtypeStruct((rows, cols), jnp.bfloat16),
         in_specs=[by_heads, by_heads] + [whole(a) for a in (keys_values, tables, gain)],
         out_specs=by_heads,
-        compiler_params=pltpu.CompilerParams(vmem_limit_bytes=24 << 20),
+        compiler_params=pltpu.CompilerParams(vmem_limit_bytes=16 << 20),
         cost_estimate=pl.CostEstimate(flops=0, bytes_accessed=0, transcendentals=0),
         name="attend",
     )(mine, other, keys_values, tables, gain)
 
 
-def product_kernel(windows, count, sides, flag, *refs):
+def product_kernel(windows, count, sides, base, flag, *refs):
     tokens, arrays, outs = refs[:sides], refs[sides : -sides - 3], refs[-sides - 3 : -3]
+    n_arrays = max(at for at, _ in windows) + 1
+    arrays, so_far = arrays[:n_arrays], arrays[n_arrays:]
     features, weights, arrived = refs[-3:]
     depth, cols = weights.shape[1:]
     rows = tokens[0].shape[0]
@@ -111,7 +113,7 @@
 
     def features_of(side, i):
         return pltpu.make_async_copy(
-            tokens[side].at[:, pl.ds(i * depth, depth)], features.at[side, i], arrived.at[side, i]
+            tokens[side].at[:, pl.ds((base + i) * depth, depth)], features.at[side, i], arrived.at[side, i]
         )
 
     def start_all(which):
@@ -125,7 +127,7 @@
     for side in range(sides):
         for r in range(0, rows, block):
             here = pl.ds(r, block)
-            total = jnp.zeros((block, cols), jnp.float32)
+            total = so_far[side][here, :] if so_far else jnp.zeros((block, cols), jnp.float32)
             for i in range(count):
                 if r == 0:
                     features_of(side, i).wait()
@@ -137,7 +139,7 @@
             outs[side][here, :] = total.astype(outs[side].dtype)
 
 
-def product(is_hub, tokens, cols, at_hub, at_leaf, dtypes):
+def product(is_hub, tokens, cols, at_hub, at_leaf, dtypes, base=0, so_far=()):
     (rows, width), depth, sides = tokens[0].shape, at_hub[0][0].shape[0], len(tokens)
     count = len(at_hub)
     arrays, windows = [], []
@@ -147,20 +149,21 @@
             arrays.append(array)
         windows.append((known[0] if known else len(arrays) - 1, low))
     return pl.pallas_call(
-        functools.partial(product_kernel, tuple(windows), count, sides),
+        functools.partial(product_kernel, tuple(windows), count, sides, base),
         out_shape=[jax.ShapeDtypeStruct((rows, cols), dtype) for dtype in dtypes],
         in_specs=[pl.BlockSpec(memory_space=pltpu.SMEM)]
-        + [pl.BlockSpec(memory_space=pl.ANY)] * (sides + len(arrays)),
+        + [pl.BlockSpec(memory_space=pl.ANY)] * (sides + len(arrays))
+        + [pl.BlockSpec(memory_space=pltpu.VMEM)] * len(so_far),
         out_specs=[pl.BlockSpec(memory_space=pltpu.VMEM)] * sides,
         scratch_shapes=[
             pltpu.VMEM((sides, count, rows, depth), jnp.bfloat16),
             pltpu.VMEM((count, depth, cols), jnp.bfloat16),
             pltpu.SemaphoreType.DMA((sides + 1, count)),
         ],
-        compiler_params=pltpu.CompilerParams(vmem_limit_bytes=20 << 20),
-        cost_estimate=pl.CostEstimate(flops=0, bytes_accessed=0, transcendentals=0),
+        compiler_params=pltpu.CompilerParams(vmem_limit_bytes=16 << 20),
+        cost_estimate=pl.CostEstimate(flops=2 * rows * cols * width, bytes_accessed=0, transcendentals=0),
         name="product",
-    )(is_hub.astype(jnp.int32)[None], *tokens, *arrays)
+    )(is_hub.astype(jnp.int32)[None], *tokens, *arrays, *so_far)
 
 
 def kv_columns(kv_weight, head, n_head):
@@ -213,7 +216,6 @@
         return [(2 * a + s, 2 * b + s) for a, b in moves for s in range(2)]
 
     swap = on_line([(a, a ^ 1) for a in range(n_line)])
-    outward = on_line([(hub_of(g), hub_of(g) ^ 1) for g in range(n_pairs)])
     across = [(a, a ^ 1) for a in range(n_dp)]
     send = lambda value, moves: lax.ppermute(value, "dp", moves)
 
@@ -222,9 +224,6 @@
             send(part, on_line([(hub_of(g), hub_of((g + s) % n_pairs)) for g in range(n_pairs)]))
             for s in range(1, n_pairs)
         ]
-
-    def to_leaf(parts):
-        return [send(part, outward) for part in parts]
 
     def woven(own, partners, hubs, leaves):
         return [own, partners] + [p for two in zip(hubs, leaves, strict=True) for p in two]
@@ -315,9 +314,19 @@
         at_leaf += [(passed, low + i * wide) for i in range(2 * (n_pairs - 1))]
         pieces = woven((owns[k], 0), got[k], hub_at[k], leaf_at[k]), at_leaf
         done = parts[: max(0, k - 2 + (k + 1 == count))][-2:]
+        base, before = 0, computed[-1:] + done
+        if k == count - 2:
+            early = product(
+                is_hub, (after(beside_tokens, *before), own_tokens), wides[-1],
+                *[[(owns[-1], 0), got[count - 1]]] * 2, (jnp.float32, jnp.float32),
+            )
+            before = early[1:]
+        if k == count - 1:
+            base, pieces = 2, [p[2:] for p in pieces]
         theirs, mine = product(
-            is_hub, (after(beside_tokens, *computed[-1:], *done), own_tokens), wide, *pieces,
-            (jnp.float32 if k == with_kv else jnp.bfloat16, jnp.float32),
+            is_hub, (after(beside_tokens, *before), own_tokens), wide, *pieces,
+            (jnp.float32 if k == with_kv else jnp.bfloat16, jnp.float32), base,
+            early if base else (),
         )
         if k == with_kv:
             other_kv = send(theirs[:, widths[k] :], across)

time: 183 us -> 181 us (0.989)
  waiting for transfers between devices: 76.8 us -> 73.5 us
    ppermute x21, waiting for transfers between devices: 75.1 us -> 71.9 us  [shards(): send = lambda value, moves: lax.ppermute(value, 'dp', moves)]
    pallas_call x5 -> x6, Pallas kernels: 20.4 us -> 20.4 us  [product(): pl.pallas_call(functools.partial(product_kernel, tuple(windows), count, s...]
    unnamed x82 -> x80, local copies, waits for them, and re-layouts: 3.88 us -> 3.89 us
  transfers between devices with their start and end apart: 24 -> 24, of which waited for: 9 -> 9; matrix products, arithmetic and copies ran while one was open for 18% -> 19% of each run, Pallas kernels for 17% -> 17%
where the time goes in v6:
time: 181 us; the launch traced here: 180 us
  waiting for transfers between devices  73.5 us (41%)
  starting transfers between devices  33.3 us (18%)
  Pallas kernels  32.8 us (18%)
  local copies, waits for them, and re-layouts  23.2 us (13%)
  other arithmetic  16.7 us (9%)
    ppermute x21, waiting for transfers between devices, shards(): send = lambda value, moves: lax.ppermute(value, 'dp', moves)  71.9 us
    ppermute x21, starting transfers between devices, shards(): send = lambda value, moves: lax.ppermute(value, 'dp', moves)  29.7 us
    pallas_call x6, Pallas kernels, product(): pl.pallas_call(functools.partial(product_kernel, tuple(windows), count, s...  20.4 us
    pallas_call x5, Pallas kernels, attend(): pl.pallas_call(functools.partial(attend_kernel, block), grid=(cols // ste...  12.4 us
    concatenate x9, other arithmetic, shards(): jnp.concatenate(blocks, axis=1)  7.32 us
    slice x9, local copies, waits for them, and re-layouts, shards(): cut = lambda k, where: where[0][:, where[1]:where[1] + wides[k]]  3.99 us
    unnamed x80, local copies, waits for them, and re-layouts  3.89 us
  transfers between devices with their start and end apart: 24, of which 9 were waited for; matrix products, arithmetic and copies ran while one was open for 19% of the time, Pallas kernels for 17%

profile of v6, /device:TPU:0, one launch (start us, length us, event | category | flops | bytes accessed | tf_op | source)
XLA Modules:
  0.0 180.4 jit_solution(17246277519068961469)
XLA Ops:
  0.0 1.9 %slice.84.refs_2_ = bf16[512,512]{1,0:T(8,128)(2,1)} slice(bf16[512,2048]{1,0:T(8,128)(2,1)} %param.7), slice={[0:512], [0:512]} | slice | bytes 1048576 | tf_op jit(solution)/shard_map/slice | solution.py:249
  1.9 3.0 %collective-permute-start.2 = (bf16[512,512]{1,0:T(8,128)(2,1)}, bf16[512,512]{1,0:T(8,128)(2,1)S(1)}, u32[]{:S(2)}, u32[]{:S(2)}) collective-permute-start(bf16[512,512]{1,0:T(8,128)(2,1)} %slice.84.refs_2_), channel_id=1, source_target_pairs={{0,8},{4,12},{8,0},{12,4},{16,24},{20,28},{24,16},{28,20},{1,9},{5... | collective-permute-start | bytes 1572872 | tf_op jit(solution)/shard_map/ppermute | solution.py:220
  6.6 2.9 %collective-permute-start.6 = (bf16[512,128]{1,0:T(8,128)(2,1)S(1)}, bf16[512,128]{1,0:T(8,128)(2,1)S(1)}, u32[]{:S(2)}, u32[]{:S(2)}) collective-permute-start(bf16[512,128]{1,0:T(8,128)(2,1)S(1)} %get-tuple-element.84), channel_id=1, source_target_pairs={{0,1},{1,3},{2,0},{3,2},{4,5},{5,7},{6,4},{7,6},{8,9},{9,11},{10,8... | collective-permute-start | bytes 393224 | tf_op jit(solution)/shard_map/ppermute | solution.py:177
  13.8 3.3 %collective-permute-done.2.refs_3_ = bf16[512,512]{1,0:T(8,128)(2,1)S(1)} collective-permute-done((bf16[512,512]{1,0:T(8,128)(2,1)}, bf16[512,512]{1,0:T(8,128)(2,1)S(1)}, u32[]{:S(2)}, u32[]{:S(2)}) %collective-permute-start.2) | collective-permute-done | bytes 524320 | tf_op jit(solution)/shard_map/ppermute | solution.py:220
  18.4 1.7 collective-permute-start.7
  33.3 23.7 %collective-permute-done.7.refs_3_ = bf16[512,1664]{1,0:T(8,128)(2,1)S(1)} collective-permute-done((bf16[512,1664]{1,0:T(8,128)(2,1)}, bf16[512,1664]{1,0:T(8,128)(2,1)S(1)}, u32[]{:S(2)}, u32[]{:S(2)}) %collective-permute-start.7) | collective-permute-done | bytes 1703968 | tf_op jit(solution)/shard_map/ppermute | solution.py:220
  58.5 1.7 constant_dynamic-slice_fusion.4
  64.2 19.0 %collective-permute-done.8.refs_6_.refs_3_ = bf16[512,1152]{1,0:T(8,128)(2,1)S(1)} collective-permute-done((bf16[512,1152]{1,0:T(8,128)(2,1)S(1)}, bf16[512,1152]{1,0:T(8,128)(2,1)S(1)}, u32[]{:S(2)}, u32[]{:S(2)}) %collective-permute-start.8) | collective-permute-done | bytes 1179680 | tf_op jit(solution)/shard_map/ppermute | solution.py:220
  83.2 5.0 %collective-permute-start.12 = (bf16[512,1280]{1,0:T(8,128)(2,1)S(1)}, bf16[512,1280]{1,0:T(8,128)(2,1)S(1)}, u32[]{:S(2)}, u32[]{:S(2)}) collective-permute-start(bf16[512,1280]{1,0:T(8,128)(2,1)S(1)} %pad_maximum_fusion.3), channel_id=1, source_target_pairs={{0,8},{4,12},{8,0},{12,4},{16,24},{20,28},{24,16},{28,20},{1,9},{5... | collective-permute-start | bytes 3932168 | tf_op jit(solution)/shard_map/ppermute | solution.py:220
  92.0 4.0 %product.6 = (bf16[512,512]{1,0:T(8,128)(2,1)}, f32[512,512]{1,0:T(8,128)S(1)}) custom-call(s32[1]{0:T(128)} %bitcast.flag, bf16[512,2048]{1,0:T(8,128)(2,1)S(1)} %pad_maximum_fusion.refs_0_, bf16[512,2048]{1,0:T(8,128)(2,1)S(1)} %pad_maximum_fusion.1.refs_1_, bf16[512,512]{1,0:T(8,128)(2,1)} %slice.84.refs_2_, bf16[512,512]{1,0:T(8,128)(2,1)S(1)} %copy-done.26, ...), custom_call_target="tpu_custom_call" | custom-call | flops 1073741824 | tf_op jit(solution)/shard_map/product/pallas_call | solution.py:151
  99.7 15.3 %collective-permute-done.12.refs_6_ = bf16[512,1280]{1,0:T(8,128)(2,1)S(1)} collective-permute-done((bf16[512,1280]{1,0:T(8,128)(2,1)S(1)}, bf16[512,1280]{1,0:T(8,128)(2,1)S(1)}, u32[]{:S(2)}, u32[]{:S(2)}) %collective-permute-start.12) | collective-permute-done | bytes 1310752 | tf_op jit(solution)/shard_map/ppermute | solution.py:220
  115.0 2.0 %collective-permute-start.16 = (bf16[512,1024]{1,0:T(8,128)(2,1)}, bf16[512,1024]{1,0:T(8,128)(2,1)}, u32[]{:S(2)}, u32[]{:S(2)}) collective-permute-start(bf16[512,1024]{1,0:T(8,128)(2,1)} %pad_maximum_fusion.8), channel_id=1, source_target_pairs={{0,8},{4,12},{8,0},{12,4},{16,24},{20,28},{24,16},{28,20},{1,9},{5... | collective-permute-start | bytes 3145736 | tf_op jit(solution)/shard_map/ppermute | solution.py:220
  117.0 5.5 %product.7 = (f32[512,640]{1,0:T(8,128)S(1)}, f32[512,640]{1,0:T(8,128)S(1)}) custom-call(s32[1]{0:T(128)} %bitcast.flag, bf16[512,2048]{1,0:T(8,128)(2,1)S(1)} %pad_maximum_fusion.refs_0_, bf16[512,2048]{1,0:T(8,128)(2,1)S(1)} %pad_maximum_fusion.1.refs_1_, bf16[512,640]{1,0:T(8,128)(2,1)S(1)} %copy-done.11, bf16[512,1664]{1,0:T(8,128)(2,1)S(1)} %copy-done.3, ...), custom_call_target="tpu_custom_call" | custom-call | flops 1342177280 | tf_op jit(solution)/shard_map/product/pallas_call | solution.py:151
  124.0 1.8 fusion.2
  136.7 2.0 %collective-permute-done.13 = f32[512,256]{1,0:T(8,128)} collective-permute-done((f32[512,256]{1,0:T(8,128)}, f32[512,256]{1,0:T(8,128)}, u32[]{:S(2)}, u32[]{:S(2)}) %collective-permute-start.13) | collective-permute-done | bytes 524320 | tf_op jit(solution)/shard_map/ppermute | solution.py:220
  142.3 4.0 %product.8 = (bf16[512,512]{1,0:T(8,128)(2,1)S(1)}, f32[512,512]{1,0:T(8,128)S(1)}) custom-call(s32[1]{0:T(128)} %bitcast.flag, bf16[512,2048]{1,0:T(8,128)(2,1)S(1)} %copy-done.1, bf16[512,2048]{1,0:T(8,128)(2,1)S(1)} %pad_maximum_fusion.1.refs_1_, bf16[512,512]{1,0:T(8,128)(2,1)S(1)} %copy-done.17, bf16[512,1664]{1,0:T(8,128)(2,1)S(1)} %copy-done.4, ...), custom_call_target="tpu_custom_call" | custom-call | flops 1073741824 | tf_op jit(solution)/shard_map/product/pallas_call | solution.py:151
  147.3 2.5 %collective-permute-done.9.other = bf16[512,512]{1,0:T(8,128)(2,1)S(1)} collective-permute-done((bf16[512,512]{1,0:T(8,128)(2,1)}, bf16[512,512]{1,0:T(8,128)(2,1)S(1)}, u32[]{:S(2)}, u32[]{:S(2)}) %collective-permute-start.9) | collective-permute-done | bytes 524320 | tf_op jit(solution)/shard_map/ppermute | solution.py:220
  149.8 2.9 %attend.5 = bf16[512,512]{1,0:T(8,128)(2,1)S(1)} custom-call(f32[512,512]{1,0:T(8,128)S(1)} %copy-done.23, bf16[512,512]{1,0:T(8,128)(2,1)S(1)} %collective-permute-done.9.other, bf16[512,256]{1,0:T(8,128)(2,1)S(1)} %pad_maximum_fusion.12.keys_values, f32[512,384]{1,0:T(8,128)S(1)} %concatenate.71.tables, f32[1,128]{1,0:T(1,128)S(1)} %bitcast.6), custom_call_target="tpu_custom_call" | custom-call | tf_op jit(solution)/shard_map/attend/pallas_call | solution.py:87
  154.2 4.8 %collective-permute-done.19.refs_6_ = bf16[512,1024]{1,0:T(8,128)(2,1)S(1)} collective-permute-done((bf16[512,1024]{1,0:T(8,128)(2,1)S(1)}, bf16[512,1024]{1,0:T(8,128)(2,1)S(1)}, u32[]{:S(2)}, u32[]{:S(2)}) %collective-permute-start.19) | collective-permute-done | bytes 1048608 | tf_op jit(solution)/shard_map/ppermute | solution.py:220
  158.9 3.9 %product.10 = (bf16[512,512]{1,0:T(8,128)(2,1)S(1)}, f32[512,512]{1,0:T(8,128)S(1)}) custom-call(s32[1]{0:T(128)} %bitcast.flag, bf16[512,2048]{1,0:T(8,128)(2,1)S(1)} %copy-done.1, bf16[512,2048]{1,0:T(8,128)(2,1)S(1)} %pad_maximum_fusion.1.refs_1_, bf16[512,512]{1,0:T(8,128)(2,1)S(1)} %copy-done.15, bf16[512,1664]{1,0:T(8,128)(2,1)S(1)} %copy-done.4, ...), custom_call_target="tpu_custom_call" | custom-call | flops 1073741824 | tf_op jit(solution)/shard_map/product/pallas_call | solution.py:151
  163.9 1.8 %collective-permute-start.22 = (bf16[512,256]{1,0:T(8,128)(2,1)S(1)}, bf16[512,256]{1,0:T(8,128)(2,1)S(1)}, u32[]{:S(2)}, u32[]{:S(2)}) collective-permute-start(bf16[512,256]{1,0:T(8,128)(2,1)S(1)} %pad_maximum_fusion.13), channel_id=1, source_target_pairs={{0,8},{4,12},{8,0},{12,4},{16,24},{20,28},{24,16},{28,20},{1,9},{5... | collective-permute-start | bytes 786440 | tf_op jit(solution)/shard_map/ppermute | solution.py:220
  165.8 2.3 %attend.6 = bf16[512,384]{1,0:T(8,128)(2,1)S(1)} custom-call(f32[512,384]{1,0:T(8,128)S(1)} %slice.99.mine, bf16[512,384]{1,0:T(8,128)(2,1)S(1)} %collective-permute-done.14.other, bf16[512,256]{1,0:T(8,128)(2,1)S(1)} %pad_maximum_fusion.12.keys_values, f32[512,384]{1,0:T(8,128)S(1)} %concatenate.71.tables, f32[1,128]{1,0:T(1,128)S(1)} %bitcast.7), custom_call_target="tpu_custom_call" | custom-call | tf_op jit(solution)/shard_map/attend/pallas_call | solution.py:87
  168.3 2.9 %attend.7 = bf16[512,512]{1,0:T(8,128)(2,1)S(1)} custom-call(f32[512,512]{1,0:T(8,128)S(1)} %get-tuple-element.47.mine, bf16[512,512]{1,0:T(8,128)(2,1)S(1)} %collective-permute-done.17.other, bf16[512,256]{1,0:T(8,128)(2,1)S(1)} %pad_maximum_fusion.12.keys_values, f32[512,384]{1,0:T(8,128)S(1)} %concatenate.71.tables, f32[1,128]{1,0:T(1,128)S(1)} %bitcast.8), custom_call_target="tpu_custom_call" | custom-call | tf_op jit(solution)/shard_map/attend/pallas_call | solution.py:87
  175.3 2.9 %attend.8 = bf16[512,512]{1,0:T(8,128)(2,1)S(1)} custom-call(f32[512,512]{1,0:T(8,128)S(1)} %get-tuple-element.54.mine, bf16[512,512]{1,0:T(8,128)(2,1)S(1)} %collective-permute-done.20.other, bf16[512,256]{1,0:T(8,128)(2,1)S(1)} %pad_maximum_fusion.12.keys_values, f32[512,384]{1,0:T(8,128)S(1)} %concatenate.71.tables, f32[1,128]{1,0:T(1,128)S(1)} %bitcast.9), custom_call_target="tpu_custom_call" | custom-call | tf_op jit(solution)/shard_map/attend/pallas_call | solution.py:87
  (171 shorter events, 58.8 us)
Async XLA Ops:
  1.9 15.2 %collective-permute-start.2 = (bf16[512,512]{1,0:T(8,128)(2,1)}, bf16[512,512]{1,0:T(8,128)(2,1)S(1)}, u32[]{:S(2)}, u32[]{:S(2)}) collective-permute-start(bf16[512,512]{1,0:T(8,128)(2,1)} %slice.84.refs_2_), channel_id=1, source_target_pairs={{0,8},{4,12},{8,0},{12,4},{16,24},{20,28},{24,16},{28,20},{1,9},{5... | collective-permute-start | bytes 1572872 | tf_op jit(solution)/shard_map/ppermute | solution.py:220
  5.9 6.1 %collective-permute-start.5 = (bf16[512,128]{1,0:T(8,128)(2,1)S(1)}, bf16[512,128]{1,0:T(8,128)(2,1)S(1)}, u32[]{:S(2)}, u32[]{:S(2)}) collective-permute-start(bf16[512,128]{1,0:T(8,128)(2,1)S(1)} %get-tuple-element.83), channel_id=1, source_target_pairs={{0,0},{1,2},{2,1},{3,3},{4,4},{5,6},{6,5},{7,7},{8,8},{9,10},{10,9... | collective-permute-start | bytes 393224 | tf_op jit(solution)/shard_map/ppermute | solution.py:173
  6.6 7.1 %collective-permute-start.6 = (bf16[512,128]{1,0:T(8,128)(2,1)S(1)}, bf16[512,128]{1,0:T(8,128)(2,1)S(1)}, u32[]{:S(2)}, u32[]{:S(2)}) collective-permute-start(bf16[512,128]{1,0:T(8,128)(2,1)S(1)} %get-tuple-element.84), channel_id=1, source_target_pairs={{0,1},{1,3},{2,0},{3,2},{4,5},{5,7},{6,4},{7,6},{8,9},{9,11},{10,8... | collective-permute-start | bytes 393224 | tf_op jit(solution)/shard_map/ppermute | solution.py:177
  9.5 22.5 %collective-permute-start.3 = (bf16[512,512]{1,0:T(8,128)(2,1)}, bf16[512,512]{1,0:T(8,128)(2,1)}, u32[]{:S(2)}, u32[]{:S(2)}) collective-permute-start(bf16[512,512]{1,0:T(8,128)(2,1)} %slice.84.refs_2_), channel_id=1, source_target_pairs={{8,16},{12,20},{16,8},{20,12},{9,17},{13,21},{17,9},{21,13},{10,18... | collective-permute-start | bytes 1572872 | tf_op jit(solution)/shard_map/ppermute | solution.py:220
  18.4 38.6 %collective-permute-start.7 = (bf16[512,1664]{1,0:T(8,128)(2,1)}, bf16[512,1664]{1,0:T(8,128)(2,1)S(1)}, u32[]{:S(2)}, u32[]{:S(2)}) collective-permute-start(bf16[512,1664]{1,0:T(8,128)(2,1)} %pad_maximum_fusion.2), channel_id=1, source_target_pairs={{0,8},{4,12},{8,0},{12,4},{16,24},{20,28},{24,16},{28,20},{1,9},{5... | collective-permute-start | bytes 5111816 | tf_op jit(solution)/shard_map/ppermute | solution.py:220
  24.1 36.1 %collective-permute-start = (bf16[256,2048]{1,0:T(8,128)(2,1)}, bf16[256,2048]{1,0:T(8,128)(2,1)}, u32[]{:S(2)}, u32[]{:S(2)}) collective-permute-start(bf16[256,2048]{1,0:T(8,128)(2,1)} %pad_maximum_fusion.6), channel_id=1, source_target_pairs={{0,4},{4,0},{8,12},{12,8},{16,20},{20,16},{24,28},{28,24},{1,5},{5... | collective-permute-start | bytes 3145736 | tf_op jit(solution)/shard_map/ppermute | solution.py:220
  25.7 2.8 %collective-permute-start.4 = (bf16[512,512]{1,0:T(8,128)(2,1)S(1)}, bf16[512,512]{1,0:T(8,128)(2,1)S(1)}, u32[]{:S(2)}, u32[]{:S(2)}) collective-permute-start(bf16[512,512]{1,0:T(8,128)(2,1)S(1)} %collective-permute-done.2.refs_3_), channel_id=1, source_target_pairs={{8,16},{12,20},{16,8},{20,12},{9,17},{13,21},{17,9},{21,13},{10,18... | collective-permute-start | bytes 1572872 | tf_op jit(solution)/shard_map/ppermute | solution.py:220
  29.3 32.2 %collective-permute-start.10 = (bf16[512,1152]{1,0:T(8,128)(2,1)}, bf16[512,1152]{1,0:T(8,128)(2,1)S(1)}, u32[]{:S(2)}, u32[]{:S(2)}) collective-permute-start(bf16[512,1152]{1,0:T(8,128)(2,1)} %pad_maximum_fusion.5), channel_id=1, source_target_pairs={{8,16},{12,20},{16,8},{20,12},{9,17},{13,21},{17,9},{21,13},{10,18... | collective-permute-start | bytes 3538952 | tf_op jit(solution)/shard_map/ppermute | solution.py:220
  57.0 26.2 %collective-permute-start.8 = (bf16[512,1152]{1,0:T(8,128)(2,1)S(1)}, bf16[512,1152]{1,0:T(8,128)(2,1)S(1)}, u32[]{:S(2)}, u32[]{:S(2)}) collective-permute-start(bf16[512,1152]{1,0:T(8,128)(2,1)S(1)} %pad_maximum_fusion.4), channel_id=1, source_target_pairs={{0,8},{4,12},{8,0},{12,4},{16,24},{20,28},{24,16},{28,20},{1,9},{5... | collective-permute-start | bytes 3538952 | tf_op jit(solution)/shard_map/ppermute | solution.py:220
  60.2 28.1 %collective-permute-start.1 = (bf16[256,2048]{1,0:T(8,128)(2,1)}, bf16[256,2048]{1,0:T(8,128)(2,1)S(1)}, u32[]{:S(2)}, u32[]{:S(2)}) collective-permute-start(bf16[256,2048]{1,0:T(8,128)(2,1)} %collective-permute-done), channel_id=1, source_target_pairs={{0,1},{1,0},{2,3},{3,2},{4,5},{5,4},{6,7},{7,6},{8,9},{9,8},{10,11... | collective-permute-start | bytes 3145736 | tf_op jit(solution)/shard_map/ppermute | solution.py:255
  60.4 2.9 %collective-permute-start.11 = (bf16[512,640]{1,0:T(8,128)(2,1)S(1)}, bf16[512,640]{1,0:T(8,128)(2,1)S(1)}, u32[]{:S(2)}, u32[]{:S(2)}) collective-permute-start(bf16[512,640]{1,0:T(8,128)(2,1)S(1)} %slice.110), channel_id=1, source_target_pairs={{8,16},{12,20},{16,8},{20,12},{9,17},{13,21},{17,9},{21,13},{10,18... | collective-permute-start | bytes 1966088 | tf_op jit(solution)/shard_map/ppermute | solution.py:220
  63.4 32.6 %collective-permute-start.15 = (bf16[512,1024]{1,0:T(8,128)(2,1)S(1)}, bf16[512,1024]{1,0:T(8,128)(2,1)S(1)}, u32[]{:S(2)}, u32[]{:S(2)}) collective-permute-start(bf16[512,1024]{1,0:T(8,128)(2,1)S(1)} %pad_maximum_fusion.7), channel_id=1, source_target_pairs={{8,16},{12,20},{16,8},{20,12},{9,17},{13,21},{17,9},{21,13},{10,18... | collective-permute-start | bytes 3145736 | tf_op jit(solution)/shard_map/ppermute | solution.py:220
  83.2 31.7 %collective-permute-start.12 = (bf16[512,1280]{1,0:T(8,128)(2,1)S(1)}, bf16[512,1280]{1,0:T(8,128)(2,1)S(1)}, u32[]{:S(2)}, u32[]{:S(2)}) collective-permute-start(bf16[512,1280]{1,0:T(8,128)(2,1)S(1)} %pad_maximum_fusion.3), channel_id=1, source_target_pairs={{0,8},{4,12},{8,0},{12,4},{16,24},{20,28},{24,16},{28,20},{1,9},{5... | collective-permute-start | bytes 3932168 | tf_op jit(solution)/shard_map/ppermute | solution.py:220
  96.0 34.5 %collective-permute-start.18 = (bf16[512,640]{1,0:T(8,128)(2,1)}, bf16[512,640]{1,0:T(8,128)(2,1)}, u32[]{:S(2)}, u32[]{:S(2)}) collective-permute-start(bf16[512,640]{1,0:T(8,128)(2,1)} %pad_maximum_fusion.11), channel_id=1, source_target_pairs={{8,16},{12,20},{16,8},{20,12},{9,17},{13,21},{17,9},{21,13},{10,18... | collective-permute-start | bytes 1966088 | tf_op jit(solution)/shard_map/ppermute | solution.py:220
  115.0 25.0 %collective-permute-start.16 = (bf16[512,1024]{1,0:T(8,128)(2,1)}, bf16[512,1024]{1,0:T(8,128)(2,1)}, u32[]{:S(2)}, u32[]{:S(2)}) collective-permute-start(bf16[512,1024]{1,0:T(8,128)(2,1)} %pad_maximum_fusion.8), channel_id=1, source_target_pairs={{0,8},{4,12},{8,0},{12,4},{16,24},{20,28},{24,16},{28,20},{1,9},{5... | collective-permute-start | bytes 3145736 | tf_op jit(solution)/shard_map/ppermute | solution.py:220
  123.5 15.2 %collective-permute-start.13 = (f32[512,256]{1,0:T(8,128)}, f32[512,256]{1,0:T(8,128)}, u32[]{:S(2)}, u32[]{:S(2)}) collective-permute-start(f32[512,256]{1,0:T(8,128)} %slice.94), channel_id=1, source_target_pairs={{0,4},{4,0},{8,12},{12,8},{16,20},{20,16},{24,28},{28,24},{1,5},{5... | collective-permute-start | bytes 1572872 | tf_op jit(solution)/shard_map/ppermute | solution.py:220
  128.1 21.7 %collective-permute-start.9 = (bf16[512,512]{1,0:T(8,128)(2,1)}, bf16[512,512]{1,0:T(8,128)(2,1)S(1)}, u32[]{:S(2)}, u32[]{:S(2)}) collective-permute-start(bf16[512,512]{1,0:T(8,128)(2,1)} %get-tuple-element.38), channel_id=1, source_target_pairs={{0,4},{4,0},{8,12},{12,8},{16,20},{20,16},{24,28},{28,24},{1,5},{5... | collective-permute-start | bytes 1572872 | tf_op jit(solution)/shard_map/ppermute | solution.py:220
  130.5 33.4 %collective-permute-start.21 = (bf16[512,128]{1,0:T(8,128)(2,1)S(1)}, bf16[512,128]{1,0:T(8,128)(2,1)S(1)}, u32[]{:S(2)}, u32[]{:S(2)}) collective-permute-start(bf16[512,128]{1,0:T(8,128)(2,1)S(1)} %slice.123), channel_id=1, source_target_pairs={{8,16},{12,20},{16,8},{20,12},{9,17},{13,21},{17,9},{21,13},{10,18... | collective-permute-start | bytes 393224 | tf_op jit(solution)/shard_map/ppermute | solution.py:220
  136.1 29.7 %collective-permute-start.14 = (bf16[512,384]{1,0:T(8,128)(2,1)S(1)}, bf16[512,384]{1,0:T(8,128)(2,1)S(1)}, u32[]{:S(2)}, u32[]{:S(2)}) collective-permute-start(bf16[512,384]{1,0:T(8,128)(2,1)S(1)} %slice.134), channel_id=1, source_target_pairs={{0,4},{4,0},{8,12},{12,8},{16,20},{20,16},{24,28},{28,24},{1,5},{5... | collective-permute-start | bytes 1179656 | tf_op jit(solution)/shard_map/ppermute | solution.py:220
  140.0 18.9 %collective-permute-start.19 = (bf16[512,1024]{1,0:T(8,128)(2,1)S(1)}, bf16[512,1024]{1,0:T(8,128)(2,1)S(1)}, u32[]{:S(2)}, u32[]{:S(2)}) collective-permute-start(bf16[512,1024]{1,0:T(8,128)(2,1)S(1)} %pad_maximum_fusion.9), channel_id=1, source_target_pairs={{0,8},{4,12},{8,0},{12,4},{16,24},{20,28},{24,16},{28,20},{1,9},{5... | collective-permute-start | bytes 3145736 | tf_op jit(solution)/shard_map/ppermute | solution.py:220
  146.3 22.0 %collective-permute-start.17 = (bf16[512,512]{1,0:T(8,128)(2,1)S(1)}, bf16[512,512]{1,0:T(8,128)(2,1)S(1)}, u32[]{:S(2)}, u32[]{:S(2)}) collective-permute-start(bf16[512,512]{1,0:T(8,128)(2,1)S(1)} %get-tuple-element.48), channel_id=1, source_target_pairs={{0,4},{4,0},{8,12},{12,8},{16,20},{20,16},{24,28},{28,24},{1,5},{5... | collective-permute-start | bytes 1572872 | tf_op jit(solution)/shard_map/ppermute | solution.py:220
  162.9 12.4 %collective-permute-start.20 = (bf16[512,512]{1,0:T(8,128)(2,1)S(1)}, bf16[512,512]{1,0:T(8,128)(2,1)S(1)}, u32[]{:S(2)}, u32[]{:S(2)}) collective-permute-start(bf16[512,512]{1,0:T(8,128)(2,1)S(1)} %get-tuple-element.55), channel_id=1, source_target_pairs={{0,4},{4,0},{8,12},{12,8},{16,20},{20,16},{24,28},{28,24},{1,5},{5... | collective-permute-start | bytes 1572872 | tf_op jit(solution)/shard_map/ppermute | solution.py:220
  163.9 7.2 %collective-permute-start.22 = (bf16[512,256]{1,0:T(8,128)(2,1)S(1)}, bf16[512,256]{1,0:T(8,128)(2,1)S(1)}, u32[]{:S(2)}, u32[]{:S(2)}) collective-permute-start(bf16[512,256]{1,0:T(8,128)(2,1)S(1)} %pad_maximum_fusion.13), channel_id=1, source_target_pairs={{0,8},{4,12},{8,0},{12,4},{16,24},{20,28},{24,16},{28,20},{1,9},{5... | collective-permute-start | bytes 786440 | tf_op jit(solution)/shard_map/ppermute | solution.py:220
  172.8 5.5 %collective-permute-start.23 = (bf16[512,128]{1,0:T(8,128)(2,1)S(1)}, bf16[512,128]{1,0:T(8,128)(2,1)S(1)}, u32[]{:S(2)}, u32[]{:S(2)}) collective-permute-start(bf16[512,128]{1,0:T(8,128)(2,1)S(1)} %get-tuple-element.62), channel_id=1, source_target_pairs={{0,4},{4,0},{8,12},{12,8},{16,20},{20,16},{24,28},{28,24},{1,5},{5... | collective-permute-start | bytes 393224 | tf_op jit(solution)/shard_map/ppermute | solution.py:220
  (40 other events, 258.8 us)
